TPU v7x, 32 devices: a whole 2x2x4 slice. The times are simulated.
32 devices in a mesh: row: 8 (over z, y), col: 4 (over x, core).
Axes of the slice: x: 2, y: 2, z: 4, core: 2. Of those that a mesh axis runs over, the one named last changes fastest.
Arguments:
- curl_tiles: bfloat16 [8, 128, 1024], P(None, 'col', 'row'), may hold values from -0.005859375 to 0.005859375
- gradient: bfloat16 [1024, 1536], P(('row', 'col')), may hold values from -6 to 6
- a_pattern: int32 [8, 8], replicated, may hold values 0 or 1
- g_pattern: int32 [8, 12], replicated, may hold values 0 or 1
Outputs:
- galerkin: float32 [1536, 1536], P('row', 'col')
Inputs may be any that keep to these rules, and one draw needn't show every extreme that they name: `a_pattern`: 1 keeps a block in the pattern, 0 leaves it out. `g_pattern`: 1 keeps a block in the pattern, 0 leaves it out.
All inputs are finite; a program needn't handle non-finite values.
Results may differ from a plain program's by a relative error of at most 0.0003.
Values may be sent and summed in bfloat16 or wider, within the bound.
No kernel may reach another device: no remote copies, remote signals or barrier semaphores. Data moves between devices by JAX's collectives and lax.ppermute only.
A program may use at most 64 MiB of HBM per device.

v0:
```python
import jax
import jax.numpy as jnp
from jax import lax
from jax.sharding import PartitionSpec as P

BLOCK = 128


def block_hits(position, block_total):
    return (position[:, None] // BLOCK == jnp.arange(block_total, dtype=jnp.int32)[None, :]).astype(
        jnp.float32
    )


def body(curl_tiles, gradient, a_pattern, g_pattern):
    row_count = lax.axis_size("row")
    row_pos = lax.axis_index("row")
    col_pos = lax.axis_index("col")
    rows_here = curl_tiles.shape[1]
    span_rows = curl_tiles.shape[2]
    fine_blocks = a_pattern.shape[0]
    strided_total = row_count * rows_here
    offsets = jnp.arange(rows_here, dtype=jnp.int32)
    column_index = (
        jnp.arange(row_count, dtype=jnp.int32)[:, None] * span_rows
        + col_pos * rows_here
        + offsets[None, :]
    ).reshape(-1)
    row_index = row_pos * span_rows + jnp.arange(span_rows, dtype=jnp.int32)
    own_index = row_pos * span_rows + col_pos * rows_here + offsets
    picked = jnp.dot(block_hits(row_index, fine_blocks), a_pattern.astype(jnp.float32))
    keep_a = jnp.dot(block_hits(column_index, fine_blocks), picked.T)
    masked_a = curl_tiles.reshape(strided_total, span_rows) * keep_a.astype(jnp.bfloat16)
    keep_g = jnp.dot(block_hits(own_index, fine_blocks), g_pattern.astype(jnp.float32))
    masked_g = gradient * jnp.repeat(keep_g, BLOCK, axis=1).astype(jnp.bfloat16)
    g_group = lax.all_gather(masked_g, "col", axis=0, tiled=True)
    g_strided = lax.all_gather(masked_g, "row", axis=0, tiled=True)
    portion = g_strided
    product_t = lax.psum_scatter(
        lax.dot_general(
            portion, masked_a, (((0,), (0,)), ((), ())), preferred_element_type=jnp.float32
        ),
        "col",
        scatter_dimension=0,
        tiled=True,
    )
    portion = g_group.astype(jnp.float32)
    return lax.psum_scatter(
        lax.dot_general(
            portion,
            product_t,
            (((0,), (1,)), ((), ())),
            precision=lax.Precision.HIGHEST,
            preferred_element_type=jnp.float32,
        ),
        "row",
        scatter_dimension=0,
        tiled=True,
    )


def solution(mesh):
    placed = (P(None, "col", "row"), P(("row", "col"), None), P(), P())
    return jax.shard_map(
        body, mesh=mesh, in_specs=placed, out_specs=P("row", "col"), check_vma=False
    )
```

profile of v0, /device:TPU:0, one launch (start us, length us, event | category | flops | bytes accessed | tf_op | source)
XLA Modules:
  0.0 150.2 jit_solution(17114769942040533137)
XLA Ops:
  6.5 0.0 reduce-scatter.3.cloned.1.call-start
  6.6 0.1 iota_add_fusion
  6.6 0.1 add.97
  6.7 0.9 convolution_convert_fusion.1
  7.6 0.1 copy.6
  7.7 0.1 broadcast_in_dim.2
  7.9 0.9 bitcast_multiply_fusion
  8.8 33.8 %all_gather.7 = bf16[256,1536]{1,0:T(8,128)(2,1)S(1)} all-gather(bf16[32,1536]{1,0:T(8,128)(2,1)S(1)} %bitcast_multiply_fusion), channel_id=1, replica_groups=mesh['row'=8,'col'=4] {'row'}, dimensions={0}, use_global_device_ids=true | all-gather | bytes 884736 | tf_op jit(solution)/shard_map/all_gather | solution.py:37
  42.6 0.9 fusion.4
  43.4 2.3 %fusion.1 = f32[1536,128]{1,0:T(8,128)} fusion(bf16[256,1536]{1,0:T(8,128)(2,1)S(1)} %all_gather.7, bf16[256,128]{1,0:T(8,128)(2,1)} %bitcast.9, bf16[128,8]{1,0:T(8,128)(2,1)S(1)} %fusion.4, s32[256]{0:T(256)S(1)} %and_select_fusion.1), kind=kOutput, calls=%fused_computation.2 | convolution fusion | flops 101222400 | bytes 1641472 | tf_op jit(solution)/shard_map/dot_general | solution.py:40
  45.7 0.0 reduce-scatter.3.cloned.1.call-update
  45.8 0.0 reduce-scatter.5.cloned.1.call-start
  45.8 6.5 %all_gather.6 = bf16[128,1536]{1,0:T(8,128)(2,1)S(1)} all-gather(bf16[32,1536]{1,0:T(8,128)(2,1)S(1)} %bitcast_multiply_fusion), channel_id=1, replica_groups=mesh['row'=8,'col'=4] {'col'}, dimensions={0}, use_global_device_ids=true | all-gather | bytes 491520 | tf_op jit(solution)/shard_map/all_gather | solution.py:36
  52.3 17.9 %reduce-scatter.3.cloned.1.call-done = f32[384,128]{1,0:T(8,128)} async-done(((f32[1536,128]{1,0:T(8,128)}), f32[384,128]{1,0:T(8,128)}) %reduce-scatter.3.cloned.1.call-update) | async-done | bytes 196624 | tf_op jit(solution)/shard_map/reduce_scatter | solution.py:39
  70.2 3.5 %fusion.9 = f32[1536,384]{1,0:T(8,128)} fusion(bf16[128,1536]{1,0:T(8,128)(2,1)S(1)} %all_gather.6, f32[384,128]{1,0:T(8,128)} %reduce-scatter.3.cloned.1.call-done), kind=kOutput, calls=%fused_computation.28 | convolution fusion | flops 905969664 | bytes 2949120 | tf_op jit(solution)/shard_map/dot_general | solution.py:49
  73.7 0.0 reduce-scatter.5.cloned.1.call-update
  73.7 69.6 %reduce-scatter.5.cloned.1.call-done = f32[192,384]{1,0:T(8,128)} async-done(((f32[1536,384]{1,0:T(8,128)}), f32[192,384]{1,0:T(8,128)}) %reduce-scatter.5.cloned.1.call-update) | async-done | bytes 294928 | tf_op jit(solution)/shard_map/reduce_scatter | solution.py:48
  (4 shorter events, 0.0 us)
Async XLA Ops:
  6.5 63.7 %reduce-scatter.3.cloned.1.call-start = ((), (), s32[]{:S(2)}) async-start(), calls=%async_computation.2 | async-start | bytes 983040 | tf_op jit(solution)/shard_map/reduce_scatter | solution.py:39
  45.8 97.6 %reduce-scatter.5.cloned.1.call-start = ((), (), s32[]{:S(2)}) async-start(), calls=%async_computation.3 | async-start | bytes 2654208 | tf_op jit(solution)/shard_map/reduce_scatter | solution.py:48
Sparse Core Ops, SparseCore 0:
  45.9 24.2 reduce-scatter.2
  74.1 69.1 reduce-scatter.4
where the time goes:
time: 150 us
  waiting for transfers between devices  87.5 us (58%)
  blocking collectives  40.2 us (27%)
  between operations  13.4 us (9%)
  matrix products  7.56 us (5%)
    reduce_scatter x1, waiting for transfers between devices, body(): lax.psum_scatter(lax.dot_general(portion, product_t, (((0,), (1,)), ((),...  69.6 us
    all_gather x1, blocking collectives, body(): g_strided = lax.all_gather(masked_g, 'row', axis=0, tiled=True)  33.8 us
    reduce_scatter x1, waiting for transfers between devices, body(): lax.psum_scatter(lax.dot_general(portion, masked_a, (((0,), (0,)), ((), (...  17.9 us
    all_gather x1, blocking collectives, body(): g_group = lax.all_gather(masked_g, 'col', axis=0, tiled=True)  6.47 us
    dot_general x1, matrix products, body(): lax.dot_general(portion, product_t, (((0,), (1,)), ((), ())), precision=l...  3.5 us
  transfers between devices with their start and end apart: 2, of which 2 were waited for; matrix products, arithmetic and copies ran while one was open for 0% of the time, Pallas kernels for 0%

commit v1 on v0

--- a/solution.py
+++ b/solution.py
@@ -1,9 +1,14 @@
+import functools
+
 import jax
 import jax.numpy as jnp
 from jax import lax
+from jax.experimental import pallas as pl
+from jax.experimental.pallas import tpu as pltpu
 from jax.sharding import PartitionSpec as P
 
 BLOCK = 128
+GATHER_LIMIT = 8 * 1024 * 1024
 
 
 def block_hits(position, block_total):
@@ -12,7 +17,7 @@
     )
 
 
-def body(curl_tiles, gradient, a_pattern, g_pattern):
+def reducing_body(curl_tiles, gradient, a_pattern, g_pattern):
     row_count = lax.axis_size("row")
     row_pos = lax.axis_index("row")
     col_pos = lax.axis_index("col")
@@ -35,19 +40,17 @@
     masked_g = gradient * jnp.repeat(keep_g, BLOCK, axis=1).astype(jnp.bfloat16)
     g_group = lax.all_gather(masked_g, "col", axis=0, tiled=True)
     g_strided = lax.all_gather(masked_g, "row", axis=0, tiled=True)
-    portion = g_strided
     product_t = lax.psum_scatter(
         lax.dot_general(
-            portion, masked_a, (((0,), (0,)), ((), ())), preferred_element_type=jnp.float32
+            g_strided, masked_a, (((0,), (0,)), ((), ())), preferred_element_type=jnp.float32
         ),
         "col",
         scatter_dimension=0,
         tiled=True,
     )
-    portion = g_group.astype(jnp.float32)
     return lax.psum_scatter(
         lax.dot_general(
-            portion,
+            g_group.astype(jnp.float32),
             product_t,
             (((0,), (1,)), ((), ())),
             precision=lax.Precision.HIGHEST,
@@ -59,8 +62,150 @@
     )
 
 
+def ring_row(position, count):
+    return jnp.where(position < count // 2, 2 * position, 2 * (count - 1 - position) + 1)
+
+
+def ring_position(row, count):
+    return jnp.where(row % 2 == 0, row // 2, count - 1 - row // 2)
+
+
+def ring_rows(count):
+    return list(range(0, count, 2)) + list(range(count - 1, 0, -2))
+
+
+def pack_kernel(a_pattern, g_pattern, a_ref, g_ref, out_ref):
+    row = lax.axis_index("row")
+    tiles, rows_here, _ = a_ref.shape
+    for k in range(tiles):
+        out_ref[k * rows_here : (k + 1) * rows_here, :] = jnp.where(a_pattern[row, k] != 0, a_ref[k], 0)
+    base = tiles * rows_here
+    for j in range(g_ref.shape[1] // BLOCK):
+        out_ref[base + j * rows_here : base + (j + 1) * rows_here, :] = jnp.where(
+            g_pattern[row, j] != 0, g_ref[:, j * BLOCK : (j + 1) * BLOCK], 0
+        )
+
+
+def product_kernel(count, rows_here, *refs):
+    pieces = [refs[4 * d : 4 * d + 4] for d in range(count)]
+    out_ref, g_cols, g_rows, total = refs[4 * count :]
+    row, col = lax.axis_index("row"), lax.axis_index("col")
+    position = ring_position(row, count)
+    a_rows = count * rows_here
+    out_rows, out_cols = out_ref.shape
+    col_blocks, row_blocks = out_cols // BLOCK, g_rows.shape[1] // BLOCK
+    first_col = col * col_blocks
+    first_row = (row * out_rows) // BLOCK
+    for d in range(count):
+        source = ring_row(lax.rem(position - d + count, count), count)
+        for m in range(4):
+            ref = pieces[d][m]
+            below = pl.ds(pl.multiple_of(m * a_rows + source * rows_here, 32), rows_here)
+            for j in range(col_blocks):
+                start = pl.multiple_of(a_rows + (first_col + j) * rows_here, 32)
+                g_cols[below, j * BLOCK : (j + 1) * BLOCK] = ref[pl.ds(start, rows_here), :]
+            below = pl.ds(pl.multiple_of(d * BLOCK + (col ^ m) * rows_here, 32), rows_here)
+            for j in range(row_blocks):
+                start = pl.multiple_of(a_rows + (first_row + j) * rows_here, 32)
+                g_rows[below, j * BLOCK : (j + 1) * BLOCK] = ref[pl.ds(start, rows_here), :]
+    for m in range(4):
+        part = None
+        for d in range(0, count, 2):
+            a = jnp.concatenate([pieces[d][m][:a_rows, :], pieces[d + 1][m][:a_rows, :]], axis=1)
+            term = lax.dot_general(
+                g_rows[d * BLOCK : (d + 2) * BLOCK, :],
+                a,
+                (((0,), (1,)), ((), ())),
+                preferred_element_type=jnp.float32,
+            )
+            part = term if part is None else part + term
+        high = part.astype(jnp.bfloat16)
+        rest = part - high.astype(jnp.float32)
+        middle = rest.astype(jnp.bfloat16)
+        low = (rest - middle.astype(jnp.float32)).astype(jnp.bfloat16)
+        g = g_cols[m * a_rows : (m + 1) * a_rows, :]
+        term = sum(jnp.dot(x, g, preferred_element_type=jnp.float32) for x in (low, middle, high))
+        if m == 0:
+            total[...] = term
+        else:
+            total[...] += term
+    shift = pl.multiple_of(row * out_rows - first_row * BLOCK, 64)
+    out_ref[...] = total[pl.ds(shift, out_rows), :]
+
+
+def gathering_body(count, curl_tiles, gradient, a_pattern, g_pattern):
+    rows_here = curl_tiles.shape[1]
+    coarse = gradient.shape[1]
+    out_rows, out_cols = coarse // count, coarse // 4
+    a_rows = count * rows_here
+    own = pl.pallas_call(
+        pack_kernel,
+        out_shape=jax.ShapeDtypeStruct((a_rows + coarse // BLOCK * rows_here, BLOCK), jnp.bfloat16),
+        in_specs=[pl.BlockSpec(memory_space=pltpu.SMEM)] * 2 + [pl.BlockSpec(memory_space=pltpu.VMEM)] * 2,
+        out_specs=pl.BlockSpec(memory_space=pltpu.VMEM),
+        name="pack",
+    )(a_pattern, g_pattern, curl_tiles, gradient)
+    order = ring_rows(count)
+    axes = ("row", "col")
+
+    def along(step):
+        return [
+            (order[p] * 4 + c, order[(p + step) % count] * 4 + c) for p in range(count) for c in range(4)
+        ]
+
+    def across(mask):
+        return [(i, i ^ mask) for i in range(4 * count)]
+
+    forward, backward = along(1), along(-1)
+    held = {(0, 0): own, (0, 2): lax.ppermute(own, axes, across(2))}
+    half = count // 2
+    for step in range(1, half):
+        for m in (0, 2):
+            held[step, m] = lax.ppermute(held[step - 1, m], axes, forward)
+            held[count - step, m] = lax.ppermute(held[(count - step + 1) % count, m], axes, backward)
+    held[half, 0] = lax.ppermute(held[half - 1, 0], axes, forward)
+    held[half, 2] = lax.ppermute(held[half + 1, 2], axes, backward)
+    for (d, m), piece in list(held.items()):
+        held[d, m + 1] = lax.ppermute(piece, axes, across(1))
+    window = -(-(out_rows + 64) // BLOCK) * BLOCK
+    return pl.pallas_call(
+        functools.partial(product_kernel, count, rows_here),
+        out_shape=jax.ShapeDtypeStruct((out_rows, out_cols), jnp.float32),
+        in_specs=[pl.BlockSpec(memory_space=pltpu.VMEM)] * (4 * count),
+        out_specs=pl.BlockSpec(memory_space=pltpu.VMEM),
+        scratch_shapes=[
+            pltpu.VMEM((4 * a_rows, out_cols), jnp.bfloat16),
+            pltpu.VMEM((4 * a_rows, window), jnp.bfloat16),
+            pltpu.VMEM((window, out_cols), jnp.float32),
+        ],
+        compiler_params=pltpu.CompilerParams(vmem_limit_bytes=16 * 1024 * 1024),
+        name="product",
+    )(*(held[d, m] for d in range(count) for m in range(4)))
+
+
+def gathers(mesh, curl_tiles, gradient):
+    count, width = mesh.shape["row"], mesh.shape["col"]
+    coarse = gradient.shape[1]
+    return (
+        width == 4
+        and count % 2 == 0
+        and curl_tiles.shape[2] // count == BLOCK
+        and curl_tiles.shape[1] // width == 32
+        and coarse % (width * BLOCK) == 0
+        and coarse % (count * 64) == 0
+        and 2 * (curl_tiles.size + gradient.size) <= GATHER_LIMIT
+    )
+
+
 def solution(mesh):
     placed = (P(None, "col", "row"), P(("row", "col"), None), P(), P())
-    return jax.shard_map(
-        body, mesh=mesh, in_specs=placed, out_specs=P("row", "col"), check_vma=False
-    )
+
+    def run(curl_tiles, gradient, a_pattern, g_pattern):
+        body = reducing_body
+        if gathers(mesh, curl_tiles, gradient):
+            body = functools.partial(gathering_body, mesh.shape["row"])
+        return jax.shard_map(
+            body, mesh=mesh, in_specs=placed, out_specs=P("row", "col"), check_vma=False
+        )(curl_tiles, gradient, a_pattern, g_pattern)
+
+    return run

time: 150 us -> 45 us (0.30)
  waiting for transfers between devices: 87.5 us -> 19.1 us
  blocking collectives: 40.2 us -> 0 us
  starting transfers between devices: 0.04 us -> 19.8 us
  between operations: 13.4 us -> 0.05 us
  matrix products: 7.56 us -> 0 us
  Pallas kernels: 0 us -> 4.97 us
    reduce_scatter x2 -> x0, waiting for transfers between devices: 87.5 us -> none  [the longest x1 69.6 us: body(): lax.psum_scatter(lax.dot_general(portion, product_t, (((0,), (1,)), ((),...]
    all_gather x2 -> x0, blocking collectives: 40.2 us -> none  [the longest x1 33.8 us: body(): g_strided = lax.all_gather(masked_g, 'row', axis=0, tiled=True)]
    ppermute x0 -> x31, starting transfers between devices: none -> 19.8 us  [the longest x6 10.8 us: gathering_body(): lax.ppermute(held[(count - step + 1) % count, m], axes, backward)]
    ppermute x0 -> x31, waiting for transfers between devices: none -> 19.1 us  [the longest x6 11.5 us: gathering_body(): lax.ppermute(held[(count - step + 1) % count, m], axes, backward)]
    dot_general x4 -> x0, matrix products: 7.56 us -> none  [the longest x1 3.5 us: body(): lax.dot_general(portion, product_t, (((0,), (1,)), ((), ())), precision=l...]
    pallas_call x0 -> x2, Pallas kernels: none -> 4.97 us  [the longest x1 3.31 us: gathering_body(): pl.pallas_call(functools.partial(product_kernel, count, rows_here), out_s...]
  transfers between devices with their start and end apart: 2 -> 31, of which waited for: 2 -> 13; matrix products, arithmetic and copies ran while one was open for 0% -> 0% of each run, Pallas kernels for 0% -> 0%
where the time goes in v1:
time: 45 us; the launch traced here: 44.8 us
  starting transfers between devices  19.8 us (44%)
  waiting for transfers between devices  19.1 us (42%)
  Pallas kernels  4.97 us (11%)
  local copies, waits for them, and re-layouts  0.92 us (2%)
    ppermute x6, waiting for transfers between devices, gathering_body(): lax.ppermute(held[(count - step + 1) % count, m], axes, backward)  11.5 us
    ppermute x6, starting transfers between devices, gathering_body(): lax.ppermute(held[(count - step + 1) % count, m], axes, backward)  10.8 us
    ppermute x6, waiting for transfers between devices, gathering_body(): held[step, m] = lax.ppermute(held[step - 1, m], axes, forward)  4.32 us
    pallas_call x1, Pallas kernels, gathering_body(): pl.pallas_call(functools.partial(product_kernel, count, rows_here), out_s...  3.31 us
    ppermute x6, starting transfers between devices, gathering_body(): held[step, m] = lax.ppermute(held[step - 1, m], axes, forward)  3.26 us
    ppermute x1, starting transfers between devices, gathering_body(): held = {(0, 0): own, (0, 2): lax.ppermute(own, axes, across(2))}  1.94 us
    ppermute x16, starting transfers between devices, gathering_body(): held[d, m + 1] = lax.ppermute(piece, axes, across(1))  1.85 us
    pallas_call x1, Pallas kernels, gathering_body(): pl.pallas_call(pack_kernel, out_shape=jax.ShapeDtypeStruct((a_rows + coar...  1.66 us
  transfers between devices with their start and end apart: 31, of which 13 were waited for; matrix products, arithmetic and copies ran while one was open for 0% of the time, Pallas kernels for 0%

profile of v1, /device:TPU:0, one launch (start us, length us, event | category | flops | bytes accessed | tf_op | source)
XLA Modules:
  0.0 44.8 jit_solution(15486024768400319408)
XLA Ops:
  0.0 1.7 %pack.1.refs_0_ = bf16[640,128]{1,0:T(8,128)(2,1)} custom-call(s32[8,8]{1,0:T(8,128)} %a_pattern.1, s32[8,12]{1,0:T(8,128)} %g_pattern.1, bf16[8,32,128]{2,1,0:T(8,128)(2,1)} %a_ref.1, bf16[32,1536]{1,0:T(8,128)(2,1)} %g_ref.1), custom_call_target="tpu_custom_call" | custom-call | tf_op jit(solution)/shard_map/pack/pallas_call | solution.py:141
  1.7 3.0 %collective-permute-start.22 = (bf16[640,128]{1,0:T(8,128)(2,1)}, bf16[640,128]{1,0:T(8,128)(2,1)S(1)}, u32[]{:S(2)}, u32[]{:S(2)}) collective-permute-start(bf16[640,128]{1,0:T(8,128)(2,1)} %pack.1.refs_0_), channel_id=1, source_target_pairs={{0,4},{1,5},{2,6},{3,7},{8,0},{9,1},{10,2},{11,3},{16,8},{17,9},{1... | collective-permute-start | bytes 491528 | tf_op jit(solution)/shard_map/ppermute | solution.py:165
  4.6 0.1 collective-permute-start.3
  4.7 1.9 %collective-permute-start.1 = (bf16[640,128]{1,0:T(8,128)(2,1)}, bf16[640,128]{1,0:T(8,128)(2,1)S(1)}, u32[]{:S(2)}, u32[]{:S(2)}) collective-permute-start(bf16[640,128]{1,0:T(8,128)(2,1)} %pack.1.refs_0_), channel_id=1, source_target_pairs={{0,2},{1,3},{2,0},{3,1},{4,6},{5,7},{6,4},{7,5},{8,10},{9,11},{10,... | collective-permute-start | bytes 491528 | tf_op jit(solution)/shard_map/ppermute | solution.py:160
  6.6 0.0 collective-permute-start
  6.6 2.5 %collective-permute-done.22.refs_28_ = bf16[640,128]{1,0:T(8,128)(2,1)S(1)} collective-permute-done((bf16[640,128]{1,0:T(8,128)(2,1)}, bf16[640,128]{1,0:T(8,128)(2,1)S(1)}, u32[]{:S(2)}, u32[]{:S(2)}) %collective-permute-start.22) | collective-permute-done | bytes 163872 | tf_op jit(solution)/shard_map/ppermute | solution.py:165
  9.1 0.0 collective-permute-start.29
  9.1 1.7 %collective-permute-start.23 = (bf16[640,128]{1,0:T(8,128)(2,1)S(1)}, bf16[640,128]{1,0:T(8,128)(2,1)S(1)}, u32[]{:S(2)}, u32[]{:S(2)}) collective-permute-start(bf16[640,128]{1,0:T(8,128)(2,1)S(1)} %collective-permute-done.22.refs_28_), channel_id=1, source_target_pairs={{0,4},{1,5},{2,6},{3,7},{8,0},{9,1},{10,2},{11,3},{16,8},{17,9},{1... | collective-permute-start | bytes 491528 | tf_op jit(solution)/shard_map/ppermute | solution.py:165
  10.8 0.0 collective-permute-done.3.refs_4_
  10.8 0.3 collective-permute-start.7
  11.1 0.0 collective-permute-done.1.refs_2_
  11.1 0.0 collective-permute-start.4
  11.1 0.0 collective-permute-done.refs_1_
  11.1 1.7 %collective-permute-start.17 = (bf16[640,128]{1,0:T(8,128)(2,1)S(1)}, bf16[640,128]{1,0:T(8,128)(2,1)S(1)}, u32[]{:S(2)}, u32[]{:S(2)}) collective-permute-start(bf16[640,128]{1,0:T(8,128)(2,1)S(1)} %collective-permute-done.1.refs_2_), channel_id=1, source_target_pairs={{0,4},{1,5},{2,6},{3,7},{8,0},{9,1},{10,2},{11,3},{16,8},{17,9},{1... | collective-permute-start | bytes 491528 | tf_op jit(solution)/shard_map/ppermute | solution.py:165
  12.9 0.0 collective-permute-done.29.refs_29_
  12.9 0.3 collective-permute-start.5
  13.2 2.9 %collective-permute-done.23.refs_24_ = bf16[640,128]{1,0:T(8,128)(2,1)S(1)} collective-permute-done((bf16[640,128]{1,0:T(8,128)(2,1)S(1)}, bf16[640,128]{1,0:T(8,128)(2,1)S(1)}, u32[]{:S(2)}, u32[]{:S(2)}) %collective-permute-start.23) | collective-permute-done | bytes 163872 | tf_op jit(solution)/shard_map/ppermute | solution.py:165
  16.1 0.0 collective-permute-start.2
  16.1 1.7 %collective-permute-done.7.refs_8_ = bf16[640,128]{1,0:T(8,128)(2,1)S(1)} collective-permute-done((bf16[640,128]{1,0:T(8,128)(2,1)S(1)}, bf16[640,128]{1,0:T(8,128)(2,1)S(1)}, u32[]{:S(2)}, u32[]{:S(2)}) %collective-permute-start.7) | collective-permute-done | bytes 163872 | tf_op jit(solution)/shard_map/ppermute | solution.py:164
  17.8 0.0 collective-permute-start.27
  17.8 0.0 collective-permute-done.4.refs_5_
  17.8 1.6 %collective-permute-start.24 = (bf16[640,128]{1,0:T(8,128)(2,1)S(1)}, bf16[640,128]{1,0:T(8,128)(2,1)S(1)}, u32[]{:S(2)}, u32[]{:S(2)}) collective-permute-start(bf16[640,128]{1,0:T(8,128)(2,1)S(1)} %collective-permute-done.23.refs_24_), channel_id=1, source_target_pairs={{0,4},{1,5},{2,6},{3,7},{8,0},{9,1},{10,2},{11,3},{16,8},{17,9},{1... | collective-permute-start | bytes 491528 | tf_op jit(solution)/shard_map/ppermute | solution.py:165
  19.4 0.0 collective-permute-done.17.refs_30_
  19.4 1.6 %collective-permute-start.11 = (bf16[640,128]{1,0:T(8,128)(2,1)S(1)}, bf16[640,128]{1,0:T(8,128)(2,1)S(1)}, u32[]{:S(2)}, u32[]{:S(2)}) collective-permute-start(bf16[640,128]{1,0:T(8,128)(2,1)S(1)} %collective-permute-done.7.refs_8_), channel_id=1, source_target_pairs={{0,8},{1,9},{2,10},{3,11},{8,16},{9,17},{10,18},{11,19},{16,24},{1... | collective-permute-start | bytes 491528 | tf_op jit(solution)/shard_map/ppermute | solution.py:164
  21.0 0.0 collective-permute-done.5.refs_6_
  21.0 0.0 collective-permute-start.8
  21.0 0.0 collective-permute-done.2.refs_3_
  21.0 1.2 %collective-permute-start.18 = (bf16[640,128]{1,0:T(8,128)(2,1)S(1)}, bf16[640,128]{1,0:T(8,128)(2,1)S(1)}, u32[]{:S(2)}, u32[]{:S(2)}) collective-permute-start(bf16[640,128]{1,0:T(8,128)(2,1)S(1)} %collective-permute-done.17.refs_30_), channel_id=1, source_target_pairs={{0,4},{1,5},{2,6},{3,7},{8,0},{9,1},{10,2},{11,3},{16,8},{17,9},{1... | collective-permute-start | bytes 491528 | tf_op jit(solution)/shard_map/ppermute | solution.py:165
  22.2 0.0 collective-permute-done.27.refs_25_
  22.2 0.2 collective-permute-start.30
  22.4 2.3 %collective-permute-done.24.refs_20_ = bf16[640,128]{1,0:T(8,128)(2,1)S(1)} collective-permute-done((bf16[640,128]{1,0:T(8,128)(2,1)S(1)}, bf16[640,128]{1,0:T(8,128)(2,1)S(1)}, u32[]{:S(2)}, u32[]{:S(2)}) %collective-permute-start.24) | collective-permute-done | bytes 163872 | tf_op jit(solution)/shard_map/ppermute | solution.py:165
  24.7 0.0 collective-permute-start.9
  24.8 1.0 %collective-permute-done.11.refs_12_ = bf16[640,128]{1,0:T(8,128)(2,1)S(1)} collective-permute-done((bf16[640,128]{1,0:T(8,128)(2,1)S(1)}, bf16[640,128]{1,0:T(8,128)(2,1)S(1)}, u32[]{:S(2)}, u32[]{:S(2)}) %collective-permute-start.11) | collective-permute-done | bytes 163872 | tf_op jit(solution)/shard_map/ppermute | solution.py:164
  25.7 0.0 collective-permute-start.6
  25.7 0.0 collective-permute-done.8.refs_9_
  25.7 0.5 %collective-permute-start.25 = (bf16[640,128]{1,0:T(8,128)(2,1)S(1)}, bf16[640,128]{1,0:T(8,128)(2,1)S(1)}, u32[]{:S(2)}, u32[]{:S(2)}) collective-permute-start(bf16[640,128]{1,0:T(8,128)(2,1)S(1)} %collective-permute-done.24.refs_20_), channel_id=1, source_target_pairs={{0,1},{1,0},{2,3},{3,2},{4,5},{5,4},{6,7},{7,6},{8,9},{9,8},{10,11... | collective-permute-start | bytes 491528 | tf_op jit(solution)/shard_map/ppermute | solution.py:169
  26.3 1.7 %collective-permute-done.18.refs_26_ = bf16[640,128]{1,0:T(8,128)(2,1)S(1)} collective-permute-done((bf16[640,128]{1,0:T(8,128)(2,1)S(1)}, bf16[640,128]{1,0:T(8,128)(2,1)S(1)}, u32[]{:S(2)}, u32[]{:S(2)}) %collective-permute-start.18) | collective-permute-done | bytes 163872 | tf_op jit(solution)/shard_map/ppermute | solution.py:165
  28.0 1.6 %collective-permute-start.19 = (bf16[640,128]{1,0:T(8,128)(2,1)S(1)}, bf16[640,128]{1,0:T(8,128)(2,1)S(1)}, u32[]{:S(2)}, u32[]{:S(2)}) collective-permute-start(bf16[640,128]{1,0:T(8,128)(2,1)S(1)} %collective-permute-done.18.refs_26_), channel_id=1, source_target_pairs={{0,4},{1,5},{2,6},{3,7},{8,0},{9,1},{10,2},{11,3},{16,8},{17,9},{1... | collective-permute-start | bytes 491528 | tf_op jit(solution)/shard_map/ppermute | solution.py:165
  29.5 0.0 collective-permute-done.30.refs_31_
  29.5 0.5 %collective-permute-start.15 = (bf16[640,128]{1,0:T(8,128)(2,1)S(1)}, bf16[640,128]{1,0:T(8,128)(2,1)S(1)}, u32[]{:S(2)}, u32[]{:S(2)}) collective-permute-start(bf16[640,128]{1,0:T(8,128)(2,1)S(1)} %collective-permute-done.11.refs_12_), channel_id=1, source_target_pairs={{0,8},{1,9},{2,10},{3,11},{8,16},{9,17},{10,18},{11,19},{16,24},{1... | collective-permute-start | bytes 491528 | tf_op jit(solution)/shard_map/ppermute | solution.py:166
  30.0 0.3 collective-permute-done.9.refs_10_
  30.3 0.0 collective-permute-start.12
  30.3 0.0 collective-permute-done.6.refs_7_
  30.3 0.5 %collective-permute-start.28 = (bf16[640,128]{1,0:T(8,128)(2,1)S(1)}, bf16[640,128]{1,0:T(8,128)(2,1)S(1)}, u32[]{:S(2)}, u32[]{:S(2)}) collective-permute-start(bf16[640,128]{1,0:T(8,128)(2,1)S(1)} %collective-permute-done.18.refs_26_), channel_id=1, source_target_pairs={{0,1},{1,0},{2,3},{3,2},{4,5},{5,4},{6,7},{7,6},{8,9},{9,8},{10,11... | collective-permute-start | bytes 491528 | tf_op jit(solution)/shard_map/ppermute | solution.py:169
  30.8 0.0 collective-permute-done.25.refs_21_
  30.8 0.9 %collective-permute-start.13 = (bf16[640,128]{1,0:T(8,128)(2,1)S(1)}, bf16[640,128]{1,0:T(8,128)(2,1)S(1)}, u32[]{:S(2)}, u32[]{:S(2)}) collective-permute-start(bf16[640,128]{1,0:T(8,128)(2,1)S(1)} %collective-permute-done.9.refs_10_), channel_id=1, source_target_pairs={{0,8},{1,9},{2,10},{3,11},{8,16},{9,17},{10,18},{11,19},{16,24},{1... | collective-permute-start | bytes 491528 | tf_op jit(solution)/shard_map/ppermute | solution.py:164
  31.7 2.2 %collective-permute-done.19.refs_22_ = bf16[640,128]{1,0:T(8,128)(2,1)S(1)} collective-permute-done((bf16[640,128]{1,0:T(8,128)(2,1)S(1)}, bf16[640,128]{1,0:T(8,128)(2,1)S(1)}, u32[]{:S(2)}, u32[]{:S(2)}) %collective-permute-start.19) | collective-permute-done | bytes 163872 | tf_op jit(solution)/shard_map/ppermute | solution.py:165
  33.9 1.5 %collective-permute-start.20 = (bf16[640,128]{1,0:T(8,128)(2,1)S(1)}, bf16[640,128]{1,0:T(8,128)(2,1)S(1)}, u32[]{:S(2)}, u32[]{:S(2)}) collective-permute-start(bf16[640,128]{1,0:T(8,128)(2,1)S(1)} %collective-permute-done.19.refs_22_), channel_id=1, source_target_pairs={{0,4},{1,5},{2,6},{3,7},{8,0},{9,1},{10,2},{11,3},{16,8},{17,9},{1... | collective-permute-start | bytes 491528 | tf_op jit(solution)/shard_map/ppermute | solution.py:167
  35.4 1.3 %collective-permute-done.15.refs_16_ = bf16[640,128]{1,0:T(8,128)(2,1)S(1)} collective-permute-done((bf16[640,128]{1,0:T(8,128)(2,1)S(1)}, bf16[640,128]{1,0:T(8,128)(2,1)S(1)}, u32[]{:S(2)}, u32[]{:S(2)}) %collective-permute-start.15) | collective-permute-done | bytes 163872 | tf_op jit(solution)/shard_map/ppermute | solution.py:166
  36.7 0.0 collective-permute-start.10
  36.7 0.0 collective-permute-done.12.refs_13_
  36.7 0.5 %collective-permute-start.26 = (bf16[640,128]{1,0:T(8,128)(2,1)S(1)}, bf16[640,128]{1,0:T(8,128)(2,1)S(1)}, u32[]{:S(2)}, u32[]{:S(2)}) collective-permute-start(bf16[640,128]{1,0:T(8,128)(2,1)S(1)} %collective-permute-done.19.refs_22_), channel_id=1, source_target_pairs={{0,1},{1,0},{2,3},{3,2},{4,5},{5,4},{6,7},{7,6},{8,9},{9,8},{10,11... | collective-permute-start | bytes 491528 | tf_op jit(solution)/shard_map/ppermute | solution.py:169
  37.2 0.0 collective-permute-done.28.refs_27_
  37.2 0.1 collective-permute-start.16
  37.3 1.3 %collective-permute-done.13.refs_14_ = bf16[640,128]{1,0:T(8,128)(2,1)S(1)} collective-permute-done((bf16[640,128]{1,0:T(8,128)(2,1)S(1)}, bf16[640,128]{1,0:T(8,128)(2,1)S(1)}, u32[]{:S(2)}, u32[]{:S(2)}) %collective-permute-start.13) | collective-permute-done | bytes 163872 | tf_op jit(solution)/shard_map/ppermute | solution.py:164
  38.6 0.0 collective-permute-start.14
  38.6 0.6 %collective-permute-done.20.refs_18_ = bf16[640,128]{1,0:T(8,128)(2,1)S(1)} collective-permute-done((bf16[640,128]{1,0:T(8,128)(2,1)S(1)}, bf16[640,128]{1,0:T(8,128)(2,1)S(1)}, u32[]{:S(2)}, u32[]{:S(2)}) %collective-permute-start.20) | collective-permute-done | bytes 163872 | tf_op jit(solution)/shard_map/ppermute | solution.py:167
  39.2 0.0 collective-permute-done.10.refs_11_
  39.2 0.0 collective-permute-done.16.refs_17_
  39.2 0.0 collective-permute-done.26.refs_23_
  39.2 0.8 %collective-permute-done.14.refs_15_ = bf16[640,128]{1,0:T(8,128)(2,1)S(1)} collective-permute-done((bf16[640,128]{1,0:T(8,128)(2,1)S(1)}, bf16[640,128]{1,0:T(8,128)(2,1)S(1)}, u32[]{:S(2)}, u32[]{:S(2)}) %collective-permute-start.14) | collective-permute-done | bytes 163872 | tf_op jit(solution)/shard_map/ppermute | solution.py:169
  40.0 0.6 %collective-permute-done.21.refs_19_ = bf16[640,128]{1,0:T(8,128)(2,1)S(1)} collective-permute-done((bf16[640,128]{1,0:T(8,128)(2,1)S(1)}, bf16[640,128]{1,0:T(8,128)(2,1)S(1)}, u32[]{:S(2)}, u32[]{:S(2)}) %collective-permute-start.21) | collective-permute-done | bytes 163872 | tf_op jit(solution)/shard_map/ppermute | solution.py:169
  40.6 0.9 %copy-done = bf16[640,128]{1,0:T(8,128)(2,1)S(1)} copy-done((bf16[640,128]{1,0:T(8,128)(2,1)S(1)}, bf16[640,128]{1,0:T(8,128)(2,1)}, u32[]{:S(2)}) %copy-start) | copy-done | bytes 163864
  41.5 3.3 %product.1 = f32[192,384]{1,0:T(8,128)} custom-call(bf16[640,128]{1,0:T(8,128)(2,1)S(1)} %copy-done, bf16[640,128]{1,0:T(8,128)(2,1)S(1)} %collective-permute-done.refs_1_, bf16[640,128]{1,0:T(8,128)(2,1)S(1)} %collective-permute-done.1.refs_2_, bf16[640,128]{1,0:T(8,128)(2,1)S(1)} %collective-permute-done.2.refs_3_, ...), custom_call_target="tpu_custom_call" | custom-call | tf_op jit(solution)/shard_map/product/pallas_call | solution.py:171
  (2 shorter events, 0.0 us)
Async XLA Ops:
  1.7 7.4 %collective-permute-start.22 = (bf16[640,128]{1,0:T(8,128)(2,1)}, bf16[640,128]{1,0:T(8,128)(2,1)S(1)}, u32[]{:S(2)}, u32[]{:S(2)}) collective-permute-start(bf16[640,128]{1,0:T(8,128)(2,1)} %pack.1.refs_0_), channel_id=1, source_target_pairs={{0,4},{1,5},{2,6},{3,7},{8,0},{9,1},{10,2},{11,3},{16,8},{17,9},{1... | collective-permute-start | bytes 491528 | tf_op jit(solution)/shard_map/ppermute | solution.py:165
  4.6 6.2 %collective-permute-start.3 = (bf16[640,128]{1,0:T(8,128)(2,1)}, bf16[640,128]{1,0:T(8,128)(2,1)S(1)}, u32[]{:S(2)}, u32[]{:S(2)}) collective-permute-start(bf16[640,128]{1,0:T(8,128)(2,1)} %pack.1.refs_0_), channel_id=1, source_target_pairs={{0,8},{1,9},{2,10},{3,11},{8,16},{9,17},{10,18},{11,19},{16,24},{1... | collective-permute-start | bytes 491528 | tf_op jit(solution)/shard_map/ppermute | solution.py:164
  4.7 6.4 %collective-permute-start.1 = (bf16[640,128]{1,0:T(8,128)(2,1)}, bf16[640,128]{1,0:T(8,128)(2,1)S(1)}, u32[]{:S(2)}, u32[]{:S(2)}) collective-permute-start(bf16[640,128]{1,0:T(8,128)(2,1)} %pack.1.refs_0_), channel_id=1, source_target_pairs={{0,2},{1,3},{2,0},{3,1},{4,6},{5,7},{6,4},{7,5},{8,10},{9,11},{10,... | collective-permute-start | bytes 491528 | tf_op jit(solution)/shard_map/ppermute | solution.py:160
  6.6 4.5 %collective-permute-start = (bf16[640,128]{1,0:T(8,128)(2,1)}, bf16[640,128]{1,0:T(8,128)(2,1)S(1)}, u32[]{:S(2)}, u32[]{:S(2)}) collective-permute-start(bf16[640,128]{1,0:T(8,128)(2,1)} %pack.1.refs_0_), channel_id=1, source_target_pairs={{0,1},{1,0},{2,3},{3,2},{4,5},{5,4},{6,7},{7,6},{8,9},{9,8},{10,11... | collective-permute-start | bytes 491528 | tf_op jit(solution)/shard_map/ppermute | solution.py:169
  9.1 3.8 %collective-permute-start.29 = (bf16[640,128]{1,0:T(8,128)(2,1)S(1)}, bf16[640,128]{1,0:T(8,128)(2,1)S(1)}, u32[]{:S(2)}, u32[]{:S(2)}) collective-permute-start(bf16[640,128]{1,0:T(8,128)(2,1)S(1)} %collective-permute-done.22.refs_28_), channel_id=1, source_target_pairs={{0,1},{1,0},{2,3},{3,2},{4,5},{5,4},{6,7},{7,6},{8,9},{9,8},{10,11... | collective-permute-start | bytes 491528 | tf_op jit(solution)/shard_map/ppermute | solution.py:169
  9.1 7.0 %collective-permute-start.23 = (bf16[640,128]{1,0:T(8,128)(2,1)S(1)}, bf16[640,128]{1,0:T(8,128)(2,1)S(1)}, u32[]{:S(2)}, u32[]{:S(2)}) collective-permute-start(bf16[640,128]{1,0:T(8,128)(2,1)S(1)} %collective-permute-done.22.refs_28_), channel_id=1, source_target_pairs={{0,4},{1,5},{2,6},{3,7},{8,0},{9,1},{10,2},{11,3},{16,8},{17,9},{1... | collective-permute-start | bytes 491528 | tf_op jit(solution)/shard_map/ppermute | solution.py:165
  10.8 7.0 %collective-permute-start.7 = (bf16[640,128]{1,0:T(8,128)(2,1)S(1)}, bf16[640,128]{1,0:T(8,128)(2,1)S(1)}, u32[]{:S(2)}, u32[]{:S(2)}) collective-permute-start(bf16[640,128]{1,0:T(8,128)(2,1)S(1)} %collective-permute-done.3.refs_4_), channel_id=1, source_target_pairs={{0,8},{1,9},{2,10},{3,11},{8,16},{9,17},{10,18},{11,19},{16,24},{1... | collective-permute-start | bytes 491528 | tf_op jit(solution)/shard_map/ppermute | solution.py:164
  11.1 6.7 %collective-permute-start.4 = (bf16[640,128]{1,0:T(8,128)(2,1)S(1)}, bf16[640,128]{1,0:T(8,128)(2,1)S(1)}, u32[]{:S(2)}, u32[]{:S(2)}) collective-permute-start(bf16[640,128]{1,0:T(8,128)(2,1)S(1)} %collective-permute-done.3.refs_4_), channel_id=1, source_target_pairs={{0,1},{1,0},{2,3},{3,2},{4,5},{5,4},{6,7},{7,6},{8,9},{9,8},{10,11... | collective-permute-start | bytes 491528 | tf_op jit(solution)/shard_map/ppermute | solution.py:169
  11.1 8.3 %collective-permute-start.17 = (bf16[640,128]{1,0:T(8,128)(2,1)S(1)}, bf16[640,128]{1,0:T(8,128)(2,1)S(1)}, u32[]{:S(2)}, u32[]{:S(2)}) collective-permute-start(bf16[640,128]{1,0:T(8,128)(2,1)S(1)} %collective-permute-done.1.refs_2_), channel_id=1, source_target_pairs={{0,4},{1,5},{2,6},{3,7},{8,0},{9,1},{10,2},{11,3},{16,8},{17,9},{1... | collective-permute-start | bytes 491528 | tf_op jit(solution)/shard_map/ppermute | solution.py:165
  12.9 8.1 %collective-permute-start.5 = (bf16[640,128]{1,0:T(8,128)(2,1)S(1)}, bf16[640,128]{1,0:T(8,128)(2,1)S(1)}, u32[]{:S(2)}, u32[]{:S(2)}) collective-permute-start(bf16[640,128]{1,0:T(8,128)(2,1)S(1)} %collective-permute-done.1.refs_2_), channel_id=1, source_target_pairs={{0,8},{1,9},{2,10},{3,11},{8,16},{9,17},{10,18},{11,19},{16,24},{1... | collective-permute-start | bytes 491528 | tf_op jit(solution)/shard_map/ppermute | solution.py:164
  16.1 4.9 %collective-permute-start.2 = (bf16[640,128]{1,0:T(8,128)(2,1)S(1)}, bf16[640,128]{1,0:T(8,128)(2,1)S(1)}, u32[]{:S(2)}, u32[]{:S(2)}) collective-permute-start(bf16[640,128]{1,0:T(8,128)(2,1)S(1)} %collective-permute-done.1.refs_2_), channel_id=1, source_target_pairs={{0,1},{1,0},{2,3},{3,2},{4,5},{5,4},{6,7},{7,6},{8,9},{9,8},{10,11... | collective-permute-start | bytes 491528 | tf_op jit(solution)/shard_map/ppermute | solution.py:169
  17.8 4.4 %collective-permute-start.27 = (bf16[640,128]{1,0:T(8,128)(2,1)S(1)}, bf16[640,128]{1,0:T(8,128)(2,1)S(1)}, u32[]{:S(2)}, u32[]{:S(2)}) collective-permute-start(bf16[640,128]{1,0:T(8,128)(2,1)S(1)} %collective-permute-done.23.refs_24_), channel_id=1, source_target_pairs={{0,1},{1,0},{2,3},{3,2},{4,5},{5,4},{6,7},{7,6},{8,9},{9,8},{10,11... | collective-permute-start | bytes 491528 | tf_op jit(solution)/shard_map/ppermute | solution.py:169
  17.8 6.9 %collective-permute-start.24 = (bf16[640,128]{1,0:T(8,128)(2,1)S(1)}, bf16[640,128]{1,0:T(8,128)(2,1)S(1)}, u32[]{:S(2)}, u32[]{:S(2)}) collective-permute-start(bf16[640,128]{1,0:T(8,128)(2,1)S(1)} %collective-permute-done.23.refs_24_), channel_id=1, source_target_pairs={{0,4},{1,5},{2,6},{3,7},{8,0},{9,1},{10,2},{11,3},{16,8},{17,9},{1... | collective-permute-start | bytes 491528 | tf_op jit(solution)/shard_map/ppermute | solution.py:165
  19.4 6.3 %collective-permute-start.11 = (bf16[640,128]{1,0:T(8,128)(2,1)S(1)}, bf16[640,128]{1,0:T(8,128)(2,1)S(1)}, u32[]{:S(2)}, u32[]{:S(2)}) collective-permute-start(bf16[640,128]{1,0:T(8,128)(2,1)S(1)} %collective-permute-done.7.refs_8_), channel_id=1, source_target_pairs={{0,8},{1,9},{2,10},{3,11},{8,16},{9,17},{10,18},{11,19},{16,24},{1... | collective-permute-start | bytes 491528 | tf_op jit(solution)/shard_map/ppermute | solution.py:164
  21.0 4.8 %collective-permute-start.8 = (bf16[640,128]{1,0:T(8,128)(2,1)S(1)}, bf16[640,128]{1,0:T(8,128)(2,1)S(1)}, u32[]{:S(2)}, u32[]{:S(2)}) collective-permute-start(bf16[640,128]{1,0:T(8,128)(2,1)S(1)} %collective-permute-done.7.refs_8_), channel_id=1, source_target_pairs={{0,1},{1,0},{2,3},{3,2},{4,5},{5,4},{6,7},{7,6},{8,9},{9,8},{10,11... | collective-permute-start | bytes 491528 | tf_op jit(solution)/shard_map/ppermute | solution.py:169
  21.0 7.0 %collective-permute-start.18 = (bf16[640,128]{1,0:T(8,128)(2,1)S(1)}, bf16[640,128]{1,0:T(8,128)(2,1)S(1)}, u32[]{:S(2)}, u32[]{:S(2)}) collective-permute-start(bf16[640,128]{1,0:T(8,128)(2,1)S(1)} %collective-permute-done.17.refs_30_), channel_id=1, source_target_pairs={{0,4},{1,5},{2,6},{3,7},{8,0},{9,1},{10,2},{11,3},{16,8},{17,9},{1... | collective-permute-start | bytes 491528 | tf_op jit(solution)/shard_map/ppermute | solution.py:165
  22.2 7.3 %collective-permute-start.30 = (bf16[640,128]{1,0:T(8,128)(2,1)S(1)}, bf16[640,128]{1,0:T(8,128)(2,1)S(1)}, u32[]{:S(2)}, u32[]{:S(2)}) collective-permute-start(bf16[640,128]{1,0:T(8,128)(2,1)S(1)} %collective-permute-done.17.refs_30_), channel_id=1, source_target_pairs={{0,1},{1,0},{2,3},{3,2},{4,5},{5,4},{6,7},{7,6},{8,9},{9,8},{10,11... | collective-permute-start | bytes 491528 | tf_op jit(solution)/shard_map/ppermute | solution.py:169
  24.7 5.5 %collective-permute-start.9 = (bf16[640,128]{1,0:T(8,128)(2,1)S(1)}, bf16[640,128]{1,0:T(8,128)(2,1)S(1)}, u32[]{:S(2)}, u32[]{:S(2)}) collective-permute-start(bf16[640,128]{1,0:T(8,128)(2,1)S(1)} %collective-permute-done.5.refs_6_), channel_id=1, source_target_pairs={{0,8},{1,9},{2,10},{3,11},{8,16},{9,17},{10,18},{11,19},{16,24},{1... | collective-permute-start | bytes 491528 | tf_op jit(solution)/shard_map/ppermute | solution.py:164
  25.7 4.5 %collective-permute-start.6 = (bf16[640,128]{1,0:T(8,128)(2,1)S(1)}, bf16[640,128]{1,0:T(8,128)(2,1)S(1)}, u32[]{:S(2)}, u32[]{:S(2)}) collective-permute-start(bf16[640,128]{1,0:T(8,128)(2,1)S(1)} %collective-permute-done.5.refs_6_), channel_id=1, source_target_pairs={{0,1},{1,0},{2,3},{3,2},{4,5},{5,4},{6,7},{7,6},{8,9},{9,8},{10,11... | collective-permute-start | bytes 491528 | tf_op jit(solution)/shard_map/ppermute | solution.py:169
  25.7 5.0 %collective-permute-start.25 = (bf16[640,128]{1,0:T(8,128)(2,1)S(1)}, bf16[640,128]{1,0:T(8,128)(2,1)S(1)}, u32[]{:S(2)}, u32[]{:S(2)}) collective-permute-start(bf16[640,128]{1,0:T(8,128)(2,1)S(1)} %collective-permute-done.24.refs_20_), channel_id=1, source_target_pairs={{0,1},{1,0},{2,3},{3,2},{4,5},{5,4},{6,7},{7,6},{8,9},{9,8},{10,11... | collective-permute-start | bytes 491528 | tf_op jit(solution)/shard_map/ppermute | solution.py:169
  28.0 5.9 %collective-permute-start.19 = (bf16[640,128]{1,0:T(8,128)(2,1)S(1)}, bf16[640,128]{1,0:T(8,128)(2,1)S(1)}, u32[]{:S(2)}, u32[]{:S(2)}) collective-permute-start(bf16[640,128]{1,0:T(8,128)(2,1)S(1)} %collective-permute-done.18.refs_26_), channel_id=1, source_target_pairs={{0,4},{1,5},{2,6},{3,7},{8,0},{9,1},{10,2},{11,3},{16,8},{17,9},{1... | collective-permute-start | bytes 491528 | tf_op jit(solution)/shard_map/ppermute | solution.py:165
  29.5 7.1 %collective-permute-start.15 = (bf16[640,128]{1,0:T(8,128)(2,1)S(1)}, bf16[640,128]{1,0:T(8,128)(2,1)S(1)}, u32[]{:S(2)}, u32[]{:S(2)}) collective-permute-start(bf16[640,128]{1,0:T(8,128)(2,1)S(1)} %collective-permute-done.11.refs_12_), channel_id=1, source_target_pairs={{0,8},{1,9},{2,10},{3,11},{8,16},{9,17},{10,18},{11,19},{16,24},{1... | collective-permute-start | bytes 491528 | tf_op jit(solution)/shard_map/ppermute | solution.py:166
  30.3 6.4 %collective-permute-start.12 = (bf16[640,128]{1,0:T(8,128)(2,1)S(1)}, bf16[640,128]{1,0:T(8,128)(2,1)S(1)}, u32[]{:S(2)}, u32[]{:S(2)}) collective-permute-start(bf16[640,128]{1,0:T(8,128)(2,1)S(1)} %collective-permute-done.11.refs_12_), channel_id=1, source_target_pairs={{0,1},{1,0},{2,3},{3,2},{4,5},{5,4},{6,7},{7,6},{8,9},{9,8},{10,11... | collective-permute-start | bytes 491528 | tf_op jit(solution)/shard_map/ppermute | solution.py:169
  30.3 6.9 %collective-permute-start.28 = (bf16[640,128]{1,0:T(8,128)(2,1)S(1)}, bf16[640,128]{1,0:T(8,128)(2,1)S(1)}, u32[]{:S(2)}, u32[]{:S(2)}) collective-permute-start(bf16[640,128]{1,0:T(8,128)(2,1)S(1)} %collective-permute-done.18.refs_26_), channel_id=1, source_target_pairs={{0,1},{1,0},{2,3},{3,2},{4,5},{5,4},{6,7},{7,6},{8,9},{9,8},{10,11... | collective-permute-start | bytes 491528 | tf_op jit(solution)/shard_map/ppermute | solution.py:169
  30.8 7.8 %collective-permute-start.13 = (bf16[640,128]{1,0:T(8,128)(2,1)S(1)}, bf16[640,128]{1,0:T(8,128)(2,1)S(1)}, u32[]{:S(2)}, u32[]{:S(2)}) collective-permute-start(bf16[640,128]{1,0:T(8,128)(2,1)S(1)} %collective-permute-done.9.refs_10_), channel_id=1, source_target_pairs={{0,8},{1,9},{2,10},{3,11},{8,16},{9,17},{10,18},{11,19},{16,24},{1... | collective-permute-start | bytes 491528 | tf_op jit(solution)/shard_map/ppermute | solution.py:164
  33.9 5.3 %collective-permute-start.20 = (bf16[640,128]{1,0:T(8,128)(2,1)S(1)}, bf16[640,128]{1,0:T(8,128)(2,1)S(1)}, u32[]{:S(2)}, u32[]{:S(2)}) collective-permute-start(bf16[640,128]{1,0:T(8,128)(2,1)S(1)} %collective-permute-done.19.refs_22_), channel_id=1, source_target_pairs={{0,4},{1,5},{2,6},{3,7},{8,0},{9,1},{10,2},{11,3},{16,8},{17,9},{1... | collective-permute-start | bytes 491528 | tf_op jit(solution)/shard_map/ppermute | solution.py:167
  36.7 2.5 %collective-permute-start.10 = (bf16[640,128]{1,0:T(8,128)(2,1)S(1)}, bf16[640,128]{1,0:T(8,128)(2,1)S(1)}, u32[]{:S(2)}, u32[]{:S(2)}) collective-permute-start(bf16[640,128]{1,0:T(8,128)(2,1)S(1)} %collective-permute-done.9.refs_10_), channel_id=1, source_target_pairs={{0,1},{1,0},{2,3},{3,2},{4,5},{5,4},{6,7},{7,6},{8,9},{9,8},{10,11... | collective-permute-start | bytes 491528 | tf_op jit(solution)/shard_map/ppermute | solution.py:169
  36.7 2.5 %collective-permute-start.26 = (bf16[640,128]{1,0:T(8,128)(2,1)S(1)}, bf16[640,128]{1,0:T(8,128)(2,1)S(1)}, u32[]{:S(2)}, u32[]{:S(2)}) collective-permute-start(bf16[640,128]{1,0:T(8,128)(2,1)S(1)} %collective-permute-done.19.refs_22_), channel_id=1, source_target_pairs={{0,1},{1,0},{2,3},{3,2},{4,5},{5,4},{6,7},{7,6},{8,9},{9,8},{10,11... | collective-permute-start | bytes 491528 | tf_op jit(solution)/shard_map/ppermute | solution.py:169
  37.2 2.0 %collective-permute-start.16 = (bf16[640,128]{1,0:T(8,128)(2,1)S(1)}, bf16[640,128]{1,0:T(8,128)(2,1)S(1)}, u32[]{:S(2)}, u32[]{:S(2)}) collective-permute-start(bf16[640,128]{1,0:T(8,128)(2,1)S(1)} %collective-permute-done.15.refs_16_), channel_id=1, source_target_pairs={{0,1},{1,0},{2,3},{3,2},{4,5},{5,4},{6,7},{7,6},{8,9},{9,8},{10,11... | collective-permute-start | bytes 491528 | tf_op jit(solution)/shard_map/ppermute | solution.py:169
  38.6 1.4 %collective-permute-start.14 = (bf16[640,128]{1,0:T(8,128)(2,1)S(1)}, bf16[640,128]{1,0:T(8,128)(2,1)S(1)}, u32[]{:S(2)}, u32[]{:S(2)}) collective-permute-start(bf16[640,128]{1,0:T(8,128)(2,1)S(1)} %collective-permute-done.13.refs_14_), channel_id=1, source_target_pairs={{0,1},{1,0},{2,3},{3,2},{4,5},{5,4},{6,7},{7,6},{8,9},{9,8},{10,11... | collective-permute-start | bytes 491528 | tf_op jit(solution)/shard_map/ppermute | solution.py:169
  39.2 1.4 %collective-permute-start.21 = (bf16[640,128]{1,0:T(8,128)(2,1)S(1)}, bf16[640,128]{1,0:T(8,128)(2,1)S(1)}, u32[]{:S(2)}, u32[]{:S(2)}) collective-permute-start(bf16[640,128]{1,0:T(8,128)(2,1)S(1)} %collective-permute-done.20.refs_18_), channel_id=1, source_target_pairs={{0,1},{1,0},{2,3},{3,2},{4,5},{5,4},{6,7},{7,6},{8,9},{9,8},{10,11... | collective-permute-start | bytes 491528 | tf_op jit(solution)/shard_map/ppermute | solution.py:169
  40.6 0.9 %copy-start = (bf16[640,128]{1,0:T(8,128)(2,1)S(1)}, bf16[640,128]{1,0:T(8,128)(2,1)}, u32[]{:S(2)}) copy-start(bf16[640,128]{1,0:T(8,128)(2,1)} %pack.1.refs_0_) | copy-start | bytes 491524

commit v2 on v0

--- a/solution.py
+++ b/solution.py
@@ -1,9 +1,14 @@
+import functools
+
 import jax
 import jax.numpy as jnp
 from jax import lax
+from jax.experimental import pallas as pl
+from jax.experimental.pallas import tpu as pltpu
 from jax.sharding import PartitionSpec as P
 
 BLOCK = 128
+GATHER_LIMIT = 8 * 1024 * 1024
 
 
 def block_hits(position, block_total):
@@ -12,7 +17,7 @@
     )
 
 
-def body(curl_tiles, gradient, a_pattern, g_pattern):
+def reducing_body(curl_tiles, gradient, a_pattern, g_pattern):
     row_count = lax.axis_size("row")
     row_pos = lax.axis_index("row")
     col_pos = lax.axis_index("col")
@@ -35,19 +40,17 @@
     masked_g = gradient * jnp.repeat(keep_g, BLOCK, axis=1).astype(jnp.bfloat16)
     g_group = lax.all_gather(masked_g, "col", axis=0, tiled=True)
     g_strided = lax.all_gather(masked_g, "row", axis=0, tiled=True)
-    portion = g_strided
     product_t = lax.psum_scatter(
         lax.dot_general(
-            portion, masked_a, (((0,), (0,)), ((), ())), preferred_element_type=jnp.float32
+            g_strided, masked_a, (((0,), (0,)), ((), ())), preferred_element_type=jnp.float32
         ),
         "col",
         scatter_dimension=0,
         tiled=True,
     )
-    portion = g_group.astype(jnp.float32)
     return lax.psum_scatter(
         lax.dot_general(
-            portion,
+            g_group.astype(jnp.float32),
             product_t,
             (((0,), (1,)), ((), ())),
             precision=lax.Precision.HIGHEST,
@@ -59,8 +62,329 @@
     )
 
 
+def ring_row(position, count):
+    return jnp.where(position < count // 2, 2 * position, 2 * (count - 1 - position) + 1)
+
+
+def ring_position(row, count):
+    return jnp.where(row % 2 == 0, row // 2, count - 1 - row // 2)
+
+
+def ring_rows(count):
+    return list(range(0, count, 2)) + list(range(count - 1, 0, -2))
+
+
+def layout(count, rows_here, coarse):
+    a_rows = count * rows_here
+    col_blocks = coarse // 4 // BLOCK
+    row_blocks = -(-(coarse // count + 64) // BLOCK)
+    crossing = a_rows + (2 * col_blocks + row_blocks) * rows_here
+    share = a_rows + (col_blocks + row_blocks) * rows_here
+    return a_rows, col_blocks, row_blocks, crossing, share
+
+
+def first_window(row, count, coarse):
+    return (row * (coarse // count)) // BLOCK
+
+
+def aligned(start):
+    return pl.multiple_of(start, 32)
+
+
+def put(out_ref, at, ref, start, rows):
+    out_ref[at : at + rows, :] = ref[pl.ds(start, rows), :]
+    return at + rows
+
+
+def cut_kernel(count, rows_here, coarse, items, *refs):
+    a_rows, col_blocks, row_blocks, _, _ = layout(count, rows_here, coarse)
+    row, col = lax.axis_index("row"), lax.axis_index("col")
+    second = col % 2 == 1
+    for (sources, steps, over), out_ref in zip(items, refs[len(refs) - len(items) :]):
+        step = jnp.where(second, steps[1] + count, steps[0] + count)
+        there = ring_row(lax.rem(ring_position(row, count) + step, count), count)
+        half = aligned(a_rows + ((col // 2) ^ over) * (2 * col_blocks * rows_here))
+        window = aligned(a_rows + first_window(there, count, coarse) * rows_here)
+        at = 0
+        for start, n in ((0, a_rows), (half, 2 * col_blocks * rows_here), (window, row_blocks * rows_here)):
+            part = refs[sources[0]][pl.ds(start, n), :]
+            if sources[1] != sources[0]:
+                part = jnp.where(second, refs[sources[1]][pl.ds(start, n), :], part)
+            out_ref[at : at + n, :] = part
+            at += n
+
+
+def pack_kernel(count, rows_here, coarse, a_pattern, g_pattern, a_ref, g_ref, out_ref):
+    row = lax.axis_index("row")
+    a_rows = layout(count, rows_here, coarse)[0]
+    for k in range(count):
+        out_ref[k * rows_here : (k + 1) * rows_here, :] = jnp.where(a_pattern[row, k] != 0, a_ref[k], 0)
+    for j in range(coarse // BLOCK):
+        out_ref[a_rows + j * rows_here : a_rows + (j + 1) * rows_here, :] = jnp.where(
+            g_pattern[row, j] != 0, g_ref[:, j * BLOCK : (j + 1) * BLOCK], 0
+        )
+
+
+class Piece:
+    def __init__(self, kind, ref, begin, sizes):
+        self.kind, self.ref, self.begin, self.sizes = kind, ref, begin, sizes
+
+    def tiles(self):
+        return self.ref[self.begin : self.begin + self.sizes[0], :]
+
+    def columns(self, rows_here, col):
+        a_rows, col_blocks = self.sizes[:2]
+        start = self.begin + a_rows
+        if self.kind == "whole":
+            start = aligned(start + col * (col_blocks * rows_here))
+        elif self.kind == "cross":
+            start = aligned(start + (col % 2) * (col_blocks * rows_here))
+        return start
+
+    def window(self, rows_here, first):
+        a_rows, col_blocks = self.sizes[:2]
+        start = self.begin + a_rows
+        if self.kind == "whole":
+            return aligned(start + first * rows_here)
+        return start + (2 if self.kind == "cross" else 1) * col_blocks * rows_here
+
+
+def pieces_of(spec, refs, sizes):
+    return {key: Piece(kind, refs[index], begin, sizes) for key, (kind, index, begin) in spec.items()}
+
+
+def collect_kernel(count, rows_here, coarse, spec, *refs):
+    sizes = layout(count, rows_here, coarse)
+    a_rows, col_blocks, row_blocks = sizes[:3]
+    row, col = lax.axis_index("row"), lax.axis_index("col")
+    first = first_window(row, count, coarse)
+    for out_ref, owner in ((refs[-2], col), (refs[-1], col ^ 1)):
+        at = 0
+        for piece in pieces_of(spec, refs, sizes).values():
+            at = put(out_ref, at, piece.ref, piece.begin, a_rows)
+            at = put(out_ref, at, piece.ref, piece.columns(rows_here, owner), col_blocks * rows_here)
+            at = put(out_ref, at, piece.ref, piece.window(rows_here, first), row_blocks * rows_here)
+
+
+def place_kernel_part(pieces, count, rows_here, coarse, distances, g_cols, g_rows):
+    _, col_blocks, row_blocks, _, _ = layout(count, rows_here, coarse)
+    a_rows = count * rows_here
+    row, col = lax.axis_index("row"), lax.axis_index("col")
+    position = ring_position(row, count)
+    first = first_window(row, count, coarse)
+    for (d, m), piece in pieces.items():
+        source = ring_row(lax.rem(position - d + count, count), count)
+        if g_cols is not None:
+            below = pl.ds(aligned(m * a_rows + source * rows_here), rows_here)
+            start = piece.columns(rows_here, col)
+            for j in range(col_blocks):
+                g_cols[below, j * BLOCK : (j + 1) * BLOCK] = piece.ref[pl.ds(start + j * rows_here, rows_here), :]
+        if d in distances:
+            below = pl.ds(aligned(distances.index(d) * BLOCK + (col ^ m) * rows_here), rows_here)
+            start = piece.window(rows_here, first)
+            for j in range(row_blocks):
+                g_rows[below, j * BLOCK : (j + 1) * BLOCK] = piece.ref[pl.ds(start + j * rows_here, rows_here), :]
+
+
+def partial_product(pieces, m, distances, g_rows):
+    part = None
+    for i in range(0, len(distances), 2):
+        pair = distances[i : i + 2]
+        tiles = [pieces[d, m].tiles() for d in pair]
+        term = lax.dot_general(
+            g_rows[i * BLOCK : (i + len(pair)) * BLOCK, :],
+            tiles[0] if len(tiles) == 1 else jnp.concatenate(tiles, axis=1),
+            (((0,), (1,)), ((), ())),
+            preferred_element_type=jnp.float32,
+        )
+        part = term if part is None else part + term
+    return part
+
+
+def early_kernel(count, rows_here, coarse, spec, distances, *refs):
+    part_ref, g_cols, g_rows = refs[-3:]
+    sizes = layout(count, rows_here, coarse)
+    a_rows = sizes[0]
+    pieces = pieces_of(spec, refs, sizes)
+    place_kernel_part(pieces, count, rows_here, coarse, distances, g_cols, g_rows)
+    for m in range(4):
+        part_ref[:, m * a_rows : (m + 1) * a_rows] = partial_product(pieces, m, distances, g_rows)
+
+
+def product_kernel(count, rows_here, coarse, late, spec, distances, *refs):
+    part_ref, g_early, out_ref, g_cols, g_rows, total, highs, lows = refs[-8:]
+    sizes = layout(count, rows_here, coarse)
+    a_rows = sizes[0]
+    pieces = pieces_of(spec, refs, sizes)
+    g_cols[...] = g_early[...]
+    place_kernel_part({key: pieces[key] for key in late}, count, rows_here, coarse, distances, g_cols, g_rows)
+    rest = {key: piece for key, piece in pieces.items() if key not in late}
+    place_kernel_part(rest, count, rows_here, coarse, distances, None, g_rows)
+    for m in range(4):
+        columns = slice(m * a_rows, (m + 1) * a_rows)
+        part = part_ref[:, columns] + partial_product(pieces, m, distances, g_rows)
+        high = part.astype(jnp.bfloat16)
+        highs[:, columns] = high
+        lows[:, columns] = (part - high.astype(jnp.float32)).astype(jnp.bfloat16)
+    total[...] = jnp.dot(lows[...], g_cols[...], preferred_element_type=jnp.float32) + jnp.dot(
+        highs[...], g_cols[...], preferred_element_type=jnp.float32
+    )
+    row = lax.axis_index("row")
+    out_rows = out_ref.shape[0]
+    shift = pl.multiple_of(row * out_rows - first_window(row, count, coarse) * BLOCK, 64)
+    out_ref[...] = total[pl.ds(shift, out_rows), :]
+
+
+def gathering_body(count, curl_tiles, gradient, a_pattern, g_pattern):
+    rows_here = curl_tiles.shape[1]
+    coarse = gradient.shape[1]
+    out_rows, out_cols = coarse // count, coarse // 4
+    a_rows, _, row_blocks, crossing, share = layout(count, rows_here, coarse)
+    packed = a_rows + coarse // BLOCK * rows_here
+    whole, scalars = pl.BlockSpec(memory_space=pltpu.VMEM), pl.BlockSpec(memory_space=pltpu.SMEM)
+    limit = pltpu.CompilerParams(vmem_limit_bytes=8 * 1024 * 1024)
+    sizes = (count, rows_here, coarse)
+    axes = ("row", "col")
+
+    def rows(n):
+        return pltpu.VMEM((n, BLOCK), jnp.bfloat16)
+
+    def call(kernel, out, operands, name, *given, **options):
+        return pl.pallas_call(
+            functools.partial(kernel, *sizes, *given),
+            out_shape=out,
+            in_specs=options.pop("in_specs", [whole] * len(operands)),
+            out_specs=[whole] * len(out) if isinstance(out, list) else whole,
+            name=name,
+            **options,
+        )(*operands)
+
+    order = ring_rows(count)
+
+    def along(step):
+        return [
+            (order[p] * 4 + c, order[(p + step) % count] * 4 + c) for p in range(count) for c in range(4)
+        ]
+
+    def across(piece, mask):
+        return lax.ppermute(piece, axes, [(i, i ^ mask) for i in range(4 * count)])
+
+    forward, backward = along(1), along(-1)
+    half = count // 2
+    own = call(
+        pack_kernel,
+        rows(packed),
+        (a_pattern, g_pattern, curl_tiles, gradient),
+        "pack",
+        in_specs=[scalars] * 2 + [whole] * 2,
+    )
+    held = {(0, 0): ("whole", own, 0), (0, 2): ("whole", across(own, 2), 0)}
+
+    def operands_of(pieces):
+        buffers, spec = [], {}
+        for key, (kind, buffer, begin) in pieces.items():
+            if not any(buffer is b for b in buffers):
+                buffers.append(buffer)
+            spec[key] = (kind, [buffer is b for b in buffers].index(True), begin)
+        return buffers, spec
+
+    def exchange(pieces, *over):
+        buffers, spec = operands_of(pieces)
+        mine, theirs = call(
+            collect_kernel,
+            [rows(len(pieces) * share)] * 2,
+            [*buffers, *over],
+            "collect",
+            spec,
+            compiler_params=limit,
+        )
+        theirs = across(theirs, 1)
+        return {
+            (d, m + other): ("share", (mine, theirs)[other], i * share)
+            for i, (d, m) in enumerate(spec)
+            for other in (0, 1)
+        }
+
+    def cut(items, *operands):
+        return call(cut_kernel, [rows(crossing)] * len(items), operands, "cut", items, compiler_params=limit)
+
+    for m in (0, 2):
+        ahead = back = held[0, m][1]
+        for step in range(1, half):
+            if m == 2 and step == half - 1:
+                ahead, back = cut([((0, 0), (1, 1), 0), ((1, 1), (-1, -1), 0)], ahead, back)
+            ahead, back = lax.ppermute(ahead, axes, forward), lax.ppermute(back, axes, backward)
+            kind = "cross" if m == 2 and step == half - 1 else "whole"
+            held[step, m], held[count - step, m] = (kind, ahead, 0), (kind, back, 0)
+    split = [pair for pair in forward if pair[0] % 2 == 0] + [pair for pair in backward if pair[0] % 2 == 1]
+    straight, diagonal = cut(
+        [((0, 1), (1, -1), 0), ((0, 1), (1, -1), 1)], held[half - 1, 0][1], held[half + 1, 0][1]
+    )
+    held[half, 0] = ("cross", lax.ppermute(straight, axes, split), 0)
+    held[half, 2] = ("cross", lax.ppermute(diagonal, axes, [(i, j ^ 2) for i, j in split]), 0)
+    early = {key: held[key] for key in held if min(key[0], count - key[0]) <= (3, 2)[key[1] // 2]}
+    got = exchange(early)
+    distances = [d for d in range(count) if (d, 0) in early and (d, 2) in early]
+    buffers, spec = operands_of(got)
+    part, g_cols = call(
+        early_kernel,
+        [
+            pltpu.VMEM((row_blocks * BLOCK, 4 * a_rows), jnp.float32),
+            pltpu.VMEM((4 * a_rows, out_cols), jnp.bfloat16),
+        ],
+        buffers,
+        "early",
+        spec,
+        distances,
+        scratch_shapes=[pltpu.VMEM((len(distances) * BLOCK, row_blocks * BLOCK), jnp.bfloat16)],
+        compiler_params=limit,
+    )
+    late = {key: piece for key, piece in held.items() if key not in early}
+    late.update({(d, m + 1): (kind, across(piece, 1), begin) for (d, m), (kind, piece, begin) in list(late.items())})
+    late_distances = [d for d in range(count) if d not in distances]
+    last_pieces = {**late, **{key: p for key, p in got.items() if key[0] in late_distances}}
+    buffers, spec = operands_of(last_pieces)
+    return call(
+        product_kernel,
+        jax.ShapeDtypeStruct((out_rows, out_cols), jnp.float32),
+        buffers + [part, g_cols],
+        "product",
+        tuple(late),
+        spec,
+        late_distances,
+        scratch_shapes=[
+            pltpu.VMEM((4 * a_rows, out_cols), jnp.bfloat16),
+            pltpu.VMEM((len(late_distances) * BLOCK, row_blocks * BLOCK), jnp.bfloat16),
+            pltpu.VMEM((row_blocks * BLOCK, out_cols), jnp.float32),
+            *[pltpu.VMEM((row_blocks * BLOCK, 4 * a_rows), jnp.bfloat16)] * 2,
+        ],
+        compiler_params=limit,
+    )
+
+
+def gathers(mesh, curl_tiles, gradient):
+    count, width = mesh.shape["row"], mesh.shape["col"]
+    coarse = gradient.shape[1]
+    return (
+        width == 4
+        and count % 2 == 0
+        and curl_tiles.shape[2] // count == BLOCK
+        and curl_tiles.shape[1] // width == 32
+        and coarse % (width * BLOCK) == 0
+        and coarse % (count * 64) == 0
+        and 2 * (curl_tiles.size + gradient.size) <= GATHER_LIMIT
+    )
+
+
 def solution(mesh):
     placed = (P(None, "col", "row"), P(("row", "col"), None), P(), P())
-    return jax.shard_map(
-        body, mesh=mesh, in_specs=placed, out_specs=P("row", "col"), check_vma=False
-    )
+
+    def run(curl_tiles, gradient, a_pattern, g_pattern):
+        body = reducing_body
+        if gathers(mesh, curl_tiles, gradient):
+            body = functools.partial(gathering_body, mesh.shape["row"])
+        return jax.shard_map(
+            body, mesh=mesh, in_specs=placed, out_specs=P("row", "col"), check_vma=False
+        )(curl_tiles, gradient, a_pattern, g_pattern)
+
+    return run

time: 150 us -> 39.5 us (0.26)
  waiting for transfers between devices: 87.5 us -> 15.5 us
  blocking collectives: 40.2 us -> 0 us
  starting transfers between devices: 0.04 us -> 19.3 us
  between operations: 13.4 us -> 0.09 us
  matrix products: 7.56 us -> 0 us
  Pallas kernels: 0 us -> 3.93 us
    reduce_scatter x2 -> x0, waiting for transfers between devices: 87.5 us -> none  [the longest x1 69.6 us: body(): lax.psum_scatter(lax.dot_general(portion, product_t, (((0,), (1,)), ((),...]
    all_gather x2 -> x0, blocking collectives: 40.2 us -> none  [the longest x1 33.8 us: body(): g_strided = lax.all_gather(masked_g, 'row', axis=0, tiled=True)]
    ppermute x0 -> x20, starting transfers between devices: none -> 19.3 us  [the longest x6 11.4 us: gathering_body(): lax.ppermute(back, axes, backward)]
    ppermute x0 -> x20, waiting for transfers between devices: none -> 15.5 us  [the longest x6 9.79 us: gathering_body(): lax.ppermute(back, axes, backward)]
    dot_general x4 -> x0, matrix products: 7.56 us -> none  [the longest x1 3.5 us: body(): lax.dot_general(portion, product_t, (((0,), (1,)), ((), ())), precision=l...]
    pallas_call x0 -> x6, Pallas kernels: none -> 3.93 us  [call(): pl.pallas_call(functools.partial(kernel, *sizes, *given), out_shape=out,...]
  transfers between devices with their start and end apart: 2 -> 20, of which waited for: 2 -> 11; matrix products, arithmetic and copies ran while one was open for 0% -> 0% of each run, Pallas kernels for 0% -> 2%
where the time goes in v2:
time: 39.5 us; the launch traced here: 38.8 us
  starting transfers between devices  19.3 us (49%)
  waiting for transfers between devices  15.5 us (39%)
  Pallas kernels  3.93 us (10%)
    ppermute x6, starting transfers between devices, gathering_body(): lax.ppermute(back, axes, backward)  11.4 us
    ppermute x6, waiting for transfers between devices, gathering_body(): lax.ppermute(back, axes, backward)  9.79 us
    pallas_call x6, Pallas kernels, call(): pl.pallas_call(functools.partial(kernel, *sizes, *given), out_shape=out,...  3.93 us
    ppermute x6, waiting for transfers between devices, gathering_body(): lax.ppermute(ahead, axes, forward)  3.51 us
    ppermute x6, starting transfers between devices, across(): return lax.ppermute(piece, axes, [(i, i ^ mask) for i in range(4 * count)])  2.92 us
    ppermute x1, starting transfers between devices, gathering_body(): lax.ppermute(diagonal, axes, [(i, j ^ 2) for i, j in split])  2.67 us
    ppermute x1, waiting for transfers between devices, gathering_body(): held[half, 0] = ('cross', lax.ppermute(straight, axes, split), 0)  2.03 us
    ppermute x6, starting transfers between devices, gathering_body(): lax.ppermute(ahead, axes, forward)  1.89 us
  transfers between devices with their start and end apart: 20, of which 11 were waited for; matrix products, arithmetic and copies ran while one was open for 0% of the time, Pallas kernels for 2%

profile of v2, /device:TPU:0, one launch (start us, length us, event | category | flops | bytes accessed | tf_op | source)
XLA Modules:
  0.0 38.8 jit_solution(6287671084421641408)
XLA Ops:
  0.0 1.0 %pack.1.refs_0_ = bf16[640,128]{1,0:T(8,128)(2,1)S(1)} custom-call(s32[8,8]{1,0:T(8,128)} %a_pattern.1, s32[8,12]{1,0:T(8,128)} %g_pattern.1, bf16[8,32,128]{2,1,0:T(8,128)(2,1)} %a_ref.1, bf16[32,1536]{1,0:T(8,128)(2,1)} %g_ref.1), custom_call_target="tpu_custom_call" | custom-call | tf_op jit(solution)/shard_map/pack/pallas_call | solution.py:253
  1.0 3.0 %collective-permute-start.10 = (bf16[640,128]{1,0:T(8,128)(2,1)S(1)}, bf16[640,128]{1,0:T(8,128)(2,1)S(1)}, u32[]{:S(2)}, u32[]{:S(2)}) collective-permute-start(bf16[640,128]{1,0:T(8,128)(2,1)S(1)} %pack.1.refs_0_), channel_id=1, source_target_pairs={{0,4},{1,5},{2,6},{3,7},{8,0},{9,1},{10,2},{11,3},{16,8},{17,9},{1... | collective-permute-start | bytes 491528 | tf_op jit(solution)/shard_map/ppermute | solution.py:316
  4.0 0.1 collective-permute-start.7
  4.1 1.9 %collective-permute-start = (bf16[640,128]{1,0:T(8,128)(2,1)S(1)}, bf16[640,128]{1,0:T(8,128)(2,1)S(1)}, u32[]{:S(2)}, u32[]{:S(2)}) collective-permute-start(bf16[640,128]{1,0:T(8,128)(2,1)S(1)} %pack.1.refs_0_), channel_id=1, source_target_pairs={{0,2},{1,3},{2,0},{3,1},{4,6},{5,7},{6,4},{7,5},{8,10},{9,11},{10,... | collective-permute-start | bytes 491528 | tf_op jit(solution)/shard_map/ppermute | solution.py:270
  6.0 2.3 %collective-permute-done.10.refs_3_ = bf16[640,128]{1,0:T(8,128)(2,1)S(1)} collective-permute-done((bf16[640,128]{1,0:T(8,128)(2,1)S(1)}, bf16[640,128]{1,0:T(8,128)(2,1)S(1)}, u32[]{:S(2)}, u32[]{:S(2)}) %collective-permute-start.10) | collective-permute-done | bytes 163872 | tf_op jit(solution)/shard_map/ppermute | solution.py:316
  8.3 1.7 %collective-permute-start.11 = (bf16[640,128]{1,0:T(8,128)(2,1)S(1)}, bf16[640,128]{1,0:T(8,128)(2,1)S(1)}, u32[]{:S(2)}, u32[]{:S(2)}) collective-permute-start(bf16[640,128]{1,0:T(8,128)(2,1)S(1)} %collective-permute-done.10.refs_3_), channel_id=1, source_target_pairs={{0,4},{1,5},{2,6},{3,7},{8,0},{9,1},{10,2},{11,3},{16,8},{17,9},{1... | collective-permute-start | bytes 491528 | tf_op jit(solution)/shard_map/ppermute | solution.py:316
  10.0 0.0 collective-permute-done.7.refs_2_
  10.0 0.3 collective-permute-start.8
  10.3 0.0 collective-permute-done.refs_1_
  10.3 1.7 %collective-permute-start.3 = (bf16[640,128]{1,0:T(8,128)(2,1)S(1)}, bf16[640,128]{1,0:T(8,128)(2,1)S(1)}, u32[]{:S(2)}, u32[]{:S(2)}) collective-permute-start(bf16[640,128]{1,0:T(8,128)(2,1)S(1)} %collective-permute-done.refs_1_), channel_id=1, source_target_pairs={{0,4},{1,5},{2,6},{3,7},{8,0},{9,1},{10,2},{11,3},{16,8},{17,9},{1... | collective-permute-start | bytes 491528 | tf_op jit(solution)/shard_map/ppermute | solution.py:316
  12.0 0.3 collective-permute-start.1
  12.3 3.1 %collective-permute-done.11.refs_5_ = bf16[640,128]{1,0:T(8,128)(2,1)S(1)} collective-permute-done((bf16[640,128]{1,0:T(8,128)(2,1)S(1)}, bf16[640,128]{1,0:T(8,128)(2,1)S(1)}, u32[]{:S(2)}, u32[]{:S(2)}) %collective-permute-start.11) | collective-permute-done | bytes 163872 | tf_op jit(solution)/shard_map/ppermute | solution.py:316
  15.4 1.7 %collective-permute-start.12 = (bf16[640,128]{1,0:T(8,128)(2,1)S(1)}, bf16[640,128]{1,0:T(8,128)(2,1)S(1)}, u32[]{:S(2)}, u32[]{:S(2)}) collective-permute-start(bf16[640,128]{1,0:T(8,128)(2,1)S(1)} %collective-permute-done.11.refs_5_), channel_id=1, source_target_pairs={{0,4},{1,5},{2,6},{3,7},{8,0},{9,1},{10,2},{11,3},{16,8},{17,9},{1... | collective-permute-start | bytes 491528 | tf_op jit(solution)/shard_map/ppermute | solution.py:316
  17.1 0.0 collective-permute-done.8.refs_4_
  17.1 0.3 collective-permute-start.9
  17.4 1.5 %collective-permute-done.3.refs_9_ = bf16[640,128]{1,0:T(8,128)(2,1)S(1)} collective-permute-done((bf16[640,128]{1,0:T(8,128)(2,1)S(1)}, bf16[640,128]{1,0:T(8,128)(2,1)S(1)}, u32[]{:S(2)}, u32[]{:S(2)}) %collective-permute-start.3) | collective-permute-done | bytes 163872 | tf_op jit(solution)/shard_map/ppermute | solution.py:316
  18.9 1.7 %collective-permute-start.4 = (bf16[640,128]{1,0:T(8,128)(2,1)S(1)}, bf16[640,128]{1,0:T(8,128)(2,1)S(1)}, u32[]{:S(2)}, u32[]{:S(2)}) collective-permute-start(bf16[640,128]{1,0:T(8,128)(2,1)S(1)} %collective-permute-done.3.refs_9_), channel_id=1, source_target_pairs={{0,4},{1,5},{2,6},{3,7},{8,0},{9,1},{10,2},{11,3},{16,8},{17,9},{1... | collective-permute-start | bytes 491528 | tf_op jit(solution)/shard_map/ppermute | solution.py:316
  20.6 0.0 collective-permute-done.1.refs_8_
  20.6 0.3 collective-permute-start.2
  21.0 1.5 %collective-permute-done.12.refs_1_.refs_7_ = bf16[640,128]{1,0:T(8,128)(2,1)S(1)} collective-permute-done((bf16[640,128]{1,0:T(8,128)(2,1)S(1)}, bf16[640,128]{1,0:T(8,128)(2,1)S(1)}, u32[]{:S(2)}, u32[]{:S(2)}) %collective-permute-start.12) | collective-permute-done | bytes 163872 | tf_op jit(solution)/shard_map/ppermute | solution.py:316
  22.4 1.1 %collective-permute-done.9.refs_0_.refs_6_ = bf16[640,128]{1,0:T(8,128)(2,1)S(1)} collective-permute-done((bf16[640,128]{1,0:T(8,128)(2,1)S(1)}, bf16[640,128]{1,0:T(8,128)(2,1)S(1)}, u32[]{:S(2)}, u32[]{:S(2)}) %collective-permute-start.9) | collective-permute-done | bytes 163872 | tf_op jit(solution)/shard_map/ppermute | solution.py:316
  23.5 0.7 %collective-permute-done.4.refs_1_.refs_11_ = bf16[640,128]{1,0:T(8,128)(2,1)S(1)} collective-permute-done((bf16[640,128]{1,0:T(8,128)(2,1)S(1)}, bf16[640,128]{1,0:T(8,128)(2,1)S(1)}, u32[]{:S(2)}, u32[]{:S(2)}) %collective-permute-start.4) | collective-permute-done | bytes 163872 | tf_op jit(solution)/shard_map/ppermute | solution.py:316
  24.2 1.7 %collective-permute-done.2.refs_0_.refs_10_ = bf16[640,128]{1,0:T(8,128)(2,1)S(1)} collective-permute-done((bf16[640,128]{1,0:T(8,128)(2,1)S(1)}, bf16[640,128]{1,0:T(8,128)(2,1)S(1)}, u32[]{:S(2)}, u32[]{:S(2)}) %collective-permute-start.2) | collective-permute-done | bytes 163872 | tf_op jit(solution)/shard_map/ppermute | solution.py:316
  25.9 0.2 collect.1
  26.1 0.1 collective-permute-start.19
  26.2 0.4 %collective-permute-start.5 = (bf16[512,128]{1,0:T(8,128)(2,1)S(1)}, bf16[512,128]{1,0:T(8,128)(2,1)S(1)}, u32[]{:S(2)}, u32[]{:S(2)}) collective-permute-start(bf16[512,128]{1,0:T(8,128)(2,1)S(1)} %get-tuple-element.13), channel_id=1, source_target_pairs={{0,8},{1,9},{2,10},{3,11},{8,16},{9,17},{10,18},{11,19},{16,24},{1... | collective-permute-start | bytes 393224 | tf_op jit(solution)/shard_map/ppermute | solution.py:316
  26.6 1.7 %collective-permute-start.6 = (bf16[512,128]{1,0:T(8,128)(2,1)S(1)}, bf16[512,128]{1,0:T(8,128)(2,1)S(1)}, u32[]{:S(2)}, u32[]{:S(2)}) collective-permute-start(bf16[512,128]{1,0:T(8,128)(2,1)S(1)} %get-tuple-element.14), channel_id=1, source_target_pairs={{0,4},{1,5},{2,6},{3,7},{8,0},{9,1},{10,2},{11,3},{16,8},{17,9},{1... | collective-permute-start | bytes 393224 | tf_op jit(solution)/shard_map/ppermute | solution.py:316
  28.3 0.1 cut.3
  28.4 0.4 %collective-permute-start.13 = (bf16[512,128]{1,0:T(8,128)(2,1)S(1)}, bf16[512,128]{1,0:T(8,128)(2,1)S(1)}, u32[]{:S(2)}, u32[]{:S(2)}) collective-permute-start(bf16[512,128]{1,0:T(8,128)(2,1)S(1)} %get-tuple-element.15), channel_id=1, source_target_pairs={{0,8},{2,10},{8,16},{10,18},{16,24},{18,26},{24,28},{26,30},{28,20... | collective-permute-start | bytes 393224 | tf_op jit(solution)/shard_map/ppermute | solution.py:323
  28.8 2.7 %collective-permute-start.14 = (bf16[512,128]{1,0:T(8,128)(2,1)S(1)}, bf16[512,128]{1,0:T(8,128)(2,1)S(1)}, u32[]{:S(2)}, u32[]{:S(2)}) collective-permute-start(bf16[512,128]{1,0:T(8,128)(2,1)S(1)} %get-tuple-element.16), channel_id=1, source_target_pairs={{0,10},{2,8},{8,18},{10,16},{16,26},{18,24},{24,30},{26,28},{28,22... | collective-permute-start | bytes 393224 | tf_op jit(solution)/shard_map/ppermute | solution.py:324
  31.5 0.7 %collective-permute-done.5.refs_0_ = bf16[512,128]{1,0:T(8,128)(2,1)S(1)} collective-permute-done((bf16[512,128]{1,0:T(8,128)(2,1)S(1)}, bf16[512,128]{1,0:T(8,128)(2,1)S(1)}, u32[]{:S(2)}, u32[]{:S(2)}) %collective-permute-start.5) | collective-permute-done | bytes 131104 | tf_op jit(solution)/shard_map/ppermute | solution.py:316
  32.2 0.0 collective-permute-start.15
  32.2 0.8 %collective-permute-done.6.refs_1_ = bf16[512,128]{1,0:T(8,128)(2,1)S(1)} collective-permute-done((bf16[512,128]{1,0:T(8,128)(2,1)S(1)}, bf16[512,128]{1,0:T(8,128)(2,1)S(1)}, u32[]{:S(2)}, u32[]{:S(2)}) %collective-permute-start.6) | collective-permute-done | bytes 131104 | tf_op jit(solution)/shard_map/ppermute | solution.py:316
  33.0 0.0 collective-permute-start.16
  33.0 2.0 %collective-permute-done.13.refs_2_ = bf16[512,128]{1,0:T(8,128)(2,1)S(1)} collective-permute-done((bf16[512,128]{1,0:T(8,128)(2,1)S(1)}, bf16[512,128]{1,0:T(8,128)(2,1)S(1)}, u32[]{:S(2)}, u32[]{:S(2)}) %collective-permute-start.13) | collective-permute-done | bytes 131104 | tf_op jit(solution)/shard_map/ppermute | solution.py:323
  35.0 0.0 collective-permute-start.17
  35.0 0.0 collective-permute-done.14.refs_3_
  35.0 1.0 %collective-permute-start.18 = (bf16[512,128]{1,0:T(8,128)(2,1)S(1)}, bf16[512,128]{1,0:T(8,128)(2,1)S(1)}, u32[]{:S(2)}, u32[]{:S(2)}) collective-permute-start(bf16[512,128]{1,0:T(8,128)(2,1)S(1)} %collective-permute-done.14.refs_3_), channel_id=1, source_target_pairs={{0,1},{1,0},{2,3},{3,2},{4,5},{5,4},{6,7},{7,6},{8,9},{9,8},{10,11... | collective-permute-start | bytes 393224 | tf_op jit(solution)/shard_map/ppermute | solution.py:270
  36.0 0.0 collective-permute-done.19.refs_1_.refs_9_
  36.0 0.8 %early.1 = (f32[256,1024]{1,0:T(8,128)S(1)}, bf16[1024,384]{1,0:T(8,128)(2,1)S(1)}) custom-call(bf16[4992,128]{1,0:T(8,128)(2,1)S(1)} %get-tuple-element.17.refs_0_.refs_8_, bf16[4992,128]{1,0:T(8,128)(2,1)S(1)} %collective-permute-done.19.refs_1_.refs_9_), custom_call_target="tpu_custom_call" | custom-call | tf_op jit(solution)/shard_map/early/pallas_call | solution.py:253
  36.8 0.0 collective-permute-done.15.refs_4_
  36.8 0.0 collective-permute-done.16.refs_5_
  36.8 0.0 collective-permute-done.17.refs_6_
  36.8 0.2 collective-permute-done.18.refs_7_
  37.0 1.9 %product.1 = f32[192,384]{1,0:T(8,128)} custom-call(bf16[512,128]{1,0:T(8,128)(2,1)S(1)} %collective-permute-done.5.refs_0_, bf16[512,128]{1,0:T(8,128)(2,1)S(1)} %collective-permute-done.6.refs_1_, bf16[512,128]{1,0:T(8,128)(2,1)S(1)} %collective-permute-done.13.refs_2_, bf16[512,128]{1,0:T(8,128)(2,1)S(1)} %collective-permute-done.14.refs_3_, ...), custom_call_target="tpu_custom_call" | custom-call | tf_op jit(solution)/shard_map/product/pallas_call | solution.py:253
  (1 shorter events, 0.0 us)
Async XLA Ops:
  1.0 7.3 %collective-permute-start.10 = (bf16[640,128]{1,0:T(8,128)(2,1)S(1)}, bf16[640,128]{1,0:T(8,128)(2,1)S(1)}, u32[]{:S(2)}, u32[]{:S(2)}) collective-permute-start(bf16[640,128]{1,0:T(8,128)(2,1)S(1)} %pack.1.refs_0_), channel_id=1, source_target_pairs={{0,4},{1,5},{2,6},{3,7},{8,0},{9,1},{10,2},{11,3},{16,8},{17,9},{1... | collective-permute-start | bytes 491528 | tf_op jit(solution)/shard_map/ppermute | solution.py:316
  4.0 5.9 %collective-permute-start.7 = (bf16[640,128]{1,0:T(8,128)(2,1)S(1)}, bf16[640,128]{1,0:T(8,128)(2,1)S(1)}, u32[]{:S(2)}, u32[]{:S(2)}) collective-permute-start(bf16[640,128]{1,0:T(8,128)(2,1)S(1)} %pack.1.refs_0_), channel_id=1, source_target_pairs={{0,8},{1,9},{2,10},{3,11},{8,16},{9,17},{10,18},{11,19},{16,24},{1... | collective-permute-start | bytes 491528 | tf_op jit(solution)/shard_map/ppermute | solution.py:316
  4.1 6.2 %collective-permute-start = (bf16[640,128]{1,0:T(8,128)(2,1)S(1)}, bf16[640,128]{1,0:T(8,128)(2,1)S(1)}, u32[]{:S(2)}, u32[]{:S(2)}) collective-permute-start(bf16[640,128]{1,0:T(8,128)(2,1)S(1)} %pack.1.refs_0_), channel_id=1, source_target_pairs={{0,2},{1,3},{2,0},{3,1},{4,6},{5,7},{6,4},{7,5},{8,10},{9,11},{10,... | collective-permute-start | bytes 491528 | tf_op jit(solution)/shard_map/ppermute | solution.py:270
  8.3 7.1 %collective-permute-start.11 = (bf16[640,128]{1,0:T(8,128)(2,1)S(1)}, bf16[640,128]{1,0:T(8,128)(2,1)S(1)}, u32[]{:S(2)}, u32[]{:S(2)}) collective-permute-start(bf16[640,128]{1,0:T(8,128)(2,1)S(1)} %collective-permute-done.10.refs_3_), channel_id=1, source_target_pairs={{0,4},{1,5},{2,6},{3,7},{8,0},{9,1},{10,2},{11,3},{16,8},{17,9},{1... | collective-permute-start | bytes 491528 | tf_op jit(solution)/shard_map/ppermute | solution.py:316
  10.0 7.1 %collective-permute-start.8 = (bf16[640,128]{1,0:T(8,128)(2,1)S(1)}, bf16[640,128]{1,0:T(8,128)(2,1)S(1)}, u32[]{:S(2)}, u32[]{:S(2)}) collective-permute-start(bf16[640,128]{1,0:T(8,128)(2,1)S(1)} %collective-permute-done.7.refs_2_), channel_id=1, source_target_pairs={{0,8},{1,9},{2,10},{3,11},{8,16},{9,17},{10,18},{11,19},{16,24},{1... | collective-permute-start | bytes 491528 | tf_op jit(solution)/shard_map/ppermute | solution.py:316
  10.3 8.6 %collective-permute-start.3 = (bf16[640,128]{1,0:T(8,128)(2,1)S(1)}, bf16[640,128]{1,0:T(8,128)(2,1)S(1)}, u32[]{:S(2)}, u32[]{:S(2)}) collective-permute-start(bf16[640,128]{1,0:T(8,128)(2,1)S(1)} %collective-permute-done.refs_1_), channel_id=1, source_target_pairs={{0,4},{1,5},{2,6},{3,7},{8,0},{9,1},{10,2},{11,3},{16,8},{17,9},{1... | collective-permute-start | bytes 491528 | tf_op jit(solution)/shard_map/ppermute | solution.py:316
  12.0 8.6 %collective-permute-start.1 = (bf16[640,128]{1,0:T(8,128)(2,1)S(1)}, bf16[640,128]{1,0:T(8,128)(2,1)S(1)}, u32[]{:S(2)}, u32[]{:S(2)}) collective-permute-start(bf16[640,128]{1,0:T(8,128)(2,1)S(1)} %collective-permute-done.refs_1_), channel_id=1, source_target_pairs={{0,8},{1,9},{2,10},{3,11},{8,16},{9,17},{10,18},{11,19},{16,24},{1... | collective-permute-start | bytes 491528 | tf_op jit(solution)/shard_map/ppermute | solution.py:316
  15.4 7.0 %collective-permute-start.12 = (bf16[640,128]{1,0:T(8,128)(2,1)S(1)}, bf16[640,128]{1,0:T(8,128)(2,1)S(1)}, u32[]{:S(2)}, u32[]{:S(2)}) collective-permute-start(bf16[640,128]{1,0:T(8,128)(2,1)S(1)} %collective-permute-done.11.refs_5_), channel_id=1, source_target_pairs={{0,4},{1,5},{2,6},{3,7},{8,0},{9,1},{10,2},{11,3},{16,8},{17,9},{1... | collective-permute-start | bytes 491528 | tf_op jit(solution)/shard_map/ppermute | solution.py:316
  17.1 6.4 %collective-permute-start.9 = (bf16[640,128]{1,0:T(8,128)(2,1)S(1)}, bf16[640,128]{1,0:T(8,128)(2,1)S(1)}, u32[]{:S(2)}, u32[]{:S(2)}) collective-permute-start(bf16[640,128]{1,0:T(8,128)(2,1)S(1)} %collective-permute-done.8.refs_4_), channel_id=1, source_target_pairs={{0,8},{1,9},{2,10},{3,11},{8,16},{9,17},{10,18},{11,19},{16,24},{1... | collective-permute-start | bytes 491528 | tf_op jit(solution)/shard_map/ppermute | solution.py:316
  18.9 5.3 %collective-permute-start.4 = (bf16[640,128]{1,0:T(8,128)(2,1)S(1)}, bf16[640,128]{1,0:T(8,128)(2,1)S(1)}, u32[]{:S(2)}, u32[]{:S(2)}) collective-permute-start(bf16[640,128]{1,0:T(8,128)(2,1)S(1)} %collective-permute-done.3.refs_9_), channel_id=1, source_target_pairs={{0,4},{1,5},{2,6},{3,7},{8,0},{9,1},{10,2},{11,3},{16,8},{17,9},{1... | collective-permute-start | bytes 491528 | tf_op jit(solution)/shard_map/ppermute | solution.py:316
  20.6 5.3 %collective-permute-start.2 = (bf16[640,128]{1,0:T(8,128)(2,1)S(1)}, bf16[640,128]{1,0:T(8,128)(2,1)S(1)}, u32[]{:S(2)}, u32[]{:S(2)}) collective-permute-start(bf16[640,128]{1,0:T(8,128)(2,1)S(1)} %collective-permute-done.1.refs_8_), channel_id=1, source_target_pairs={{0,8},{1,9},{2,10},{3,11},{8,16},{9,17},{10,18},{11,19},{16,24},{1... | collective-permute-start | bytes 491528 | tf_op jit(solution)/shard_map/ppermute | solution.py:316
  26.1 9.9 %collective-permute-start.19 = (bf16[4992,128]{1,0:T(8,128)(2,1)S(1)}, bf16[4992,128]{1,0:T(8,128)(2,1)S(1)}, u32[]{:S(2)}, u32[]{:S(2)}) collective-permute-start(bf16[4992,128]{1,0:T(8,128)(2,1)S(1)} %get-tuple-element.18), channel_id=1, source_target_pairs={{0,1},{1,0},{2,3},{3,2},{4,5},{5,4},{6,7},{7,6},{8,9},{9,8},{10,11... | collective-permute-start | bytes 3833864 | tf_op jit(solution)/shard_map/ppermute | solution.py:270
  26.2 5.9 %collective-permute-start.5 = (bf16[512,128]{1,0:T(8,128)(2,1)S(1)}, bf16[512,128]{1,0:T(8,128)(2,1)S(1)}, u32[]{:S(2)}, u32[]{:S(2)}) collective-permute-start(bf16[512,128]{1,0:T(8,128)(2,1)S(1)} %get-tuple-element.13), channel_id=1, source_target_pairs={{0,8},{1,9},{2,10},{3,11},{8,16},{9,17},{10,18},{11,19},{16,24},{1... | collective-permute-start | bytes 393224 | tf_op jit(solution)/shard_map/ppermute | solution.py:316
  26.6 6.3 %collective-permute-start.6 = (bf16[512,128]{1,0:T(8,128)(2,1)S(1)}, bf16[512,128]{1,0:T(8,128)(2,1)S(1)}, u32[]{:S(2)}, u32[]{:S(2)}) collective-permute-start(bf16[512,128]{1,0:T(8,128)(2,1)S(1)} %get-tuple-element.14), channel_id=1, source_target_pairs={{0,4},{1,5},{2,6},{3,7},{8,0},{9,1},{10,2},{11,3},{16,8},{17,9},{1... | collective-permute-start | bytes 393224 | tf_op jit(solution)/shard_map/ppermute | solution.py:316
  28.4 6.6 %collective-permute-start.13 = (bf16[512,128]{1,0:T(8,128)(2,1)S(1)}, bf16[512,128]{1,0:T(8,128)(2,1)S(1)}, u32[]{:S(2)}, u32[]{:S(2)}) collective-permute-start(bf16[512,128]{1,0:T(8,128)(2,1)S(1)} %get-tuple-element.15), channel_id=1, source_target_pairs={{0,8},{2,10},{8,16},{10,18},{16,24},{18,26},{24,28},{26,30},{28,20... | collective-permute-start | bytes 393224 | tf_op jit(solution)/shard_map/ppermute | solution.py:323
  28.8 6.2 %collective-permute-start.14 = (bf16[512,128]{1,0:T(8,128)(2,1)S(1)}, bf16[512,128]{1,0:T(8,128)(2,1)S(1)}, u32[]{:S(2)}, u32[]{:S(2)}) collective-permute-start(bf16[512,128]{1,0:T(8,128)(2,1)S(1)} %get-tuple-element.16), channel_id=1, source_target_pairs={{0,10},{2,8},{8,18},{10,16},{16,26},{18,24},{24,30},{26,28},{28,22... | collective-permute-start | bytes 393224 | tf_op jit(solution)/shard_map/ppermute | solution.py:324
  32.2 4.6 %collective-permute-start.15 = (bf16[512,128]{1,0:T(8,128)(2,1)S(1)}, bf16[512,128]{1,0:T(8,128)(2,1)S(1)}, u32[]{:S(2)}, u32[]{:S(2)}) collective-permute-start(bf16[512,128]{1,0:T(8,128)(2,1)S(1)} %collective-permute-done.5.refs_0_), channel_id=1, source_target_pairs={{0,1},{1,0},{2,3},{3,2},{4,5},{5,4},{6,7},{7,6},{8,9},{9,8},{10,11... | collective-permute-start | bytes 393224 | tf_op jit(solution)/shard_map/ppermute | solution.py:270
  33.0 3.8 %collective-permute-start.16 = (bf16[512,128]{1,0:T(8,128)(2,1)S(1)}, bf16[512,128]{1,0:T(8,128)(2,1)S(1)}, u32[]{:S(2)}, u32[]{:S(2)}) collective-permute-start(bf16[512,128]{1,0:T(8,128)(2,1)S(1)} %collective-permute-done.6.refs_1_), channel_id=1, source_target_pairs={{0,1},{1,0},{2,3},{3,2},{4,5},{5,4},{6,7},{7,6},{8,9},{9,8},{10,11... | collective-permute-start | bytes 393224 | tf_op jit(solution)/shard_map/ppermute | solution.py:270
  35.0 1.8 %collective-permute-start.17 = (bf16[512,128]{1,0:T(8,128)(2,1)S(1)}, bf16[512,128]{1,0:T(8,128)(2,1)S(1)}, u32[]{:S(2)}, u32[]{:S(2)}) collective-permute-start(bf16[512,128]{1,0:T(8,128)(2,1)S(1)} %collective-permute-done.13.refs_2_), channel_id=1, source_target_pairs={{0,1},{1,0},{2,3},{3,2},{4,5},{5,4},{6,7},{7,6},{8,9},{9,8},{10,11... | collective-permute-start | bytes 393224 | tf_op jit(solution)/shard_map/ppermute | solution.py:270
  35.0 2.0 %collective-permute-start.18 = (bf16[512,128]{1,0:T(8,128)(2,1)S(1)}, bf16[512,128]{1,0:T(8,128)(2,1)S(1)}, u32[]{:S(2)}, u32[]{:S(2)}) collective-permute-start(bf16[512,128]{1,0:T(8,128)(2,1)S(1)} %collective-permute-done.14.refs_3_), channel_id=1, source_target_pairs={{0,1},{1,0},{2,3},{3,2},{4,5},{5,4},{6,7},{7,6},{8,9},{9,8},{10,11... | collective-permute-start | bytes 393224 | tf_op jit(solution)/shard_map/ppermute | solution.py:270

commit v3 on v2

--- a/solution.py
+++ b/solution.py
@@ -309,11 +309,12 @@
         return call(cut_kernel, [rows(crossing)] * len(items), operands, "cut", items, compiler_params=limit)
 
     for m in (0, 2):
-        ahead = back = held[0, m][1]
+        ahead = back = own
         for step in range(1, half):
             if m == 2 and step == half - 1:
                 ahead, back = cut([((0, 0), (1, 1), 0), ((1, 1), (-1, -1), 0)], ahead, back)
-            ahead, back = lax.ppermute(ahead, axes, forward), lax.ppermute(back, axes, backward)
+            ways = [[(i, j ^ m) if step == 1 else (i, j) for i, j in way] for way in (forward, backward)]
+            ahead, back = lax.ppermute(ahead, axes, ways[0]), lax.ppermute(back, axes, ways[1])
             kind = "cross" if m == 2 and step == half - 1 else "whole"
             held[step, m], held[count - step, m] = (kind, ahead, 0), (kind, back, 0)
     split = [pair for pair in forward if pair[0] % 2 == 0] + [pair for pair in backward if pair[0] % 2 == 1]

time: 39.5 us -> 38.2 us (0.967); the launches traced: 38.8 us -> 38 us
  waiting for transfers between devices: 15.5 us -> 14.6 us
    ppermute x12, starting transfers between devices: 13.3 us -> 15.9 us  [the longest x6 15.7 us: gathering_body(): lax.ppermute(back, axes, ways[1])]
    ppermute x6, starting transfers between devices: 2.92 us -> 1.82 us  [across(): return lax.ppermute(piece, axes, [(i, i ^ mask) for i in range(4 * count)])]
    ppermute x1, starting transfers between devices: 2.67 us -> 1.61 us  [gathering_body(): lax.ppermute(diagonal, axes, [(i, j ^ 2) for i, j in split])]
    ppermute x1, waiting for transfers between devices: 2.03 us -> 1.38 us  [gathering_body(): held[half, 0] = ('cross', lax.ppermute(straight, axes, split), 0)]
where the time goes in v3:
time: 38.2 us; the launch traced here: 38 us
  starting transfers between devices  19.5 us (51%)
  waiting for transfers between devices  14.6 us (38%)
  Pallas kernels  3.92 us (10%)
    ppermute x6, starting transfers between devices, gathering_body(): lax.ppermute(back, axes, ways[1])  15.7 us
    ppermute x6, waiting for transfers between devices, gathering_body(): lax.ppermute(ahead, axes, ways[0])  7.57 us
    ppermute x6, waiting for transfers between devices, gathering_body(): lax.ppermute(back, axes, ways[1])  5.39 us
    pallas_call x6, Pallas kernels, call(): pl.pallas_call(functools.partial(kernel, *sizes, *given), out_shape=out,...  3.92 us
    ppermute x6, starting transfers between devices, across(): return lax.ppermute(piece, axes, [(i, i ^ mask) for i in range(4 * count)])  1.82 us
    ppermute x1, starting transfers between devices, gathering_body(): lax.ppermute(diagonal, axes, [(i, j ^ 2) for i, j in split])  1.61 us
    ppermute x1, waiting for transfers between devices, gathering_body(): held[half, 0] = ('cross', lax.ppermute(straight, axes, split), 0)  1.38 us
  transfers between devices with their start and end apart: 20, of which 11 were waited for; matrix products, arithmetic and copies ran while one was open for 0% of the time, Pallas kernels for 2%

profile of v3, /device:TPU:0, one launch (start us, length us, event | category | flops | bytes accessed | tf_op | source)
XLA Modules:
  0.0 38.0 jit_solution(17817115769313656584)
XLA Ops:
  0.0 1.0 %pack.1.refs_0_ = bf16[640,128]{1,0:T(8,128)(2,1)S(1)} custom-call(s32[8,8]{1,0:T(8,128)} %a_pattern.1, s32[8,12]{1,0:T(8,128)} %g_pattern.1, bf16[8,32,128]{2,1,0:T(8,128)(2,1)} %a_ref.1, bf16[32,1536]{1,0:T(8,128)(2,1)} %g_ref.1), custom_call_target="tpu_custom_call" | custom-call | tf_op jit(solution)/shard_map/pack/pallas_call | solution.py:253
  1.0 3.0 %collective-permute-start.9 = (bf16[640,128]{1,0:T(8,128)(2,1)S(1)}, bf16[640,128]{1,0:T(8,128)(2,1)S(1)}, u32[]{:S(2)}, u32[]{:S(2)}) collective-permute-start(bf16[640,128]{1,0:T(8,128)(2,1)S(1)} %pack.1.refs_0_), channel_id=1, source_target_pairs={{0,4},{1,5},{2,6},{3,7},{8,0},{9,1},{10,2},{11,3},{16,8},{17,9},{1... | collective-permute-start | bytes 491528 | tf_op jit(solution)/shard_map/ppermute | solution.py:317
  4.0 0.1 collective-permute-start.6
  4.1 2.8 %collective-permute-start.2 = (bf16[640,128]{1,0:T(8,128)(2,1)S(1)}, bf16[640,128]{1,0:T(8,128)(2,1)S(1)}, u32[]{:S(2)}, u32[]{:S(2)}) collective-permute-start(bf16[640,128]{1,0:T(8,128)(2,1)S(1)} %pack.1.refs_0_), channel_id=1, source_target_pairs={{0,6},{1,7},{2,4},{3,5},{8,2},{9,3},{10,0},{11,1},{16,10},{17,11},... | collective-permute-start | bytes 491528 | tf_op jit(solution)/shard_map/ppermute | solution.py:317
  7.0 0.1 collective-permute-start
  7.1 2.3 %collective-permute-done.9.refs_3_ = bf16[640,128]{1,0:T(8,128)(2,1)S(1)} collective-permute-done((bf16[640,128]{1,0:T(8,128)(2,1)S(1)}, bf16[640,128]{1,0:T(8,128)(2,1)S(1)}, u32[]{:S(2)}, u32[]{:S(2)}) %collective-permute-start.9) | collective-permute-done | bytes 163872 | tf_op jit(solution)/shard_map/ppermute | solution.py:317
  9.3 2.9 %collective-permute-start.10 = (bf16[640,128]{1,0:T(8,128)(2,1)S(1)}, bf16[640,128]{1,0:T(8,128)(2,1)S(1)}, u32[]{:S(2)}, u32[]{:S(2)}) collective-permute-start(bf16[640,128]{1,0:T(8,128)(2,1)S(1)} %collective-permute-done.9.refs_3_), channel_id=1, source_target_pairs={{0,4},{1,5},{2,6},{3,7},{8,0},{9,1},{10,2},{11,3},{16,8},{17,9},{1... | collective-permute-start | bytes 491528 | tf_op jit(solution)/shard_map/ppermute | solution.py:317
  12.2 0.0 collective-permute-done.6.refs_2_
  12.2 0.0 collective-permute-start.7
  12.2 1.2 %collective-permute-start.18 = (bf16[640,128]{1,0:T(8,128)(2,1)S(1)}, bf16[640,128]{1,0:T(8,128)(2,1)S(1)}, u32[]{:S(2)}, u32[]{:S(2)}) collective-permute-start(bf16[640,128]{1,0:T(8,128)(2,1)S(1)} %pack.1.refs_0_), channel_id=1, source_target_pairs={{0,2},{1,3},{2,0},{3,1},{4,6},{5,7},{6,4},{7,5},{8,10},{9,11},{10,... | collective-permute-start | bytes 491528 | tf_op jit(solution)/shard_map/ppermute | solution.py:270
  13.5 0.8 %collective-permute-done.2.refs_9_ = bf16[640,128]{1,0:T(8,128)(2,1)S(1)} collective-permute-done((bf16[640,128]{1,0:T(8,128)(2,1)S(1)}, bf16[640,128]{1,0:T(8,128)(2,1)S(1)}, u32[]{:S(2)}, u32[]{:S(2)}) %collective-permute-start.2) | collective-permute-done | bytes 163872 | tf_op jit(solution)/shard_map/ppermute | solution.py:317
  14.3 2.9 %collective-permute-start.3 = (bf16[640,128]{1,0:T(8,128)(2,1)S(1)}, bf16[640,128]{1,0:T(8,128)(2,1)S(1)}, u32[]{:S(2)}, u32[]{:S(2)}) collective-permute-start(bf16[640,128]{1,0:T(8,128)(2,1)S(1)} %collective-permute-done.2.refs_9_), channel_id=1, source_target_pairs={{0,4},{1,5},{2,6},{3,7},{8,0},{9,1},{10,2},{11,3},{16,8},{17,9},{1... | collective-permute-start | bytes 491528 | tf_op jit(solution)/shard_map/ppermute | solution.py:317
  17.2 0.9 %collective-permute-done.refs_8_ = bf16[640,128]{1,0:T(8,128)(2,1)S(1)} collective-permute-done((bf16[640,128]{1,0:T(8,128)(2,1)S(1)}, bf16[640,128]{1,0:T(8,128)(2,1)S(1)}, u32[]{:S(2)}, u32[]{:S(2)}) %collective-permute-start) | collective-permute-done | bytes 163872 | tf_op jit(solution)/shard_map/ppermute | solution.py:317
  18.0 0.0 collective-permute-start.1
  18.0 0.0 collective-permute-done.10.refs_5_
  18.0 2.0 %collective-permute-start.11 = (bf16[640,128]{1,0:T(8,128)(2,1)S(1)}, bf16[640,128]{1,0:T(8,128)(2,1)S(1)}, u32[]{:S(2)}, u32[]{:S(2)}) collective-permute-start(bf16[640,128]{1,0:T(8,128)(2,1)S(1)} %collective-permute-done.10.refs_5_), channel_id=1, source_target_pairs={{0,4},{1,5},{2,6},{3,7},{8,0},{9,1},{10,2},{11,3},{16,8},{17,9},{1... | collective-permute-start | bytes 491528 | tf_op jit(solution)/shard_map/ppermute | solution.py:317
  20.1 0.1 collective-permute-done.7.refs_4_
  20.2 0.0 collective-permute-start.8
  20.2 0.0 collective-permute-done.18.refs_1_
  20.2 0.8 %collective-permute-done.3.refs_1_.refs_11_ = bf16[640,128]{1,0:T(8,128)(2,1)S(1)} collective-permute-done((bf16[640,128]{1,0:T(8,128)(2,1)S(1)}, bf16[640,128]{1,0:T(8,128)(2,1)S(1)}, u32[]{:S(2)}, u32[]{:S(2)}) %collective-permute-start.3) | collective-permute-done | bytes 163872 | tf_op jit(solution)/shard_map/ppermute | solution.py:317
  21.0 2.8 %collective-permute-done.1.refs_0_.refs_10_ = bf16[640,128]{1,0:T(8,128)(2,1)S(1)} collective-permute-done((bf16[640,128]{1,0:T(8,128)(2,1)S(1)}, bf16[640,128]{1,0:T(8,128)(2,1)S(1)}, u32[]{:S(2)}, u32[]{:S(2)}) %collective-permute-start.1) | collective-permute-done | bytes 163872 | tf_op jit(solution)/shard_map/ppermute | solution.py:317
  23.8 0.0 collective-permute-done.11.refs_1_.refs_7_
  23.8 1.8 %collective-permute-done.8.refs_0_.refs_6_ = bf16[640,128]{1,0:T(8,128)(2,1)S(1)} collective-permute-done((bf16[640,128]{1,0:T(8,128)(2,1)S(1)}, bf16[640,128]{1,0:T(8,128)(2,1)S(1)}, u32[]{:S(2)}, u32[]{:S(2)}) %collective-permute-start.8) | collective-permute-done | bytes 163872 | tf_op jit(solution)/shard_map/ppermute | solution.py:317
  25.6 0.2 collect.1
  25.8 0.1 collective-permute-start.19
  25.9 0.1 collective-permute-start.4
  26.0 2.0 %collective-permute-start.5 = (bf16[512,128]{1,0:T(8,128)(2,1)S(1)}, bf16[512,128]{1,0:T(8,128)(2,1)S(1)}, u32[]{:S(2)}, u32[]{:S(2)}) collective-permute-start(bf16[512,128]{1,0:T(8,128)(2,1)S(1)} %get-tuple-element.14), channel_id=1, source_target_pairs={{0,4},{1,5},{2,6},{3,7},{8,0},{9,1},{10,2},{11,3},{16,8},{17,9},{1... | collective-permute-start | bytes 393224 | tf_op jit(solution)/shard_map/ppermute | solution.py:317
  28.0 0.1 cut.3
  28.1 0.1 collective-permute-start.12
  28.2 1.6 %collective-permute-start.13 = (bf16[512,128]{1,0:T(8,128)(2,1)S(1)}, bf16[512,128]{1,0:T(8,128)(2,1)S(1)}, u32[]{:S(2)}, u32[]{:S(2)}) collective-permute-start(bf16[512,128]{1,0:T(8,128)(2,1)S(1)} %get-tuple-element.16), channel_id=1, source_target_pairs={{0,10},{2,8},{8,18},{10,16},{16,26},{18,24},{24,30},{26,28},{28,22... | collective-permute-start | bytes 393224 | tf_op jit(solution)/shard_map/ppermute | solution.py:325
  29.8 2.1 %collective-permute-done.4.refs_0_ = bf16[512,128]{1,0:T(8,128)(2,1)S(1)} collective-permute-done((bf16[512,128]{1,0:T(8,128)(2,1)S(1)}, bf16[512,128]{1,0:T(8,128)(2,1)S(1)}, u32[]{:S(2)}, u32[]{:S(2)}) %collective-permute-start.4) | collective-permute-done | bytes 131104 | tf_op jit(solution)/shard_map/ppermute | solution.py:317
  31.8 0.0 collective-permute-start.14
  31.8 1.4 %collective-permute-done.5.refs_1_ = bf16[512,128]{1,0:T(8,128)(2,1)S(1)} collective-permute-done((bf16[512,128]{1,0:T(8,128)(2,1)S(1)}, bf16[512,128]{1,0:T(8,128)(2,1)S(1)}, u32[]{:S(2)}, u32[]{:S(2)}) %collective-permute-start.5) | collective-permute-done | bytes 131104 | tf_op jit(solution)/shard_map/ppermute | solution.py:317
  33.3 0.0 collective-permute-start.15
  33.3 1.4 %collective-permute-done.12.refs_2_ = bf16[512,128]{1,0:T(8,128)(2,1)S(1)} collective-permute-done((bf16[512,128]{1,0:T(8,128)(2,1)S(1)}, bf16[512,128]{1,0:T(8,128)(2,1)S(1)}, u32[]{:S(2)}, u32[]{:S(2)}) %collective-permute-start.12) | collective-permute-done | bytes 131104 | tf_op jit(solution)/shard_map/ppermute | solution.py:324
  34.6 0.0 collective-permute-start.16
  34.6 0.0 collective-permute-done.13.refs_3_
  34.6 0.5 %collective-permute-start.17 = (bf16[512,128]{1,0:T(8,128)(2,1)S(1)}, bf16[512,128]{1,0:T(8,128)(2,1)S(1)}, u32[]{:S(2)}, u32[]{:S(2)}) collective-permute-start(bf16[512,128]{1,0:T(8,128)(2,1)S(1)} %collective-permute-done.13.refs_3_), channel_id=1, source_target_pairs={{0,1},{1,0},{2,3},{3,2},{4,5},{5,4},{6,7},{7,6},{8,9},{9,8},{10,11... | collective-permute-start | bytes 393224 | tf_op jit(solution)/shard_map/ppermute | solution.py:270
  35.2 0.0 collective-permute-done.19.refs_1_.refs_9_
  35.2 0.8 %early.1 = (f32[256,1024]{1,0:T(8,128)S(1)}, bf16[1024,384]{1,0:T(8,128)(2,1)S(1)}) custom-call(bf16[4992,128]{1,0:T(8,128)(2,1)S(1)} %get-tuple-element.17.refs_0_.refs_8_, bf16[4992,128]{1,0:T(8,128)(2,1)S(1)} %collective-permute-done.19.refs_1_.refs_9_), custom_call_target="tpu_custom_call" | custom-call | tf_op jit(solution)/shard_map/early/pallas_call | solution.py:253
  36.0 0.0 collective-permute-done.14.refs_4_
  36.0 0.0 collective-permute-done.15.refs_5_
  36.0 0.0 collective-permute-done.16.refs_6_
  36.0 0.2 collective-permute-done.17.refs_7_
  36.2 1.9 %product.1 = f32[192,384]{1,0:T(8,128)} custom-call(bf16[512,128]{1,0:T(8,128)(2,1)S(1)} %collective-permute-done.4.refs_0_, bf16[512,128]{1,0:T(8,128)(2,1)S(1)} %collective-permute-done.5.refs_1_, bf16[512,128]{1,0:T(8,128)(2,1)S(1)} %collective-permute-done.12.refs_2_, bf16[512,128]{1,0:T(8,128)(2,1)S(1)} %collective-permute-done.13.refs_3_, ...), custom_call_target="tpu_custom_call" | custom-call | tf_op jit(solution)/shard_map/product/pallas_call | solution.py:253
  (1 shorter events, 0.0 us)
Async XLA Ops:
  1.0 8.3 %collective-permute-start.9 = (bf16[640,128]{1,0:T(8,128)(2,1)S(1)}, bf16[640,128]{1,0:T(8,128)(2,1)S(1)}, u32[]{:S(2)}, u32[]{:S(2)}) collective-permute-start(bf16[640,128]{1,0:T(8,128)(2,1)S(1)} %pack.1.refs_0_), channel_id=1, source_target_pairs={{0,4},{1,5},{2,6},{3,7},{8,0},{9,1},{10,2},{11,3},{16,8},{17,9},{1... | collective-permute-start | bytes 491528 | tf_op jit(solution)/shard_map/ppermute | solution.py:317
  4.0 8.2 %collective-permute-start.6 = (bf16[640,128]{1,0:T(8,128)(2,1)S(1)}, bf16[640,128]{1,0:T(8,128)(2,1)S(1)}, u32[]{:S(2)}, u32[]{:S(2)}) collective-permute-start(bf16[640,128]{1,0:T(8,128)(2,1)S(1)} %pack.1.refs_0_), channel_id=1, source_target_pairs={{0,8},{1,9},{2,10},{3,11},{8,16},{9,17},{10,18},{11,19},{16,24},{1... | collective-permute-start | bytes 491528 | tf_op jit(solution)/shard_map/ppermute | solution.py:317
  4.1 10.2 %collective-permute-start.2 = (bf16[640,128]{1,0:T(8,128)(2,1)S(1)}, bf16[640,128]{1,0:T(8,128)(2,1)S(1)}, u32[]{:S(2)}, u32[]{:S(2)}) collective-permute-start(bf16[640,128]{1,0:T(8,128)(2,1)S(1)} %pack.1.refs_0_), channel_id=1, source_target_pairs={{0,6},{1,7},{2,4},{3,5},{8,2},{9,3},{10,0},{11,1},{16,10},{17,11},... | collective-permute-start | bytes 491528 | tf_op jit(solution)/shard_map/ppermute | solution.py:317
  7.0 11.1 %collective-permute-start = (bf16[640,128]{1,0:T(8,128)(2,1)S(1)}, bf16[640,128]{1,0:T(8,128)(2,1)S(1)}, u32[]{:S(2)}, u32[]{:S(2)}) collective-permute-start(bf16[640,128]{1,0:T(8,128)(2,1)S(1)} %pack.1.refs_0_), channel_id=1, source_target_pairs={{0,10},{1,11},{2,8},{3,9},{8,18},{9,19},{10,16},{11,17},{16,26},{1... | collective-permute-start | bytes 491528 | tf_op jit(solution)/shard_map/ppermute | solution.py:317
  9.3 8.7 %collective-permute-start.10 = (bf16[640,128]{1,0:T(8,128)(2,1)S(1)}, bf16[640,128]{1,0:T(8,128)(2,1)S(1)}, u32[]{:S(2)}, u32[]{:S(2)}) collective-permute-start(bf16[640,128]{1,0:T(8,128)(2,1)S(1)} %collective-permute-done.9.refs_3_), channel_id=1, source_target_pairs={{0,4},{1,5},{2,6},{3,7},{8,0},{9,1},{10,2},{11,3},{16,8},{17,9},{1... | collective-permute-start | bytes 491528 | tf_op jit(solution)/shard_map/ppermute | solution.py:317
  12.2 7.9 %collective-permute-start.7 = (bf16[640,128]{1,0:T(8,128)(2,1)S(1)}, bf16[640,128]{1,0:T(8,128)(2,1)S(1)}, u32[]{:S(2)}, u32[]{:S(2)}) collective-permute-start(bf16[640,128]{1,0:T(8,128)(2,1)S(1)} %collective-permute-done.6.refs_2_), channel_id=1, source_target_pairs={{0,8},{1,9},{2,10},{3,11},{8,16},{9,17},{10,18},{11,19},{16,24},{1... | collective-permute-start | bytes 491528 | tf_op jit(solution)/shard_map/ppermute | solution.py:317
  12.2 7.9 %collective-permute-start.18 = (bf16[640,128]{1,0:T(8,128)(2,1)S(1)}, bf16[640,128]{1,0:T(8,128)(2,1)S(1)}, u32[]{:S(2)}, u32[]{:S(2)}) collective-permute-start(bf16[640,128]{1,0:T(8,128)(2,1)S(1)} %pack.1.refs_0_), channel_id=1, source_target_pairs={{0,2},{1,3},{2,0},{3,1},{4,6},{5,7},{6,4},{7,5},{8,10},{9,11},{10,... | collective-permute-start | bytes 491528 | tf_op jit(solution)/shard_map/ppermute | solution.py:270
  14.3 6.7 %collective-permute-start.3 = (bf16[640,128]{1,0:T(8,128)(2,1)S(1)}, bf16[640,128]{1,0:T(8,128)(2,1)S(1)}, u32[]{:S(2)}, u32[]{:S(2)}) collective-permute-start(bf16[640,128]{1,0:T(8,128)(2,1)S(1)} %collective-permute-done.2.refs_9_), channel_id=1, source_target_pairs={{0,4},{1,5},{2,6},{3,7},{8,0},{9,1},{10,2},{11,3},{16,8},{17,9},{1... | collective-permute-start | bytes 491528 | tf_op jit(solution)/shard_map/ppermute | solution.py:317
  18.0 5.8 %collective-permute-start.1 = (bf16[640,128]{1,0:T(8,128)(2,1)S(1)}, bf16[640,128]{1,0:T(8,128)(2,1)S(1)}, u32[]{:S(2)}, u32[]{:S(2)}) collective-permute-start(bf16[640,128]{1,0:T(8,128)(2,1)S(1)} %collective-permute-done.refs_8_), channel_id=1, source_target_pairs={{0,8},{1,9},{2,10},{3,11},{8,16},{9,17},{10,18},{11,19},{16,24},{1... | collective-permute-start | bytes 491528 | tf_op jit(solution)/shard_map/ppermute | solution.py:317
  18.0 5.8 %collective-permute-start.11 = (bf16[640,128]{1,0:T(8,128)(2,1)S(1)}, bf16[640,128]{1,0:T(8,128)(2,1)S(1)}, u32[]{:S(2)}, u32[]{:S(2)}) collective-permute-start(bf16[640,128]{1,0:T(8,128)(2,1)S(1)} %collective-permute-done.10.refs_5_), channel_id=1, source_target_pairs={{0,4},{1,5},{2,6},{3,7},{8,0},{9,1},{10,2},{11,3},{16,8},{17,9},{1... | collective-permute-start | bytes 491528 | tf_op jit(solution)/shard_map/ppermute | solution.py:317
  20.2 5.4 %collective-permute-start.8 = (bf16[640,128]{1,0:T(8,128)(2,1)S(1)}, bf16[640,128]{1,0:T(8,128)(2,1)S(1)}, u32[]{:S(2)}, u32[]{:S(2)}) collective-permute-start(bf16[640,128]{1,0:T(8,128)(2,1)S(1)} %collective-permute-done.7.refs_4_), channel_id=1, source_target_pairs={{0,8},{1,9},{2,10},{3,11},{8,16},{9,17},{10,18},{11,19},{16,24},{1... | collective-permute-start | bytes 491528 | tf_op jit(solution)/shard_map/ppermute | solution.py:317
  25.8 9.4 %collective-permute-start.19 = (bf16[4992,128]{1,0:T(8,128)(2,1)S(1)}, bf16[4992,128]{1,0:T(8,128)(2,1)S(1)}, u32[]{:S(2)}, u32[]{:S(2)}) collective-permute-start(bf16[4992,128]{1,0:T(8,128)(2,1)S(1)} %get-tuple-element.18), channel_id=1, source_target_pairs={{0,1},{1,0},{2,3},{3,2},{4,5},{5,4},{6,7},{7,6},{8,9},{9,8},{10,11... | collective-permute-start | bytes 3833864 | tf_op jit(solution)/shard_map/ppermute | solution.py:270
  25.9 5.9 %collective-permute-start.4 = (bf16[512,128]{1,0:T(8,128)(2,1)S(1)}, bf16[512,128]{1,0:T(8,128)(2,1)S(1)}, u32[]{:S(2)}, u32[]{:S(2)}) collective-permute-start(bf16[512,128]{1,0:T(8,128)(2,1)S(1)} %get-tuple-element.13), channel_id=1, source_target_pairs={{0,8},{1,9},{2,10},{3,11},{8,16},{9,17},{10,18},{11,19},{16,24},{1... | collective-permute-start | bytes 393224 | tf_op jit(solution)/shard_map/ppermute | solution.py:317
  26.0 7.3 %collective-permute-start.5 = (bf16[512,128]{1,0:T(8,128)(2,1)S(1)}, bf16[512,128]{1,0:T(8,128)(2,1)S(1)}, u32[]{:S(2)}, u32[]{:S(2)}) collective-permute-start(bf16[512,128]{1,0:T(8,128)(2,1)S(1)} %get-tuple-element.14), channel_id=1, source_target_pairs={{0,4},{1,5},{2,6},{3,7},{8,0},{9,1},{10,2},{11,3},{16,8},{17,9},{1... | collective-permute-start | bytes 393224 | tf_op jit(solution)/shard_map/ppermute | solution.py:317
  28.1 6.6 %collective-permute-start.12 = (bf16[512,128]{1,0:T(8,128)(2,1)S(1)}, bf16[512,128]{1,0:T(8,128)(2,1)S(1)}, u32[]{:S(2)}, u32[]{:S(2)}) collective-permute-start(bf16[512,128]{1,0:T(8,128)(2,1)S(1)} %get-tuple-element.15), channel_id=1, source_target_pairs={{0,8},{2,10},{8,16},{10,18},{16,24},{18,26},{24,28},{26,30},{28,20... | collective-permute-start | bytes 393224 | tf_op jit(solution)/shard_map/ppermute | solution.py:324
  28.2 6.5 %collective-permute-start.13 = (bf16[512,128]{1,0:T(8,128)(2,1)S(1)}, bf16[512,128]{1,0:T(8,128)(2,1)S(1)}, u32[]{:S(2)}, u32[]{:S(2)}) collective-permute-start(bf16[512,128]{1,0:T(8,128)(2,1)S(1)} %get-tuple-element.16), channel_id=1, source_target_pairs={{0,10},{2,8},{8,18},{10,16},{16,26},{18,24},{24,30},{26,28},{28,22... | collective-permute-start | bytes 393224 | tf_op jit(solution)/shard_map/ppermute | solution.py:325
  31.8 4.1 %collective-permute-start.14 = (bf16[512,128]{1,0:T(8,128)(2,1)S(1)}, bf16[512,128]{1,0:T(8,128)(2,1)S(1)}, u32[]{:S(2)}, u32[]{:S(2)}) collective-permute-start(bf16[512,128]{1,0:T(8,128)(2,1)S(1)} %collective-permute-done.4.refs_0_), channel_id=1, source_target_pairs={{0,1},{1,0},{2,3},{3,2},{4,5},{5,4},{6,7},{7,6},{8,9},{9,8},{10,11... | collective-permute-start | bytes 393224 | tf_op jit(solution)/shard_map/ppermute | solution.py:270
  33.3 2.7 %collective-permute-start.15 = (bf16[512,128]{1,0:T(8,128)(2,1)S(1)}, bf16[512,128]{1,0:T(8,128)(2,1)S(1)}, u32[]{:S(2)}, u32[]{:S(2)}) collective-permute-start(bf16[512,128]{1,0:T(8,128)(2,1)S(1)} %collective-permute-done.5.refs_1_), channel_id=1, source_target_pairs={{0,1},{1,0},{2,3},{3,2},{4,5},{5,4},{6,7},{7,6},{8,9},{9,8},{10,11... | collective-permute-start | bytes 393224 | tf_op jit(solution)/shard_map/ppermute | solution.py:270
  34.6 1.3 %collective-permute-start.16 = (bf16[512,128]{1,0:T(8,128)(2,1)S(1)}, bf16[512,128]{1,0:T(8,128)(2,1)S(1)}, u32[]{:S(2)}, u32[]{:S(2)}) collective-permute-start(bf16[512,128]{1,0:T(8,128)(2,1)S(1)} %collective-permute-done.12.refs_2_), channel_id=1, source_target_pairs={{0,1},{1,0},{2,3},{3,2},{4,5},{5,4},{6,7},{7,6},{8,9},{9,8},{10,11... | collective-permute-start | bytes 393224 | tf_op jit(solution)/shard_map/ppermute | solution.py:270
  34.6 1.5 %collective-permute-start.17 = (bf16[512,128]{1,0:T(8,128)(2,1)S(1)}, bf16[512,128]{1,0:T(8,128)(2,1)S(1)}, u32[]{:S(2)}, u32[]{:S(2)}) collective-permute-start(bf16[512,128]{1,0:T(8,128)(2,1)S(1)} %collective-permute-done.13.refs_3_), channel_id=1, source_target_pairs={{0,1},{1,0},{2,3},{3,2},{4,5},{5,4},{6,7},{7,6},{8,9},{9,8},{10,11... | collective-permute-start | bytes 393224 | tf_op jit(solution)/shard_map/ppermute | solution.py:270

commit v4 on v2

--- a/solution.py
+++ b/solution.py
@@ -186,15 +186,22 @@
                 g_rows[below, j * BLOCK : (j + 1) * BLOCK] = piece.ref[pl.ds(start + j * rows_here, rows_here), :]
 
 
-def partial_product(pieces, m, distances, g_rows):
+def window_rows(row, count, coarse, g_rows, turned):
+    out_rows = coarse // count
+    turned[...] = jnp.transpose(g_rows[...])
+    shift = pl.multiple_of(row * out_rows - first_window(row, count, coarse) * BLOCK, 64)
+    return turned[pl.ds(shift, out_rows), :]
+
+
+def partial_product(pieces, m, distances, g_turned):
     part = None
     for i in range(0, len(distances), 2):
         pair = distances[i : i + 2]
         tiles = [pieces[d, m].tiles() for d in pair]
         term = lax.dot_general(
-            g_rows[i * BLOCK : (i + len(pair)) * BLOCK, :],
+            g_turned[:, i * BLOCK : (i + len(pair)) * BLOCK],
             tiles[0] if len(tiles) == 1 else jnp.concatenate(tiles, axis=1),
-            (((0,), (1,)), ((), ())),
+            (((1,), (1,)), ((), ())),
             preferred_element_type=jnp.float32,
         )
         part = term if part is None else part + term
@@ -202,17 +209,19 @@
 
 
 def early_kernel(count, rows_here, coarse, spec, distances, *refs):
-    part_ref, g_cols, g_rows = refs[-3:]
+    part_ref, g_cols, g_rows, turned = refs[-4:]
     sizes = layout(count, rows_here, coarse)
     a_rows = sizes[0]
     pieces = pieces_of(spec, refs, sizes)
     place_kernel_part(pieces, count, rows_here, coarse, distances, g_cols, g_rows)
+    g_turned = window_rows(lax.axis_index("row"), count, coarse, g_rows, turned)
     for m in range(4):
-        part_ref[:, m * a_rows : (m + 1) * a_rows] = partial_product(pieces, m, distances, g_rows)
+        part_ref[:, m * a_rows : (m + 1) * a_rows] = partial_product(pieces, m, distances, g_turned)
 
 
 def product_kernel(count, rows_here, coarse, late, spec, distances, *refs):
-    part_ref, g_early, out_ref, g_cols, g_rows, total, highs, lows = refs[-8:]
+    part_ref, g_early, out_ref, g_cols, g_rows, turned, terms = refs[-7:]
+    out_rows = out_ref.shape[0]
     sizes = layout(count, rows_here, coarse)
     a_rows = sizes[0]
     pieces = pieces_of(spec, refs, sizes)
@@ -220,19 +229,15 @@
     place_kernel_part({key: pieces[key] for key in late}, count, rows_here, coarse, distances, g_cols, g_rows)
     rest = {key: piece for key, piece in pieces.items() if key not in late}
     place_kernel_part(rest, count, rows_here, coarse, distances, None, g_rows)
+    g_turned = window_rows(lax.axis_index("row"), count, coarse, g_rows, turned)
     for m in range(4):
         columns = slice(m * a_rows, (m + 1) * a_rows)
-        part = part_ref[:, columns] + partial_product(pieces, m, distances, g_rows)
+        part = part_ref[:, columns] + partial_product(pieces, m, distances, g_turned)
         high = part.astype(jnp.bfloat16)
-        highs[:, columns] = high
-        lows[:, columns] = (part - high.astype(jnp.float32)).astype(jnp.bfloat16)
-    total[...] = jnp.dot(lows[...], g_cols[...], preferred_element_type=jnp.float32) + jnp.dot(
-        highs[...], g_cols[...], preferred_element_type=jnp.float32
-    )
-    row = lax.axis_index("row")
-    out_rows = out_ref.shape[0]
-    shift = pl.multiple_of(row * out_rows - first_window(row, count, coarse) * BLOCK, 64)
-    out_ref[...] = total[pl.ds(shift, out_rows), :]
+        terms[:out_rows, columns] = high
+        terms[out_rows:, columns] = (part - high.astype(jnp.float32)).astype(jnp.bfloat16)
+    total = jnp.dot(terms[...], g_cols[...], preferred_element_type=jnp.float32)
+    out_ref[...] = total[:out_rows] + total[out_rows:]
 
 
 def gathering_body(count, curl_tiles, gradient, a_pattern, g_pattern):
@@ -248,6 +253,10 @@
 
     def rows(n):
         return pltpu.VMEM((n, BLOCK), jnp.bfloat16)
+
+    def turning(distances):
+        shape = (distances * BLOCK, row_blocks * BLOCK)
+        return [pltpu.VMEM(shape, jnp.bfloat16), pltpu.VMEM(shape[::-1], jnp.bfloat16)]
 
     def call(kernel, out, operands, name, *given, **options):
         return pl.pallas_call(
@@ -308,38 +317,42 @@
     def cut(items, *operands):
         return call(cut_kernel, [rows(crossing)] * len(items), operands, "cut", items, compiler_params=limit)
 
-    for m in (0, 2):
-        ahead = back = held[0, m][1]
-        for step in range(1, half):
-            if m == 2 and step == half - 1:
-                ahead, back = cut([((0, 0), (1, 1), 0), ((1, 1), (-1, -1), 0)], ahead, back)
-            ahead, back = lax.ppermute(ahead, axes, forward), lax.ppermute(back, axes, backward)
-            kind = "cross" if m == 2 and step == half - 1 else "whole"
-            held[step, m], held[count - step, m] = (kind, ahead, 0), (kind, back, 0)
-    split = [pair for pair in forward if pair[0] % 2 == 0] + [pair for pair in backward if pair[0] % 2 == 1]
+    chain = {m: (own, own) for m in (0, 2)}
+    for step, m in ((step, m) for step in range(1, half) for m in (0, 2)):
+        ahead, back = chain[m]
+        kind = "whole"
+        if m == 2 and step == half - 1:
+            ahead, back = cut([((0, 0), (1, 1), 0), ((1, 1), (-1, -1), 0)], ahead, back)
+            kind = "cross"
+        ways = [[(i, j ^ m) if step == 1 else (i, j) for i, j in way] for way in (forward, backward)]
+        back, ahead = lax.ppermute(back, axes, ways[1]), lax.ppermute(ahead, axes, ways[0])
+        chain[m] = ahead, back
+        held[step, m], held[count - step, m] = (kind, ahead, 0), (kind, back, 0)
+    split = [pair for pair in forward if pair[0] % 2 == 1] + [pair for pair in backward if pair[0] % 2 == 0]
     straight, diagonal = cut(
-        [((0, 1), (1, -1), 0), ((0, 1), (1, -1), 1)], held[half - 1, 0][1], held[half + 1, 0][1]
+        [((1, 0), (-1, 1), 0), ((1, 0), (-1, 1), 1)], held[half - 1, 0][1], held[half + 1, 0][1]
     )
     held[half, 0] = ("cross", lax.ppermute(straight, axes, split), 0)
     held[half, 2] = ("cross", lax.ppermute(diagonal, axes, [(i, j ^ 2) for i, j in split]), 0)
-    early = {key: held[key] for key in held if min(key[0], count - key[0]) <= (3, 2)[key[1] // 2]}
+    early = {key: held[key] for key in held if min(key[0], count - key[0]) < half - key[1] // 2}
+    early = dict(sorted(early.items()))
     got = exchange(early)
     distances = [d for d in range(count) if (d, 0) in early and (d, 2) in early]
     buffers, spec = operands_of(got)
     part, g_cols = call(
         early_kernel,
         [
-            pltpu.VMEM((row_blocks * BLOCK, 4 * a_rows), jnp.float32),
+            pltpu.VMEM((out_rows, 4 * a_rows), jnp.float32),
             pltpu.VMEM((4 * a_rows, out_cols), jnp.bfloat16),
         ],
         buffers,
         "early",
         spec,
         distances,
-        scratch_shapes=[pltpu.VMEM((len(distances) * BLOCK, row_blocks * BLOCK), jnp.bfloat16)],
+        scratch_shapes=turning(len(distances)),
         compiler_params=limit,
     )
-    late = {key: piece for key, piece in held.items() if key not in early}
+    late = {key: piece for key, piece in reversed(held.items()) if key not in early}
     late.update({(d, m + 1): (kind, across(piece, 1), begin) for (d, m), (kind, piece, begin) in list(late.items())})
     late_distances = [d for d in range(count) if d not in distances]
     last_pieces = {**late, **{key: p for key, p in got.items() if key[0] in late_distances}}
@@ -354,9 +367,8 @@
         late_distances,
         scratch_shapes=[
             pltpu.VMEM((4 * a_rows, out_cols), jnp.bfloat16),
-            pltpu.VMEM((len(late_distances) * BLOCK, row_blocks * BLOCK), jnp.bfloat16),
-            pltpu.VMEM((row_blocks * BLOCK, out_cols), jnp.float32),
-            *[pltpu.VMEM((row_blocks * BLOCK, 4 * a_rows), jnp.bfloat16)] * 2,
+            *turning(len(late_distances)),
+            pltpu.VMEM((2 * out_rows, 4 * a_rows), jnp.bfloat16),
         ],
         compiler_params=limit,
     )
@@ -368,6 +380,7 @@
     return (
         width == 4
         and count % 2 == 0
+        and count >= 8
         and curl_tiles.shape[2] // count == BLOCK
         and curl_tiles.shape[1] // width == 32
         and coarse % (width * BLOCK) == 0

time: 39.5 us -> 37.7 us (0.954); the launches traced: 38.8 us -> 37.5 us
  waiting for transfers between devices: 15.5 us -> 14.3 us
    ppermute x1, waiting for transfers between devices: 2.03 us -> 0.01 us  [gathering_body(): held[half, 0] = ('cross', lax.ppermute(straight, axes, split), 0)]
    ppermute x12, starting transfers between devices: 13.3 us -> 15.2 us  [the longest x6 8.6 us: gathering_body(): lax.ppermute(ahead, axes, ways[0])]
    ppermute x6, starting transfers between devices: 2.92 us -> 1.34 us  [across(): return lax.ppermute(piece, axes, [(i, i ^ mask) for i in range(4 * count)])]
    ppermute x1, starting transfers between devices: 2.67 us -> 1.12 us  [gathering_body(): lax.ppermute(diagonal, axes, [(i, j ^ 2) for i, j in split])]
    ppermute x1, starting transfers between devices: 0.39 us -> 1.58 us  [gathering_body(): held[half, 0] = ('cross', lax.ppermute(straight, axes, split), 0)]
    ppermute x12, waiting for transfers between devices: 13.3 us -> 13.9 us  [the longest x6 8.61 us: gathering_body(): lax.ppermute(ahead, axes, ways[0])]
  transfers between devices with their start and end apart: 20 -> 20, of which waited for: 11 -> 12; matrix products, arithmetic and copies ran while one was open for 0% -> 0% of each run, Pallas kernels for 2% -> 3%
where the time goes in v4:
time: 37.7 us; the launch traced here: 37.5 us
  starting transfers between devices  19.3 us (51%)
  waiting for transfers between devices  14.3 us (38%)
  Pallas kernels  3.83 us (10%)
    ppermute x6, waiting for transfers between devices, gathering_body(): lax.ppermute(ahead, axes, ways[0])  8.61 us
    ppermute x6, starting transfers between devices, gathering_body(): lax.ppermute(ahead, axes, ways[0])  8.6 us
    ppermute x6, starting transfers between devices, gathering_body(): lax.ppermute(back, axes, ways[1])  6.61 us
    ppermute x6, waiting for transfers between devices, gathering_body(): lax.ppermute(back, axes, ways[1])  5.31 us
    pallas_call x6, Pallas kernels, call(): pl.pallas_call(functools.partial(kernel, *sizes, *given), out_shape=out,...  3.83 us
    ppermute x1, starting transfers between devices, gathering_body(): held[half, 0] = ('cross', lax.ppermute(straight, axes, split), 0)  1.58 us
    ppermute x6, starting transfers between devices, across(): return lax.ppermute(piece, axes, [(i, i ^ mask) for i in range(4 * count)])  1.34 us
    ppermute x1, starting transfers between devices, gathering_body(): lax.ppermute(diagonal, axes, [(i, j ^ 2) for i, j in split])  1.12 us
  transfers between devices with their start and end apart: 20, of which 12 were waited for; matrix products, arithmetic and copies ran while one was open for 0% of the time, Pallas kernels for 3%

profile of v4, /device:TPU:0, one launch (start us, length us, event | category | flops | bytes accessed | tf_op | source)
XLA Modules:
  0.0 37.5 jit_solution(16804769039188415593)
XLA Ops:
  0.0 1.0 %pack.1.refs_0_ = bf16[640,128]{1,0:T(8,128)(2,1)S(1)} custom-call(s32[8,8]{1,0:T(8,128)} %a_pattern.1, s32[8,12]{1,0:T(8,128)} %g_pattern.1, bf16[8,32,128]{2,1,0:T(8,128)(2,1)} %a_ref.1, bf16[32,1536]{1,0:T(8,128)(2,1)} %g_ref.1), custom_call_target="tpu_custom_call" | custom-call | tf_op jit(solution)/shard_map/pack/pallas_call | solution.py:262
  1.0 3.1 %collective-permute-start = (bf16[640,128]{1,0:T(8,128)(2,1)S(1)}, bf16[640,128]{1,0:T(8,128)(2,1)S(1)}, u32[]{:S(2)}, u32[]{:S(2)}) collective-permute-start(bf16[640,128]{1,0:T(8,128)(2,1)S(1)} %pack.1.refs_0_), channel_id=1, source_target_pairs={{0,8},{1,9},{2,10},{3,11},{8,16},{9,17},{10,18},{11,19},{16,24},{1... | collective-permute-start | bytes 491528 | tf_op jit(solution)/shard_map/ppermute | solution.py:328
  4.1 0.0 collective-permute-start.3
  4.1 2.9 %collective-permute-start.10 = (bf16[640,128]{1,0:T(8,128)(2,1)S(1)}, bf16[640,128]{1,0:T(8,128)(2,1)S(1)}, u32[]{:S(2)}, u32[]{:S(2)}) collective-permute-start(bf16[640,128]{1,0:T(8,128)(2,1)S(1)} %pack.1.refs_0_), channel_id=1, source_target_pairs={{0,6},{1,7},{2,4},{3,5},{8,2},{9,3},{10,0},{11,1},{16,10},{17,11},... | collective-permute-start | bytes 491528 | tf_op jit(solution)/shard_map/ppermute | solution.py:328
  7.0 0.1 collective-permute-start.8
  7.0 1.6 %collective-permute-done.refs_2_ = bf16[640,128]{1,0:T(8,128)(2,1)S(1)} collective-permute-done((bf16[640,128]{1,0:T(8,128)(2,1)S(1)}, bf16[640,128]{1,0:T(8,128)(2,1)S(1)}, u32[]{:S(2)}, u32[]{:S(2)}) %collective-permute-start) | collective-permute-done | bytes 163872 | tf_op jit(solution)/shard_map/ppermute | solution.py:328
  8.6 2.5 %collective-permute-start.1 = (bf16[640,128]{1,0:T(8,128)(2,1)S(1)}, bf16[640,128]{1,0:T(8,128)(2,1)S(1)}, u32[]{:S(2)}, u32[]{:S(2)}) collective-permute-start(bf16[640,128]{1,0:T(8,128)(2,1)S(1)} %collective-permute-done.refs_2_), channel_id=1, source_target_pairs={{0,8},{1,9},{2,10},{3,11},{8,16},{9,17},{10,18},{11,19},{16,24},{1... | collective-permute-start | bytes 491528 | tf_op jit(solution)/shard_map/ppermute | solution.py:328
  11.1 0.1 collective-permute-done.3.refs_10_
  11.2 2.5 %collective-permute-start.4 = (bf16[640,128]{1,0:T(8,128)(2,1)S(1)}, bf16[640,128]{1,0:T(8,128)(2,1)S(1)}, u32[]{:S(2)}, u32[]{:S(2)}) collective-permute-start(bf16[640,128]{1,0:T(8,128)(2,1)S(1)} %collective-permute-done.3.refs_10_), channel_id=1, source_target_pairs={{0,4},{1,5},{2,6},{3,7},{8,0},{9,1},{10,2},{11,3},{16,8},{17,9},{1... | collective-permute-start | bytes 491528 | tf_op jit(solution)/shard_map/ppermute | solution.py:328
  13.7 0.7 %collective-permute-start.18 = (bf16[640,128]{1,0:T(8,128)(2,1)S(1)}, bf16[640,128]{1,0:T(8,128)(2,1)S(1)}, u32[]{:S(2)}, u32[]{:S(2)}) collective-permute-start(bf16[640,128]{1,0:T(8,128)(2,1)S(1)} %pack.1.refs_0_), channel_id=1, source_target_pairs={{0,2},{1,3},{2,0},{3,1},{4,6},{5,7},{6,4},{7,5},{8,10},{9,11},{10,... | collective-permute-start | bytes 491528 | tf_op jit(solution)/shard_map/ppermute | solution.py:279
  14.4 1.2 %collective-permute-done.10.refs_11_ = bf16[640,128]{1,0:T(8,128)(2,1)S(1)} collective-permute-done((bf16[640,128]{1,0:T(8,128)(2,1)S(1)}, bf16[640,128]{1,0:T(8,128)(2,1)S(1)}, u32[]{:S(2)}, u32[]{:S(2)}) %collective-permute-start.10) | collective-permute-done | bytes 163872 | tf_op jit(solution)/shard_map/ppermute | solution.py:328
  15.6 0.0 collective-permute-start.11
  15.7 2.0 %collective-permute-done.8.refs_3_ = bf16[640,128]{1,0:T(8,128)(2,1)S(1)} collective-permute-done((bf16[640,128]{1,0:T(8,128)(2,1)S(1)}, bf16[640,128]{1,0:T(8,128)(2,1)S(1)}, u32[]{:S(2)}, u32[]{:S(2)}) %collective-permute-start.8) | collective-permute-done | bytes 163872 | tf_op jit(solution)/shard_map/ppermute | solution.py:328
  17.7 0.0 collective-permute-start.9
  17.7 0.0 collective-permute-done.1.refs_4_
  17.7 1.9 %collective-permute-start.2 = (bf16[640,128]{1,0:T(8,128)(2,1)S(1)}, bf16[640,128]{1,0:T(8,128)(2,1)S(1)}, u32[]{:S(2)}, u32[]{:S(2)}) collective-permute-start(bf16[640,128]{1,0:T(8,128)(2,1)S(1)} %collective-permute-done.1.refs_4_), channel_id=1, source_target_pairs={{0,8},{1,9},{2,10},{3,11},{8,16},{9,17},{10,18},{11,19},{16,24},{1... | collective-permute-start | bytes 491528 | tf_op jit(solution)/shard_map/ppermute | solution.py:328
  19.6 0.0 collective-permute-done.4.refs_8_
  19.6 0.2 collective-permute-start.5
  19.8 0.0 collective-permute-done.18.refs_1_
  19.8 2.7 %collective-permute-done.11.refs_1_.refs_9_ = bf16[640,128]{1,0:T(8,128)(2,1)S(1)} collective-permute-done((bf16[640,128]{1,0:T(8,128)(2,1)S(1)}, bf16[640,128]{1,0:T(8,128)(2,1)S(1)}, u32[]{:S(2)}, u32[]{:S(2)}) %collective-permute-start.11) | collective-permute-done | bytes 163872 | tf_op jit(solution)/shard_map/ppermute | solution.py:328
  22.5 0.5 %collective-permute-done.9.refs_0_.refs_5_ = bf16[640,128]{1,0:T(8,128)(2,1)S(1)} collective-permute-done((bf16[640,128]{1,0:T(8,128)(2,1)S(1)}, bf16[640,128]{1,0:T(8,128)(2,1)S(1)}, u32[]{:S(2)}, u32[]{:S(2)}) %collective-permute-start.9) | collective-permute-done | bytes 163872 | tf_op jit(solution)/shard_map/ppermute | solution.py:328
  23.0 1.8 %collective-permute-done.2.refs_0_.refs_6_ = bf16[640,128]{1,0:T(8,128)(2,1)S(1)} collective-permute-done((bf16[640,128]{1,0:T(8,128)(2,1)S(1)}, bf16[640,128]{1,0:T(8,128)(2,1)S(1)}, u32[]{:S(2)}, u32[]{:S(2)}) %collective-permute-start.2) | collective-permute-done | bytes 163872 | tf_op jit(solution)/shard_map/ppermute | solution.py:328
  24.7 0.2 collective-permute-done.5.refs_1_.refs_7_
  24.9 0.2 collect.1
  25.1 0.1 collective-permute-start.19
  25.2 1.0 %collective-permute-start.12 = (bf16[512,128]{1,0:T(8,128)(2,1)S(1)}, bf16[512,128]{1,0:T(8,128)(2,1)S(1)}, u32[]{:S(2)}, u32[]{:S(2)}) collective-permute-start(bf16[512,128]{1,0:T(8,128)(2,1)S(1)} %get-tuple-element.15), channel_id=1, source_target_pairs={{0,4},{1,5},{2,6},{3,7},{8,0},{9,1},{10,2},{11,3},{16,8},{17,9},{1... | collective-permute-start | bytes 393224 | tf_op jit(solution)/shard_map/ppermute | solution.py:328
  26.2 1.1 %collective-permute-start.13 = (bf16[512,128]{1,0:T(8,128)(2,1)S(1)}, bf16[512,128]{1,0:T(8,128)(2,1)S(1)}, u32[]{:S(2)}, u32[]{:S(2)}) collective-permute-start(bf16[512,128]{1,0:T(8,128)(2,1)S(1)} %get-tuple-element.16), channel_id=1, source_target_pairs={{0,8},{1,9},{2,10},{3,11},{8,16},{9,17},{10,18},{11,19},{16,24},{1... | collective-permute-start | bytes 393224 | tf_op jit(solution)/shard_map/ppermute | solution.py:328
  27.3 0.1 cut.2
  27.4 1.1 %collective-permute-start.6 = (bf16[512,128]{1,0:T(8,128)(2,1)S(1)}, bf16[512,128]{1,0:T(8,128)(2,1)S(1)}, u32[]{:S(2)}, u32[]{:S(2)}) collective-permute-start(bf16[512,128]{1,0:T(8,128)(2,1)S(1)} %get-tuple-element.13), channel_id=1, source_target_pairs={{1,11},{3,9},{9,19},{11,17},{17,27},{19,25},{25,31},{27,29},{29,23... | collective-permute-start | bytes 393224 | tf_op jit(solution)/shard_map/ppermute | solution.py:336
  28.5 1.6 %collective-permute-start.7 = (bf16[512,128]{1,0:T(8,128)(2,1)S(1)}, bf16[512,128]{1,0:T(8,128)(2,1)S(1)}, u32[]{:S(2)}, u32[]{:S(2)}) collective-permute-start(bf16[512,128]{1,0:T(8,128)(2,1)S(1)} %get-tuple-element.14), channel_id=1, source_target_pairs={{1,9},{3,11},{9,17},{11,19},{17,25},{19,27},{25,29},{27,31},{29,21... | collective-permute-start | bytes 393224 | tf_op jit(solution)/shard_map/ppermute | solution.py:335
  30.1 1.1 %collective-permute-done.12.refs_2_ = bf16[512,128]{1,0:T(8,128)(2,1)S(1)} collective-permute-done((bf16[512,128]{1,0:T(8,128)(2,1)S(1)}, bf16[512,128]{1,0:T(8,128)(2,1)S(1)}, u32[]{:S(2)}, u32[]{:S(2)}) %collective-permute-start.12) | collective-permute-done | bytes 131104 | tf_op jit(solution)/shard_map/ppermute | solution.py:328
  31.1 0.0 collective-permute-start.16
  31.1 2.8 %collective-permute-done.13.refs_3_ = bf16[512,128]{1,0:T(8,128)(2,1)S(1)} collective-permute-done((bf16[512,128]{1,0:T(8,128)(2,1)S(1)}, bf16[512,128]{1,0:T(8,128)(2,1)S(1)}, u32[]{:S(2)}, u32[]{:S(2)}) %collective-permute-start.13) | collective-permute-done | bytes 131104 | tf_op jit(solution)/shard_map/ppermute | solution.py:328
  33.9 0.0 collective-permute-start.17
  33.9 0.0 collective-permute-done.6.refs_0_
  33.9 0.5 %collective-permute-start.14 = (bf16[512,128]{1,0:T(8,128)(2,1)S(1)}, bf16[512,128]{1,0:T(8,128)(2,1)S(1)}, u32[]{:S(2)}, u32[]{:S(2)}) collective-permute-start(bf16[512,128]{1,0:T(8,128)(2,1)S(1)} %collective-permute-done.6.refs_0_), channel_id=1, source_target_pairs={{0,1},{1,0},{2,3},{3,2},{4,5},{5,4},{6,7},{7,6},{8,9},{9,8},{10,11... | collective-permute-start | bytes 393224 | tf_op jit(solution)/shard_map/ppermute | solution.py:279
  34.4 0.0 collective-permute-done.7.refs_1_
  34.4 0.1 collective-permute-start.15
  34.5 0.0 collective-permute-done.19.refs_1_.refs_9_
  34.5 0.8 %early.1 = (f32[192,1024]{1,0:T(8,128)S(1)}, bf16[1024,384]{1,0:T(8,128)(2,1)S(1)}) custom-call(bf16[4992,128]{1,0:T(8,128)(2,1)S(1)} %get-tuple-element.17.refs_0_.refs_8_, bf16[4992,128]{1,0:T(8,128)(2,1)S(1)} %collective-permute-done.19.refs_1_.refs_9_), custom_call_target="tpu_custom_call" | custom-call | tf_op jit(solution)/shard_map/early/pallas_call | solution.py:262
  35.4 0.0 collective-permute-done.16.refs_6_
  35.4 0.0 collective-permute-done.17.refs_7_
  35.4 0.1 collective-permute-done.14.refs_4_
  35.5 0.3 collective-permute-done.15.refs_5_
  35.8 1.7 %product.1 = f32[192,384]{1,0:T(8,128)} custom-call(bf16[512,128]{1,0:T(8,128)(2,1)S(1)} %collective-permute-done.6.refs_0_, bf16[512,128]{1,0:T(8,128)(2,1)S(1)} %collective-permute-done.7.refs_1_, bf16[512,128]{1,0:T(8,128)(2,1)S(1)} %collective-permute-done.12.refs_2_, bf16[512,128]{1,0:T(8,128)(2,1)S(1)} %collective-permute-done.13.refs_3_, ...), custom_call_target="tpu_custom_call" | custom-call | tf_op jit(solution)/shard_map/product/pallas_call | solution.py:262
  (1 shorter events, 0.0 us)
Async XLA Ops:
  1.0 7.6 %collective-permute-start = (bf16[640,128]{1,0:T(8,128)(2,1)S(1)}, bf16[640,128]{1,0:T(8,128)(2,1)S(1)}, u32[]{:S(2)}, u32[]{:S(2)}) collective-permute-start(bf16[640,128]{1,0:T(8,128)(2,1)S(1)} %pack.1.refs_0_), channel_id=1, source_target_pairs={{0,8},{1,9},{2,10},{3,11},{8,16},{9,17},{10,18},{11,19},{16,24},{1... | collective-permute-start | bytes 491528 | tf_op jit(solution)/shard_map/ppermute | solution.py:328
  4.1 7.1 %collective-permute-start.3 = (bf16[640,128]{1,0:T(8,128)(2,1)S(1)}, bf16[640,128]{1,0:T(8,128)(2,1)S(1)}, u32[]{:S(2)}, u32[]{:S(2)}) collective-permute-start(bf16[640,128]{1,0:T(8,128)(2,1)S(1)} %pack.1.refs_0_), channel_id=1, source_target_pairs={{0,4},{1,5},{2,6},{3,7},{8,0},{9,1},{10,2},{11,3},{16,8},{17,9},{1... | collective-permute-start | bytes 491528 | tf_op jit(solution)/shard_map/ppermute | solution.py:328
  4.1 11.6 %collective-permute-start.10 = (bf16[640,128]{1,0:T(8,128)(2,1)S(1)}, bf16[640,128]{1,0:T(8,128)(2,1)S(1)}, u32[]{:S(2)}, u32[]{:S(2)}) collective-permute-start(bf16[640,128]{1,0:T(8,128)(2,1)S(1)} %pack.1.refs_0_), channel_id=1, source_target_pairs={{0,6},{1,7},{2,4},{3,5},{8,2},{9,3},{10,0},{11,1},{16,10},{17,11},... | collective-permute-start | bytes 491528 | tf_op jit(solution)/shard_map/ppermute | solution.py:328
  7.0 10.7 %collective-permute-start.8 = (bf16[640,128]{1,0:T(8,128)(2,1)S(1)}, bf16[640,128]{1,0:T(8,128)(2,1)S(1)}, u32[]{:S(2)}, u32[]{:S(2)}) collective-permute-start(bf16[640,128]{1,0:T(8,128)(2,1)S(1)} %pack.1.refs_0_), channel_id=1, source_target_pairs={{0,10},{1,11},{2,8},{3,9},{8,18},{9,19},{10,16},{11,17},{16,26},{1... | collective-permute-start | bytes 491528 | tf_op jit(solution)/shard_map/ppermute | solution.py:328
  8.6 9.1 %collective-permute-start.1 = (bf16[640,128]{1,0:T(8,128)(2,1)S(1)}, bf16[640,128]{1,0:T(8,128)(2,1)S(1)}, u32[]{:S(2)}, u32[]{:S(2)}) collective-permute-start(bf16[640,128]{1,0:T(8,128)(2,1)S(1)} %collective-permute-done.refs_2_), channel_id=1, source_target_pairs={{0,8},{1,9},{2,10},{3,11},{8,16},{9,17},{10,18},{11,19},{16,24},{1... | collective-permute-start | bytes 491528 | tf_op jit(solution)/shard_map/ppermute | solution.py:328
  11.2 8.4 %collective-permute-start.4 = (bf16[640,128]{1,0:T(8,128)(2,1)S(1)}, bf16[640,128]{1,0:T(8,128)(2,1)S(1)}, u32[]{:S(2)}, u32[]{:S(2)}) collective-permute-start(bf16[640,128]{1,0:T(8,128)(2,1)S(1)} %collective-permute-done.3.refs_10_), channel_id=1, source_target_pairs={{0,4},{1,5},{2,6},{3,7},{8,0},{9,1},{10,2},{11,3},{16,8},{17,9},{1... | collective-permute-start | bytes 491528 | tf_op jit(solution)/shard_map/ppermute | solution.py:328
  13.7 6.0 %collective-permute-start.18 = (bf16[640,128]{1,0:T(8,128)(2,1)S(1)}, bf16[640,128]{1,0:T(8,128)(2,1)S(1)}, u32[]{:S(2)}, u32[]{:S(2)}) collective-permute-start(bf16[640,128]{1,0:T(8,128)(2,1)S(1)} %pack.1.refs_0_), channel_id=1, source_target_pairs={{0,2},{1,3},{2,0},{3,1},{4,6},{5,7},{6,4},{7,5},{8,10},{9,11},{10,... | collective-permute-start | bytes 491528 | tf_op jit(solution)/shard_map/ppermute | solution.py:279
  15.6 6.9 %collective-permute-start.11 = (bf16[640,128]{1,0:T(8,128)(2,1)S(1)}, bf16[640,128]{1,0:T(8,128)(2,1)S(1)}, u32[]{:S(2)}, u32[]{:S(2)}) collective-permute-start(bf16[640,128]{1,0:T(8,128)(2,1)S(1)} %collective-permute-done.10.refs_11_), channel_id=1, source_target_pairs={{0,4},{1,5},{2,6},{3,7},{8,0},{9,1},{10,2},{11,3},{16,8},{17,9},{1... | collective-permute-start | bytes 491528 | tf_op jit(solution)/shard_map/ppermute | solution.py:328
  17.7 5.3 %collective-permute-start.9 = (bf16[640,128]{1,0:T(8,128)(2,1)S(1)}, bf16[640,128]{1,0:T(8,128)(2,1)S(1)}, u32[]{:S(2)}, u32[]{:S(2)}) collective-permute-start(bf16[640,128]{1,0:T(8,128)(2,1)S(1)} %collective-permute-done.8.refs_3_), channel_id=1, source_target_pairs={{0,8},{1,9},{2,10},{3,11},{8,16},{9,17},{10,18},{11,19},{16,24},{1... | collective-permute-start | bytes 491528 | tf_op jit(solution)/shard_map/ppermute | solution.py:328
  17.7 7.1 %collective-permute-start.2 = (bf16[640,128]{1,0:T(8,128)(2,1)S(1)}, bf16[640,128]{1,0:T(8,128)(2,1)S(1)}, u32[]{:S(2)}, u32[]{:S(2)}) collective-permute-start(bf16[640,128]{1,0:T(8,128)(2,1)S(1)} %collective-permute-done.1.refs_4_), channel_id=1, source_target_pairs={{0,8},{1,9},{2,10},{3,11},{8,16},{9,17},{10,18},{11,19},{16,24},{1... | collective-permute-start | bytes 491528 | tf_op jit(solution)/shard_map/ppermute | solution.py:328
  19.6 5.3 %collective-permute-start.5 = (bf16[640,128]{1,0:T(8,128)(2,1)S(1)}, bf16[640,128]{1,0:T(8,128)(2,1)S(1)}, u32[]{:S(2)}, u32[]{:S(2)}) collective-permute-start(bf16[640,128]{1,0:T(8,128)(2,1)S(1)} %collective-permute-done.4.refs_8_), channel_id=1, source_target_pairs={{0,4},{1,5},{2,6},{3,7},{8,0},{9,1},{10,2},{11,3},{16,8},{17,9},{1... | collective-permute-start | bytes 491528 | tf_op jit(solution)/shard_map/ppermute | solution.py:328
  25.1 9.5 %collective-permute-start.19 = (bf16[4992,128]{1,0:T(8,128)(2,1)S(1)}, bf16[4992,128]{1,0:T(8,128)(2,1)S(1)}, u32[]{:S(2)}, u32[]{:S(2)}) collective-permute-start(bf16[4992,128]{1,0:T(8,128)(2,1)S(1)} %get-tuple-element.18), channel_id=1, source_target_pairs={{0,1},{1,0},{2,3},{3,2},{4,5},{5,4},{6,7},{7,6},{8,9},{9,8},{10,11... | collective-permute-start | bytes 3833864 | tf_op jit(solution)/shard_map/ppermute | solution.py:279
  25.2 5.9 %collective-permute-start.12 = (bf16[512,128]{1,0:T(8,128)(2,1)S(1)}, bf16[512,128]{1,0:T(8,128)(2,1)S(1)}, u32[]{:S(2)}, u32[]{:S(2)}) collective-permute-start(bf16[512,128]{1,0:T(8,128)(2,1)S(1)} %get-tuple-element.15), channel_id=1, source_target_pairs={{0,4},{1,5},{2,6},{3,7},{8,0},{9,1},{10,2},{11,3},{16,8},{17,9},{1... | collective-permute-start | bytes 393224 | tf_op jit(solution)/shard_map/ppermute | solution.py:328
  26.2 7.7 %collective-permute-start.13 = (bf16[512,128]{1,0:T(8,128)(2,1)S(1)}, bf16[512,128]{1,0:T(8,128)(2,1)S(1)}, u32[]{:S(2)}, u32[]{:S(2)}) collective-permute-start(bf16[512,128]{1,0:T(8,128)(2,1)S(1)} %get-tuple-element.16), channel_id=1, source_target_pairs={{0,8},{1,9},{2,10},{3,11},{8,16},{9,17},{10,18},{11,19},{16,24},{1... | collective-permute-start | bytes 393224 | tf_op jit(solution)/shard_map/ppermute | solution.py:328
  27.4 6.6 %collective-permute-start.6 = (bf16[512,128]{1,0:T(8,128)(2,1)S(1)}, bf16[512,128]{1,0:T(8,128)(2,1)S(1)}, u32[]{:S(2)}, u32[]{:S(2)}) collective-permute-start(bf16[512,128]{1,0:T(8,128)(2,1)S(1)} %get-tuple-element.13), channel_id=1, source_target_pairs={{1,11},{3,9},{9,19},{11,17},{17,27},{19,25},{25,31},{27,29},{29,23... | collective-permute-start | bytes 393224 | tf_op jit(solution)/shard_map/ppermute | solution.py:336
  28.5 6.0 %collective-permute-start.7 = (bf16[512,128]{1,0:T(8,128)(2,1)S(1)}, bf16[512,128]{1,0:T(8,128)(2,1)S(1)}, u32[]{:S(2)}, u32[]{:S(2)}) collective-permute-start(bf16[512,128]{1,0:T(8,128)(2,1)S(1)} %get-tuple-element.14), channel_id=1, source_target_pairs={{1,9},{3,11},{9,17},{11,19},{17,25},{19,27},{25,29},{27,31},{29,21... | collective-permute-start | bytes 393224 | tf_op jit(solution)/shard_map/ppermute | solution.py:335
  31.1 4.2 %collective-permute-start.16 = (bf16[512,128]{1,0:T(8,128)(2,1)S(1)}, bf16[512,128]{1,0:T(8,128)(2,1)S(1)}, u32[]{:S(2)}, u32[]{:S(2)}) collective-permute-start(bf16[512,128]{1,0:T(8,128)(2,1)S(1)} %collective-permute-done.12.refs_2_), channel_id=1, source_target_pairs={{0,1},{1,0},{2,3},{3,2},{4,5},{5,4},{6,7},{7,6},{8,9},{9,8},{10,11... | collective-permute-start | bytes 393224 | tf_op jit(solution)/shard_map/ppermute | solution.py:279
  33.9 1.4 %collective-permute-start.17 = (bf16[512,128]{1,0:T(8,128)(2,1)S(1)}, bf16[512,128]{1,0:T(8,128)(2,1)S(1)}, u32[]{:S(2)}, u32[]{:S(2)}) collective-permute-start(bf16[512,128]{1,0:T(8,128)(2,1)S(1)} %collective-permute-done.13.refs_3_), channel_id=1, source_target_pairs={{0,1},{1,0},{2,3},{3,2},{4,5},{5,4},{6,7},{7,6},{8,9},{9,8},{10,11... | collective-permute-start | bytes 393224 | tf_op jit(solution)/shard_map/ppermute | solution.py:279
  33.9 1.5 %collective-permute-start.14 = (bf16[512,128]{1,0:T(8,128)(2,1)S(1)}, bf16[512,128]{1,0:T(8,128)(2,1)S(1)}, u32[]{:S(2)}, u32[]{:S(2)}) collective-permute-start(bf16[512,128]{1,0:T(8,128)(2,1)S(1)} %collective-permute-done.6.refs_0_), channel_id=1, source_target_pairs={{0,1},{1,0},{2,3},{3,2},{4,5},{5,4},{6,7},{7,6},{8,9},{9,8},{10,11... | collective-permute-start | bytes 393224 | tf_op jit(solution)/shard_map/ppermute | solution.py:279
  34.4 1.3 %collective-permute-start.15 = (bf16[512,128]{1,0:T(8,128)(2,1)S(1)}, bf16[512,128]{1,0:T(8,128)(2,1)S(1)}, u32[]{:S(2)}, u32[]{:S(2)}) collective-permute-start(bf16[512,128]{1,0:T(8,128)(2,1)S(1)} %collective-permute-done.7.refs_1_), channel_id=1, source_target_pairs={{0,1},{1,0},{2,3},{3,2},{4,5},{5,4},{6,7},{7,6},{8,9},{9,8},{10,11... | collective-permute-start | bytes 393224 | tf_op jit(solution)/shard_map/ppermute | solution.py:279

commit v5 on v4

--- a/solution.py
+++ b/solution.py
@@ -114,7 +114,7 @@
             at += n
 
 
-def pack_kernel(count, rows_here, coarse, a_pattern, g_pattern, a_ref, g_ref, out_ref):
+def pack_kernel(count, rows_here, coarse, a_pattern, g_pattern, a_ref, g_ref, out_ref, cross_ref):
     row = lax.axis_index("row")
     a_rows = layout(count, rows_here, coarse)[0]
     for k in range(count):
@@ -123,6 +123,7 @@
         out_ref[a_rows + j * rows_here : a_rows + (j + 1) * rows_here, :] = jnp.where(
             g_pattern[row, j] != 0, g_ref[:, j * BLOCK : (j + 1) * BLOCK], 0
         )
+    cut_kernel(count, rows_here, coarse, [((0, 0), (0, 0), 1)], out_ref, cross_ref)
 
 
 class Piece:
@@ -220,7 +221,7 @@
 
 
 def product_kernel(count, rows_here, coarse, late, spec, distances, *refs):
-    part_ref, g_early, out_ref, g_cols, g_rows, turned, terms = refs[-7:]
+    part_ref, g_early, out_ref, g_cols, g_rows, turned, terms, block, sent = refs[-9:]
     out_rows = out_ref.shape[0]
     sizes = layout(count, rows_here, coarse)
     a_rows = sizes[0]
@@ -236,8 +237,16 @@
         high = part.astype(jnp.bfloat16)
         terms[:out_rows, columns] = high
         terms[out_rows:, columns] = (part - high.astype(jnp.float32)).astype(jnp.bfloat16)
-    total = jnp.dot(terms[...], g_cols[...], preferred_element_type=jnp.float32)
-    out_ref[...] = total[:out_rows] + total[out_rows:]
+    copies = []
+    out_cols = out_ref.shape[1]
+    for i, (first, last) in enumerate(((0, out_cols - BLOCK), (out_cols - BLOCK, out_cols))):
+        total = jnp.dot(terms[...], g_cols[:, first:last], preferred_element_type=jnp.float32)
+        block[:, first:last] = total[:out_rows] + total[out_rows:]
+        columns = pl.ds(first, last - first)
+        copies.append(pltpu.make_async_copy(block.at[:, columns], out_ref.at[:, columns], sent.at[i]))
+        copies[-1].start()
+    for copy in copies:
+        copy.wait()
 
 
 def gathering_body(count, curl_tiles, gradient, a_pattern, g_pattern):
@@ -263,7 +272,7 @@
             functools.partial(kernel, *sizes, *given),
             out_shape=out,
             in_specs=options.pop("in_specs", [whole] * len(operands)),
-            out_specs=[whole] * len(out) if isinstance(out, list) else whole,
+            out_specs=options.pop("out_specs", [whole] * len(out) if isinstance(out, list) else whole),
             name=name,
             **options,
         )(*operands)
@@ -280,14 +289,14 @@
 
     forward, backward = along(1), along(-1)
     half = count // 2
-    own = call(
+    own, cross = call(
         pack_kernel,
-        rows(packed),
+        [rows(packed), rows(crossing)],
         (a_pattern, g_pattern, curl_tiles, gradient),
         "pack",
         in_specs=[scalars] * 2 + [whole] * 2,
     )
-    held = {(0, 0): ("whole", own, 0), (0, 2): ("whole", across(own, 2), 0)}
+    held = {(0, 0): ("whole", own, 0), (0, 2): ("cross", across(cross, 2), 0)}
 
     def operands_of(pieces):
         buffers, spec = [], {}
@@ -318,15 +327,14 @@
         return call(cut_kernel, [rows(crossing)] * len(items), operands, "cut", items, compiler_params=limit)
 
     chain = {m: (own, own) for m in (0, 2)}
-    for step, m in ((step, m) for step in range(1, half) for m in (0, 2)):
+    for m, step in ((m, step) for m in (0, 2) for step in range(1, half)):
         ahead, back = chain[m]
         kind = "whole"
         if m == 2 and step == half - 1:
             ahead, back = cut([((0, 0), (1, 1), 0), ((1, 1), (-1, -1), 0)], ahead, back)
             kind = "cross"
         ways = [[(i, j ^ m) if step == 1 else (i, j) for i, j in way] for way in (forward, backward)]
-        back, ahead = lax.ppermute(back, axes, ways[1]), lax.ppermute(ahead, axes, ways[0])
-        chain[m] = ahead, back
+        ahead, back = chain[m] = lax.ppermute(ahead, axes, ways[0]), lax.ppermute(back, axes, ways[1])
         held[step, m], held[count - step, m] = (kind, ahead, 0), (kind, back, 0)
     split = [pair for pair in forward if pair[0] % 2 == 1] + [pair for pair in backward if pair[0] % 2 == 0]
     straight, diagonal = cut(
@@ -369,7 +377,10 @@
             pltpu.VMEM((4 * a_rows, out_cols), jnp.bfloat16),
             *turning(len(late_distances)),
             pltpu.VMEM((2 * out_rows, 4 * a_rows), jnp.bfloat16),
+            pltpu.VMEM((out_rows, out_cols), jnp.float32),
+            pltpu.SemaphoreType.DMA((2,)),
         ],
+        out_specs=pl.BlockSpec(memory_space=pl.ANY),
         compiler_params=limit,
     )
 

time: 37.7 us -> 37.6 us (level)
  waiting for transfers between devices: 14.3 us -> 12.3 us
  starting transfers between devices: 19.3 us -> 21.2 us
    ppermute x6, waiting for transfers between devices: 0.42 us -> 4.46 us  [across(): return lax.ppermute(piece, axes, [(i, i ^ mask) for i in range(4 * count)])]
    ppermute x6, waiting for transfers between devices: 8.61 us -> 5.24 us  [gathering_body(): lax.ppermute(ahead, axes, ways[0])]
    ppermute x6, waiting for transfers between devices: 5.31 us -> 2.64 us  [gathering_body(): lax.ppermute(back, axes, ways[1])]
    ppermute x6, starting transfers between devices: 8.6 us -> 9.63 us  [gathering_body(): lax.ppermute(ahead, axes, ways[0])]
  transfers between devices with their start and end apart: 20 -> 20, of which waited for: 12 -> 9; matrix products, arithmetic and copies ran while one was open for 0% -> 0% of each run, Pallas kernels for 3% -> 3%
where the time goes in v5:
time: 37.6 us; the launch traced here: 37.5 us
  starting transfers between devices  21.2 us (56%)
  waiting for transfers between devices  12.3 us (33%)
  Pallas kernels  3.86 us (10%)
    ppermute x6, starting transfers between devices, gathering_body(): lax.ppermute(ahead, axes, ways[0])  9.63 us
    ppermute x6, starting transfers between devices, gathering_body(): lax.ppermute(back, axes, ways[1])  6.87 us
    ppermute x6, waiting for transfers between devices, gathering_body(): lax.ppermute(ahead, axes, ways[0])  5.24 us
    ppermute x6, waiting for transfers between devices, across(): return lax.ppermute(piece, axes, [(i, i ^ mask) for i in range(4 * count)])  4.46 us
    pallas_call x6, Pallas kernels, call(): pl.pallas_call(functools.partial(kernel, *sizes, *given), out_shape=out,...  3.86 us
    ppermute x6, waiting for transfers between devices, gathering_body(): lax.ppermute(back, axes, ways[1])  2.64 us
    ppermute x1, starting transfers between devices, gathering_body(): held[half, 0] = ('cross', lax.ppermute(straight, axes, split), 0)  1.84 us
    ppermute x6, starting transfers between devices, across(): return lax.ppermute(piece, axes, [(i, i ^ mask) for i in range(4 * count)])  1.58 us
  transfers between devices with their start and end apart: 20, of which 9 were waited for; matrix products, arithmetic and copies ran while one was open for 0% of the time, Pallas kernels for 3%

profile of v5, /device:TPU:0, one launch (start us, length us, event | category | flops | bytes accessed | tf_op | source)
XLA Modules:
  0.0 37.5 jit_solution(2841613233649728060)
XLA Ops:
  0.0 1.0 %pack.1 = (bf16[640,128]{1,0:T(8,128)(2,1)S(1)}, bf16[512,128]{1,0:T(8,128)(2,1)S(1)}) custom-call(s32[8,8]{1,0:T(8,128)} %a_pattern.1, s32[8,12]{1,0:T(8,128)} %g_pattern.1, bf16[8,32,128]{2,1,0:T(8,128)(2,1)} %a_ref.1, bf16[32,1536]{1,0:T(8,128)(2,1)} %g_ref.1), custom_call_target="tpu_custom_call" | custom-call | tf_op jit(solution)/shard_map/pack/pallas_call | solution.py:271
  1.0 3.1 %collective-permute-start = (bf16[640,128]{1,0:T(8,128)(2,1)S(1)}, bf16[640,128]{1,0:T(8,128)(2,1)S(1)}, u32[]{:S(2)}, u32[]{:S(2)}) collective-permute-start(bf16[640,128]{1,0:T(8,128)(2,1)S(1)} %get-tuple-element.15.refs_0_), channel_id=1, source_target_pairs={{0,8},{1,9},{2,10},{3,11},{8,16},{9,17},{10,18},{11,19},{16,24},{1... | collective-permute-start | bytes 491528 | tf_op jit(solution)/shard_map/ppermute | solution.py:337
  4.1 0.0 collective-permute-start.3
  4.1 2.9 %collective-permute-start.10 = (bf16[640,128]{1,0:T(8,128)(2,1)S(1)}, bf16[640,128]{1,0:T(8,128)(2,1)S(1)}, u32[]{:S(2)}, u32[]{:S(2)}) collective-permute-start(bf16[640,128]{1,0:T(8,128)(2,1)S(1)} %get-tuple-element.15.refs_0_), channel_id=1, source_target_pairs={{0,6},{1,7},{2,4},{3,5},{8,2},{9,3},{10,0},{11,1},{16,10},{17,11},... | collective-permute-start | bytes 491528 | tf_op jit(solution)/shard_map/ppermute | solution.py:337
  7.0 0.1 collective-permute-start.8
  7.1 1.6 %collective-permute-done.refs_2_ = bf16[640,128]{1,0:T(8,128)(2,1)S(1)} collective-permute-done((bf16[640,128]{1,0:T(8,128)(2,1)S(1)}, bf16[640,128]{1,0:T(8,128)(2,1)S(1)}, u32[]{:S(2)}, u32[]{:S(2)}) %collective-permute-start) | collective-permute-done | bytes 163872 | tf_op jit(solution)/shard_map/ppermute | solution.py:337
  8.6 2.5 %collective-permute-start.1 = (bf16[640,128]{1,0:T(8,128)(2,1)S(1)}, bf16[640,128]{1,0:T(8,128)(2,1)S(1)}, u32[]{:S(2)}, u32[]{:S(2)}) collective-permute-start(bf16[640,128]{1,0:T(8,128)(2,1)S(1)} %collective-permute-done.refs_2_), channel_id=1, source_target_pairs={{0,8},{1,9},{2,10},{3,11},{8,16},{9,17},{10,18},{11,19},{16,24},{1... | collective-permute-start | bytes 491528 | tf_op jit(solution)/shard_map/ppermute | solution.py:337
  11.1 0.1 collective-permute-done.3.refs_10_
  11.2 2.7 %collective-permute-start.4 = (bf16[640,128]{1,0:T(8,128)(2,1)S(1)}, bf16[640,128]{1,0:T(8,128)(2,1)S(1)}, u32[]{:S(2)}, u32[]{:S(2)}) collective-permute-start(bf16[640,128]{1,0:T(8,128)(2,1)S(1)} %collective-permute-done.3.refs_10_), channel_id=1, source_target_pairs={{0,4},{1,5},{2,6},{3,7},{8,0},{9,1},{10,2},{11,3},{16,8},{17,9},{1... | collective-permute-start | bytes 491528 | tf_op jit(solution)/shard_map/ppermute | solution.py:337
  13.9 1.7 %collective-permute-done.10.refs_11_ = bf16[640,128]{1,0:T(8,128)(2,1)S(1)} collective-permute-done((bf16[640,128]{1,0:T(8,128)(2,1)S(1)}, bf16[640,128]{1,0:T(8,128)(2,1)S(1)}, u32[]{:S(2)}, u32[]{:S(2)}) %collective-permute-start.10) | collective-permute-done | bytes 163872 | tf_op jit(solution)/shard_map/ppermute | solution.py:337
  15.7 0.0 collective-permute-start.11
  15.7 0.8 %collective-permute-done.8.refs_3_ = bf16[640,128]{1,0:T(8,128)(2,1)S(1)} collective-permute-done((bf16[640,128]{1,0:T(8,128)(2,1)S(1)}, bf16[640,128]{1,0:T(8,128)(2,1)S(1)}, u32[]{:S(2)}, u32[]{:S(2)}) %collective-permute-start.8) | collective-permute-done | bytes 163872 | tf_op jit(solution)/shard_map/ppermute | solution.py:337
  16.5 1.2 %collective-permute-start.9 = (bf16[640,128]{1,0:T(8,128)(2,1)S(1)}, bf16[640,128]{1,0:T(8,128)(2,1)S(1)}, u32[]{:S(2)}, u32[]{:S(2)}) collective-permute-start(bf16[640,128]{1,0:T(8,128)(2,1)S(1)} %collective-permute-done.8.refs_3_), channel_id=1, source_target_pairs={{0,8},{1,9},{2,10},{3,11},{8,16},{9,17},{10,18},{11,19},{16,24},{1... | collective-permute-start | bytes 491528 | tf_op jit(solution)/shard_map/ppermute | solution.py:337
  17.7 0.0 collective-permute-done.1.refs_4_
  17.7 1.8 %collective-permute-start.2 = (bf16[640,128]{1,0:T(8,128)(2,1)S(1)}, bf16[640,128]{1,0:T(8,128)(2,1)S(1)}, u32[]{:S(2)}, u32[]{:S(2)}) collective-permute-start(bf16[640,128]{1,0:T(8,128)(2,1)S(1)} %collective-permute-done.1.refs_4_), channel_id=1, source_target_pairs={{0,8},{1,9},{2,10},{3,11},{8,16},{9,17},{10,18},{11,19},{16,24},{1... | collective-permute-start | bytes 491528 | tf_op jit(solution)/shard_map/ppermute | solution.py:337
  19.5 0.0 collective-permute-done.4.refs_8_
  19.5 0.2 collective-permute-start.5
  19.7 0.8 %collective-permute-start.18 = (bf16[512,128]{1,0:T(8,128)(2,1)S(1)}, bf16[512,128]{1,0:T(8,128)(2,1)S(1)}, u32[]{:S(2)}, u32[]{:S(2)}) collective-permute-start(bf16[512,128]{1,0:T(8,128)(2,1)S(1)} %get-tuple-element.20), channel_id=1, source_target_pairs={{0,2},{1,3},{2,0},{3,1},{4,6},{5,7},{6,4},{7,5},{8,10},{9,11},{10,... | collective-permute-start | bytes 393224 | tf_op jit(solution)/shard_map/ppermute | solution.py:288
  20.5 4.2 %collective-permute-done.18.refs_1_ = bf16[512,128]{1,0:T(8,128)(2,1)S(1)} collective-permute-done((bf16[512,128]{1,0:T(8,128)(2,1)S(1)}, bf16[512,128]{1,0:T(8,128)(2,1)S(1)}, u32[]{:S(2)}, u32[]{:S(2)}) %collective-permute-start.18) | collective-permute-done | bytes 131104 | tf_op jit(solution)/shard_map/ppermute | solution.py:288
  24.7 0.0 collective-permute-done.11.refs_1_.refs_9_
  24.7 0.0 collective-permute-done.9.refs_0_.refs_5_
  24.7 0.0 collective-permute-done.2.refs_0_.refs_6_
  24.7 0.1 collective-permute-done.5.refs_1_.refs_7_
  24.8 0.2 collect.1
  25.0 0.1 collective-permute-start.19
  25.1 1.0 %collective-permute-start.12 = (bf16[512,128]{1,0:T(8,128)(2,1)S(1)}, bf16[512,128]{1,0:T(8,128)(2,1)S(1)}, u32[]{:S(2)}, u32[]{:S(2)}) collective-permute-start(bf16[512,128]{1,0:T(8,128)(2,1)S(1)} %get-tuple-element.18), channel_id=1, source_target_pairs={{0,4},{1,5},{2,6},{3,7},{8,0},{9,1},{10,2},{11,3},{16,8},{17,9},{1... | collective-permute-start | bytes 393224 | tf_op jit(solution)/shard_map/ppermute | solution.py:337
  26.2 1.0 %collective-permute-start.13 = (bf16[512,128]{1,0:T(8,128)(2,1)S(1)}, bf16[512,128]{1,0:T(8,128)(2,1)S(1)}, u32[]{:S(2)}, u32[]{:S(2)}) collective-permute-start(bf16[512,128]{1,0:T(8,128)(2,1)S(1)} %get-tuple-element.19), channel_id=1, source_target_pairs={{0,8},{1,9},{2,10},{3,11},{8,16},{9,17},{10,18},{11,19},{16,24},{1... | collective-permute-start | bytes 393224 | tf_op jit(solution)/shard_map/ppermute | solution.py:337
  27.2 0.1 cut.2
  27.3 1.3 %collective-permute-start.6 = (bf16[512,128]{1,0:T(8,128)(2,1)S(1)}, bf16[512,128]{1,0:T(8,128)(2,1)S(1)}, u32[]{:S(2)}, u32[]{:S(2)}) collective-permute-start(bf16[512,128]{1,0:T(8,128)(2,1)S(1)} %get-tuple-element.16), channel_id=1, source_target_pairs={{1,11},{3,9},{9,19},{11,17},{17,27},{19,25},{25,31},{27,29},{29,23... | collective-permute-start | bytes 393224 | tf_op jit(solution)/shard_map/ppermute | solution.py:344
  28.5 1.8 %collective-permute-start.7 = (bf16[512,128]{1,0:T(8,128)(2,1)S(1)}, bf16[512,128]{1,0:T(8,128)(2,1)S(1)}, u32[]{:S(2)}, u32[]{:S(2)}) collective-permute-start(bf16[512,128]{1,0:T(8,128)(2,1)S(1)} %get-tuple-element.17), channel_id=1, source_target_pairs={{1,9},{3,11},{9,17},{11,19},{17,25},{19,27},{25,29},{27,31},{29,21... | collective-permute-start | bytes 393224 | tf_op jit(solution)/shard_map/ppermute | solution.py:343
  30.4 0.7 %collective-permute-done.12.refs_2_ = bf16[512,128]{1,0:T(8,128)(2,1)S(1)} collective-permute-done((bf16[512,128]{1,0:T(8,128)(2,1)S(1)}, bf16[512,128]{1,0:T(8,128)(2,1)S(1)}, u32[]{:S(2)}, u32[]{:S(2)}) %collective-permute-start.12) | collective-permute-done | bytes 131104 | tf_op jit(solution)/shard_map/ppermute | solution.py:337
  31.1 0.0 collective-permute-start.16
  31.1 2.8 %collective-permute-done.13.refs_3_ = bf16[512,128]{1,0:T(8,128)(2,1)S(1)} collective-permute-done((bf16[512,128]{1,0:T(8,128)(2,1)S(1)}, bf16[512,128]{1,0:T(8,128)(2,1)S(1)}, u32[]{:S(2)}, u32[]{:S(2)}) %collective-permute-start.13) | collective-permute-done | bytes 131104 | tf_op jit(solution)/shard_map/ppermute | solution.py:337
  33.9 0.0 collective-permute-start.17
  33.9 0.0 collective-permute-done.6.refs_0_
  33.9 0.5 %collective-permute-start.14 = (bf16[512,128]{1,0:T(8,128)(2,1)S(1)}, bf16[512,128]{1,0:T(8,128)(2,1)S(1)}, u32[]{:S(2)}, u32[]{:S(2)}) collective-permute-start(bf16[512,128]{1,0:T(8,128)(2,1)S(1)} %collective-permute-done.6.refs_0_), channel_id=1, source_target_pairs={{0,1},{1,0},{2,3},{3,2},{4,5},{5,4},{6,7},{7,6},{8,9},{9,8},{10,11... | collective-permute-start | bytes 393224 | tf_op jit(solution)/shard_map/ppermute | solution.py:288
  34.4 0.0 collective-permute-done.7.refs_1_
  34.4 0.2 collective-permute-start.15
  34.6 0.0 collective-permute-done.19.refs_1_.refs_9_
  34.6 0.8 %early.1 = (f32[192,1024]{1,0:T(8,128)S(1)}, bf16[1024,384]{1,0:T(8,128)(2,1)S(1)}) custom-call(bf16[4992,128]{1,0:T(8,128)(2,1)S(1)} %get-tuple-element.21.refs_0_.refs_8_, bf16[4992,128]{1,0:T(8,128)(2,1)S(1)} %collective-permute-done.19.refs_1_.refs_9_), custom_call_target="tpu_custom_call" | custom-call | tf_op jit(solution)/shard_map/early/pallas_call | solution.py:271
  35.5 0.0 collective-permute-done.16.refs_6_
  35.5 0.0 collective-permute-done.17.refs_7_
  35.5 0.0 collective-permute-done.14.refs_4_
  35.5 0.2 collective-permute-done.15.refs_5_
  35.7 1.7 %product.1 = f32[192,384]{1,0:T(8,128)} custom-call(bf16[512,128]{1,0:T(8,128)(2,1)S(1)} %collective-permute-done.6.refs_0_, bf16[512,128]{1,0:T(8,128)(2,1)S(1)} %collective-permute-done.7.refs_1_, bf16[512,128]{1,0:T(8,128)(2,1)S(1)} %collective-permute-done.12.refs_2_, bf16[512,128]{1,0:T(8,128)(2,1)S(1)} %collective-permute-done.13.refs_3_, ...), custom_call_target="tpu_custom_call" | custom-call | tf_op jit(solution)/shard_map/product/pallas_call | solution.py:271
  (1 shorter events, 0.0 us)
Async XLA Ops:
  1.0 7.6 %collective-permute-start = (bf16[640,128]{1,0:T(8,128)(2,1)S(1)}, bf16[640,128]{1,0:T(8,128)(2,1)S(1)}, u32[]{:S(2)}, u32[]{:S(2)}) collective-permute-start(bf16[640,128]{1,0:T(8,128)(2,1)S(1)} %get-tuple-element.15.refs_0_), channel_id=1, source_target_pairs={{0,8},{1,9},{2,10},{3,11},{8,16},{9,17},{10,18},{11,19},{16,24},{1... | collective-permute-start | bytes 491528 | tf_op jit(solution)/shard_map/ppermute | solution.py:337
  4.1 7.1 %collective-permute-start.3 = (bf16[640,128]{1,0:T(8,128)(2,1)S(1)}, bf16[640,128]{1,0:T(8,128)(2,1)S(1)}, u32[]{:S(2)}, u32[]{:S(2)}) collective-permute-start(bf16[640,128]{1,0:T(8,128)(2,1)S(1)} %get-tuple-element.15.refs_0_), channel_id=1, source_target_pairs={{0,4},{1,5},{2,6},{3,7},{8,0},{9,1},{10,2},{11,3},{16,8},{17,9},{1... | collective-permute-start | bytes 491528 | tf_op jit(solution)/shard_map/ppermute | solution.py:337
  4.1 11.6 %collective-permute-start.10 = (bf16[640,128]{1,0:T(8,128)(2,1)S(1)}, bf16[640,128]{1,0:T(8,128)(2,1)S(1)}, u32[]{:S(2)}, u32[]{:S(2)}) collective-permute-start(bf16[640,128]{1,0:T(8,128)(2,1)S(1)} %get-tuple-element.15.refs_0_), channel_id=1, source_target_pairs={{0,6},{1,7},{2,4},{3,5},{8,2},{9,3},{10,0},{11,1},{16,10},{17,11},... | collective-permute-start | bytes 491528 | tf_op jit(solution)/shard_map/ppermute | solution.py:337
  7.0 9.5 %collective-permute-start.8 = (bf16[640,128]{1,0:T(8,128)(2,1)S(1)}, bf16[640,128]{1,0:T(8,128)(2,1)S(1)}, u32[]{:S(2)}, u32[]{:S(2)}) collective-permute-start(bf16[640,128]{1,0:T(8,128)(2,1)S(1)} %get-tuple-element.15.refs_0_), channel_id=1, source_target_pairs={{0,10},{1,11},{2,8},{3,9},{8,18},{9,19},{10,16},{11,17},{16,26},{1... | collective-permute-start | bytes 491528 | tf_op jit(solution)/shard_map/ppermute | solution.py:337
  8.6 9.1 %collective-permute-start.1 = (bf16[640,128]{1,0:T(8,128)(2,1)S(1)}, bf16[640,128]{1,0:T(8,128)(2,1)S(1)}, u32[]{:S(2)}, u32[]{:S(2)}) collective-permute-start(bf16[640,128]{1,0:T(8,128)(2,1)S(1)} %collective-permute-done.refs_2_), channel_id=1, source_target_pairs={{0,8},{1,9},{2,10},{3,11},{8,16},{9,17},{10,18},{11,19},{16,24},{1... | collective-permute-start | bytes 491528 | tf_op jit(solution)/shard_map/ppermute | solution.py:337
  11.2 8.3 %collective-permute-start.4 = (bf16[640,128]{1,0:T(8,128)(2,1)S(1)}, bf16[640,128]{1,0:T(8,128)(2,1)S(1)}, u32[]{:S(2)}, u32[]{:S(2)}) collective-permute-start(bf16[640,128]{1,0:T(8,128)(2,1)S(1)} %collective-permute-done.3.refs_10_), channel_id=1, source_target_pairs={{0,4},{1,5},{2,6},{3,7},{8,0},{9,1},{10,2},{11,3},{16,8},{17,9},{1... | collective-permute-start | bytes 491528 | tf_op jit(solution)/shard_map/ppermute | solution.py:337
  15.7 9.0 %collective-permute-start.11 = (bf16[640,128]{1,0:T(8,128)(2,1)S(1)}, bf16[640,128]{1,0:T(8,128)(2,1)S(1)}, u32[]{:S(2)}, u32[]{:S(2)}) collective-permute-start(bf16[640,128]{1,0:T(8,128)(2,1)S(1)} %collective-permute-done.10.refs_11_), channel_id=1, source_target_pairs={{0,4},{1,5},{2,6},{3,7},{8,0},{9,1},{10,2},{11,3},{16,8},{17,9},{1... | collective-permute-start | bytes 491528 | tf_op jit(solution)/shard_map/ppermute | solution.py:337
  16.5 8.2 %collective-permute-start.9 = (bf16[640,128]{1,0:T(8,128)(2,1)S(1)}, bf16[640,128]{1,0:T(8,128)(2,1)S(1)}, u32[]{:S(2)}, u32[]{:S(2)}) collective-permute-start(bf16[640,128]{1,0:T(8,128)(2,1)S(1)} %collective-permute-done.8.refs_3_), channel_id=1, source_target_pairs={{0,8},{1,9},{2,10},{3,11},{8,16},{9,17},{10,18},{11,19},{16,24},{1... | collective-permute-start | bytes 491528 | tf_op jit(solution)/shard_map/ppermute | solution.py:337
  17.7 7.0 %collective-permute-start.2 = (bf16[640,128]{1,0:T(8,128)(2,1)S(1)}, bf16[640,128]{1,0:T(8,128)(2,1)S(1)}, u32[]{:S(2)}, u32[]{:S(2)}) collective-permute-start(bf16[640,128]{1,0:T(8,128)(2,1)S(1)} %collective-permute-done.1.refs_4_), channel_id=1, source_target_pairs={{0,8},{1,9},{2,10},{3,11},{8,16},{9,17},{10,18},{11,19},{16,24},{1... | collective-permute-start | bytes 491528 | tf_op jit(solution)/shard_map/ppermute | solution.py:337
  19.5 5.3 %collective-permute-start.5 = (bf16[640,128]{1,0:T(8,128)(2,1)S(1)}, bf16[640,128]{1,0:T(8,128)(2,1)S(1)}, u32[]{:S(2)}, u32[]{:S(2)}) collective-permute-start(bf16[640,128]{1,0:T(8,128)(2,1)S(1)} %collective-permute-done.4.refs_8_), channel_id=1, source_target_pairs={{0,4},{1,5},{2,6},{3,7},{8,0},{9,1},{10,2},{11,3},{16,8},{17,9},{1... | collective-permute-start | bytes 491528 | tf_op jit(solution)/shard_map/ppermute | solution.py:337
  19.7 5.0 %collective-permute-start.18 = (bf16[512,128]{1,0:T(8,128)(2,1)S(1)}, bf16[512,128]{1,0:T(8,128)(2,1)S(1)}, u32[]{:S(2)}, u32[]{:S(2)}) collective-permute-start(bf16[512,128]{1,0:T(8,128)(2,1)S(1)} %get-tuple-element.20), channel_id=1, source_target_pairs={{0,2},{1,3},{2,0},{3,1},{4,6},{5,7},{6,4},{7,5},{8,10},{9,11},{10,... | collective-permute-start | bytes 393224 | tf_op jit(solution)/shard_map/ppermute | solution.py:288
  25.0 9.7 %collective-permute-start.19 = (bf16[4992,128]{1,0:T(8,128)(2,1)S(1)}, bf16[4992,128]{1,0:T(8,128)(2,1)S(1)}, u32[]{:S(2)}, u32[]{:S(2)}) collective-permute-start(bf16[4992,128]{1,0:T(8,128)(2,1)S(1)} %get-tuple-element.22), channel_id=1, source_target_pairs={{0,1},{1,0},{2,3},{3,2},{4,5},{5,4},{6,7},{7,6},{8,9},{9,8},{10,11... | collective-permute-start | bytes 3833864 | tf_op jit(solution)/shard_map/ppermute | solution.py:288
  25.1 5.9 %collective-permute-start.12 = (bf16[512,128]{1,0:T(8,128)(2,1)S(1)}, bf16[512,128]{1,0:T(8,128)(2,1)S(1)}, u32[]{:S(2)}, u32[]{:S(2)}) collective-permute-start(bf16[512,128]{1,0:T(8,128)(2,1)S(1)} %get-tuple-element.18), channel_id=1, source_target_pairs={{0,4},{1,5},{2,6},{3,7},{8,0},{9,1},{10,2},{11,3},{16,8},{17,9},{1... | collective-permute-start | bytes 393224 | tf_op jit(solution)/shard_map/ppermute | solution.py:337
  26.2 7.7 %collective-permute-start.13 = (bf16[512,128]{1,0:T(8,128)(2,1)S(1)}, bf16[512,128]{1,0:T(8,128)(2,1)S(1)}, u32[]{:S(2)}, u32[]{:S(2)}) collective-permute-start(bf16[512,128]{1,0:T(8,128)(2,1)S(1)} %get-tuple-element.19), channel_id=1, source_target_pairs={{0,8},{1,9},{2,10},{3,11},{8,16},{9,17},{10,18},{11,19},{16,24},{1... | collective-permute-start | bytes 393224 | tf_op jit(solution)/shard_map/ppermute | solution.py:337
  27.3 6.6 %collective-permute-start.6 = (bf16[512,128]{1,0:T(8,128)(2,1)S(1)}, bf16[512,128]{1,0:T(8,128)(2,1)S(1)}, u32[]{:S(2)}, u32[]{:S(2)}) collective-permute-start(bf16[512,128]{1,0:T(8,128)(2,1)S(1)} %get-tuple-element.16), channel_id=1, source_target_pairs={{1,11},{3,9},{9,19},{11,17},{17,27},{19,25},{25,31},{27,29},{29,23... | collective-permute-start | bytes 393224 | tf_op jit(solution)/shard_map/ppermute | solution.py:344
  28.5 5.9 %collective-permute-start.7 = (bf16[512,128]{1,0:T(8,128)(2,1)S(1)}, bf16[512,128]{1,0:T(8,128)(2,1)S(1)}, u32[]{:S(2)}, u32[]{:S(2)}) collective-permute-start(bf16[512,128]{1,0:T(8,128)(2,1)S(1)} %get-tuple-element.17), channel_id=1, source_target_pairs={{1,9},{3,11},{9,17},{11,19},{17,25},{19,27},{25,29},{27,31},{29,21... | collective-permute-start | bytes 393224 | tf_op jit(solution)/shard_map/ppermute | solution.py:343
  31.1 4.4 %collective-permute-start.16 = (bf16[512,128]{1,0:T(8,128)(2,1)S(1)}, bf16[512,128]{1,0:T(8,128)(2,1)S(1)}, u32[]{:S(2)}, u32[]{:S(2)}) collective-permute-start(bf16[512,128]{1,0:T(8,128)(2,1)S(1)} %collective-permute-done.12.refs_2_), channel_id=1, source_target_pairs={{0,1},{1,0},{2,3},{3,2},{4,5},{5,4},{6,7},{7,6},{8,9},{9,8},{10,11... | collective-permute-start | bytes 393224 | tf_op jit(solution)/shard_map/ppermute | solution.py:288
  33.9 1.6 %collective-permute-start.17 = (bf16[512,128]{1,0:T(8,128)(2,1)S(1)}, bf16[512,128]{1,0:T(8,128)(2,1)S(1)}, u32[]{:S(2)}, u32[]{:S(2)}) collective-permute-start(bf16[512,128]{1,0:T(8,128)(2,1)S(1)} %collective-permute-done.13.refs_3_), channel_id=1, source_target_pairs={{0,1},{1,0},{2,3},{3,2},{4,5},{5,4},{6,7},{7,6},{8,9},{9,8},{10,11... | collective-permute-start | bytes 393224 | tf_op jit(solution)/shard_map/ppermute | solution.py:288
  33.9 1.6 %collective-permute-start.14 = (bf16[512,128]{1,0:T(8,128)(2,1)S(1)}, bf16[512,128]{1,0:T(8,128)(2,1)S(1)}, u32[]{:S(2)}, u32[]{:S(2)}) collective-permute-start(bf16[512,128]{1,0:T(8,128)(2,1)S(1)} %collective-permute-done.6.refs_0_), channel_id=1, source_target_pairs={{0,1},{1,0},{2,3},{3,2},{4,5},{5,4},{6,7},{7,6},{8,9},{9,8},{10,11... | collective-permute-start | bytes 393224 | tf_op jit(solution)/shard_map/ppermute | solution.py:288
  34.4 1.3 %collective-permute-start.15 = (bf16[512,128]{1,0:T(8,128)(2,1)S(1)}, bf16[512,128]{1,0:T(8,128)(2,1)S(1)}, u32[]{:S(2)}, u32[]{:S(2)}) collective-permute-start(bf16[512,128]{1,0:T(8,128)(2,1)S(1)} %collective-permute-done.7.refs_1_), channel_id=1, source_target_pairs={{0,1},{1,0},{2,3},{3,2},{4,5},{5,4},{6,7},{7,6},{8,9},{9,8},{10,11... | collective-permute-start | bytes 393224 | tf_op jit(solution)/shard_map/ppermute | solution.py:288

commit v6 on v5

--- a/solution.py
+++ b/solution.py
@@ -296,7 +296,7 @@
         "pack",
         in_specs=[scalars] * 2 + [whole] * 2,
     )
-    held = {(0, 0): ("whole", own, 0), (0, 2): ("cross", across(cross, 2), 0)}
+    held = {(0, 0): ("whole", own, 0)}
 
     def operands_of(pieces):
         buffers, spec = [], {}
@@ -342,8 +342,8 @@
     )
     held[half, 0] = ("cross", lax.ppermute(straight, axes, split), 0)
     held[half, 2] = ("cross", lax.ppermute(diagonal, axes, [(i, j ^ 2) for i, j in split]), 0)
+    held[0, 2] = ("cross", across(cross, 2), 0)
     early = {key: held[key] for key in held if min(key[0], count - key[0]) < half - key[1] // 2}
-    early = dict(sorted(early.items()))
     got = exchange(early)
     distances = [d for d in range(count) if (d, 0) in early and (d, 2) in early]
     buffers, spec = operands_of(got)

time: 37.6 us -> 37.6 us (level)
  no operation moved by 1% of the time
where the time goes in v6:
time: 37.6 us; the launch traced here: 37.5 us
  starting transfers between devices  21.2 us (56%)
  waiting for transfers between devices  12.3 us (33%)
  Pallas kernels  3.86 us (10%)
    ppermute x6, starting transfers between devices, gathering_body(): lax.ppermute(ahead, axes, ways[0])  9.63 us
    ppermute x6, starting transfers between devices, gathering_body(): lax.ppermute(back, axes, ways[1])  6.87 us
    ppermute x6, waiting for transfers between devices, gathering_body(): lax.ppermute(ahead, axes, ways[0])  5.24 us
    ppermute x6, waiting for transfers between devices, across(): return lax.ppermute(piece, axes, [(i, i ^ mask) for i in range(4 * count)])  4.47 us
    pallas_call x6, Pallas kernels, call(): pl.pallas_call(functools.partial(kernel, *sizes, *given), out_shape=out,...  3.86 us
    ppermute x6, waiting for transfers between devices, gathering_body(): lax.ppermute(back, axes, ways[1])  2.64 us
    ppermute x1, starting transfers between devices, gathering_body(): held[half, 0] = ('cross', lax.ppermute(straight, axes, split), 0)  1.84 us
    ppermute x6, starting transfers between devices, across(): return lax.ppermute(piece, axes, [(i, i ^ mask) for i in range(4 * count)])  1.58 us
  transfers between devices with their start and end apart: 20, of which 9 were waited for; matrix products, arithmetic and copies ran while one was open for 0% of the time, Pallas kernels for 3%

profile of v6, /device:TPU:0, one launch (start us, length us, event | category | flops | bytes accessed | tf_op | source)
XLA Modules:
  0.0 37.5 jit_solution(16876457504524794680)
XLA Ops:
  0.0 1.0 %pack.1 = (bf16[640,128]{1,0:T(8,128)(2,1)S(1)}, bf16[512,128]{1,0:T(8,128)(2,1)S(1)}) custom-call(s32[8,8]{1,0:T(8,128)} %a_pattern.1, s32[8,12]{1,0:T(8,128)} %g_pattern.1, bf16[8,32,128]{2,1,0:T(8,128)(2,1)} %a_ref.1, bf16[32,1536]{1,0:T(8,128)(2,1)} %g_ref.1), custom_call_target="tpu_custom_call" | custom-call | tf_op jit(solution)/shard_map/pack/pallas_call | solution.py:271
  1.0 3.1 %collective-permute-start = (bf16[640,128]{1,0:T(8,128)(2,1)S(1)}, bf16[640,128]{1,0:T(8,128)(2,1)S(1)}, u32[]{:S(2)}, u32[]{:S(2)}) collective-permute-start(bf16[640,128]{1,0:T(8,128)(2,1)S(1)} %get-tuple-element.15.refs_0_), channel_id=1, source_target_pairs={{0,8},{1,9},{2,10},{3,11},{8,16},{9,17},{10,18},{11,19},{16,24},{1... | collective-permute-start | bytes 491528 | tf_op jit(solution)/shard_map/ppermute | solution.py:337
  4.1 0.0 collective-permute-start.3
  4.1 2.9 %collective-permute-start.10 = (bf16[640,128]{1,0:T(8,128)(2,1)S(1)}, bf16[640,128]{1,0:T(8,128)(2,1)S(1)}, u32[]{:S(2)}, u32[]{:S(2)}) collective-permute-start(bf16[640,128]{1,0:T(8,128)(2,1)S(1)} %get-tuple-element.15.refs_0_), channel_id=1, source_target_pairs={{0,6},{1,7},{2,4},{3,5},{8,2},{9,3},{10,0},{11,1},{16,10},{17,11},... | collective-permute-start | bytes 491528 | tf_op jit(solution)/shard_map/ppermute | solution.py:337
  7.0 0.1 collective-permute-start.8
  7.1 1.6 %collective-permute-done.refs_1_ = bf16[640,128]{1,0:T(8,128)(2,1)S(1)} collective-permute-done((bf16[640,128]{1,0:T(8,128)(2,1)S(1)}, bf16[640,128]{1,0:T(8,128)(2,1)S(1)}, u32[]{:S(2)}, u32[]{:S(2)}) %collective-permute-start) | collective-permute-done | bytes 163872 | tf_op jit(solution)/shard_map/ppermute | solution.py:337
  8.6 2.5 %collective-permute-start.1 = (bf16[640,128]{1,0:T(8,128)(2,1)S(1)}, bf16[640,128]{1,0:T(8,128)(2,1)S(1)}, u32[]{:S(2)}, u32[]{:S(2)}) collective-permute-start(bf16[640,128]{1,0:T(8,128)(2,1)S(1)} %collective-permute-done.refs_1_), channel_id=1, source_target_pairs={{0,8},{1,9},{2,10},{3,11},{8,16},{9,17},{10,18},{11,19},{16,24},{1... | collective-permute-start | bytes 491528 | tf_op jit(solution)/shard_map/ppermute | solution.py:337
  11.1 0.1 collective-permute-done.3.refs_2_
  11.2 2.7 %collective-permute-start.4 = (bf16[640,128]{1,0:T(8,128)(2,1)S(1)}, bf16[640,128]{1,0:T(8,128)(2,1)S(1)}, u32[]{:S(2)}, u32[]{:S(2)}) collective-permute-start(bf16[640,128]{1,0:T(8,128)(2,1)S(1)} %collective-permute-done.3.refs_2_), channel_id=1, source_target_pairs={{0,4},{1,5},{2,6},{3,7},{8,0},{9,1},{10,2},{11,3},{16,8},{17,9},{1... | collective-permute-start | bytes 491528 | tf_op jit(solution)/shard_map/ppermute | solution.py:337
  13.9 1.7 %collective-permute-done.10.refs_8_ = bf16[640,128]{1,0:T(8,128)(2,1)S(1)} collective-permute-done((bf16[640,128]{1,0:T(8,128)(2,1)S(1)}, bf16[640,128]{1,0:T(8,128)(2,1)S(1)}, u32[]{:S(2)}, u32[]{:S(2)}) %collective-permute-start.10) | collective-permute-done | bytes 163872 | tf_op jit(solution)/shard_map/ppermute | solution.py:337
  15.7 0.0 collective-permute-start.11
  15.7 0.8 %collective-permute-done.8.refs_7_ = bf16[640,128]{1,0:T(8,128)(2,1)S(1)} collective-permute-done((bf16[640,128]{1,0:T(8,128)(2,1)S(1)}, bf16[640,128]{1,0:T(8,128)(2,1)S(1)}, u32[]{:S(2)}, u32[]{:S(2)}) %collective-permute-start.8) | collective-permute-done | bytes 163872 | tf_op jit(solution)/shard_map/ppermute | solution.py:337
  16.5 1.2 %collective-permute-start.9 = (bf16[640,128]{1,0:T(8,128)(2,1)S(1)}, bf16[640,128]{1,0:T(8,128)(2,1)S(1)}, u32[]{:S(2)}, u32[]{:S(2)}) collective-permute-start(bf16[640,128]{1,0:T(8,128)(2,1)S(1)} %collective-permute-done.8.refs_7_), channel_id=1, source_target_pairs={{0,8},{1,9},{2,10},{3,11},{8,16},{9,17},{10,18},{11,19},{16,24},{1... | collective-permute-start | bytes 491528 | tf_op jit(solution)/shard_map/ppermute | solution.py:337
  17.7 0.0 collective-permute-done.1.refs_3_
  17.7 1.8 %collective-permute-start.2 = (bf16[640,128]{1,0:T(8,128)(2,1)S(1)}, bf16[640,128]{1,0:T(8,128)(2,1)S(1)}, u32[]{:S(2)}, u32[]{:S(2)}) collective-permute-start(bf16[640,128]{1,0:T(8,128)(2,1)S(1)} %collective-permute-done.1.refs_3_), channel_id=1, source_target_pairs={{0,8},{1,9},{2,10},{3,11},{8,16},{9,17},{10,18},{11,19},{16,24},{1... | collective-permute-start | bytes 491528 | tf_op jit(solution)/shard_map/ppermute | solution.py:337
  19.5 0.0 collective-permute-done.4.refs_4_
  19.5 0.2 collective-permute-start.5
  19.7 0.8 %collective-permute-start.18 = (bf16[512,128]{1,0:T(8,128)(2,1)S(1)}, bf16[512,128]{1,0:T(8,128)(2,1)S(1)}, u32[]{:S(2)}, u32[]{:S(2)}) collective-permute-start(bf16[512,128]{1,0:T(8,128)(2,1)S(1)} %get-tuple-element.20), channel_id=1, source_target_pairs={{0,2},{1,3},{2,0},{3,1},{4,6},{5,7},{6,4},{7,5},{8,10},{9,11},{10,... | collective-permute-start | bytes 393224 | tf_op jit(solution)/shard_map/ppermute | solution.py:288
  20.5 4.2 %collective-permute-done.18.refs_11_ = bf16[512,128]{1,0:T(8,128)(2,1)S(1)} collective-permute-done((bf16[512,128]{1,0:T(8,128)(2,1)S(1)}, bf16[512,128]{1,0:T(8,128)(2,1)S(1)}, u32[]{:S(2)}, u32[]{:S(2)}) %collective-permute-start.18) | collective-permute-done | bytes 131104 | tf_op jit(solution)/shard_map/ppermute | solution.py:288
  24.7 0.0 collective-permute-done.11.refs_1_.refs_10_
  24.7 0.0 collective-permute-done.9.refs_0_.refs_9_
  24.7 0.0 collective-permute-done.2.refs_0_.refs_5_
  24.7 0.1 collective-permute-done.5.refs_1_.refs_6_
  24.8 0.2 collect.1
  25.0 0.1 collective-permute-start.19
  25.1 1.0 %collective-permute-start.12 = (bf16[512,128]{1,0:T(8,128)(2,1)S(1)}, bf16[512,128]{1,0:T(8,128)(2,1)S(1)}, u32[]{:S(2)}, u32[]{:S(2)}) collective-permute-start(bf16[512,128]{1,0:T(8,128)(2,1)S(1)} %get-tuple-element.18), channel_id=1, source_target_pairs={{0,4},{1,5},{2,6},{3,7},{8,0},{9,1},{10,2},{11,3},{16,8},{17,9},{1... | collective-permute-start | bytes 393224 | tf_op jit(solution)/shard_map/ppermute | solution.py:337
  26.2 1.0 %collective-permute-start.13 = (bf16[512,128]{1,0:T(8,128)(2,1)S(1)}, bf16[512,128]{1,0:T(8,128)(2,1)S(1)}, u32[]{:S(2)}, u32[]{:S(2)}) collective-permute-start(bf16[512,128]{1,0:T(8,128)(2,1)S(1)} %get-tuple-element.19), channel_id=1, source_target_pairs={{0,8},{1,9},{2,10},{3,11},{8,16},{9,17},{10,18},{11,19},{16,24},{1... | collective-permute-start | bytes 393224 | tf_op jit(solution)/shard_map/ppermute | solution.py:337
  27.2 0.1 cut.2
  27.3 1.3 %collective-permute-start.6 = (bf16[512,128]{1,0:T(8,128)(2,1)S(1)}, bf16[512,128]{1,0:T(8,128)(2,1)S(1)}, u32[]{:S(2)}, u32[]{:S(2)}) collective-permute-start(bf16[512,128]{1,0:T(8,128)(2,1)S(1)} %get-tuple-element.16), channel_id=1, source_target_pairs={{1,11},{3,9},{9,19},{11,17},{17,27},{19,25},{25,31},{27,29},{29,23... | collective-permute-start | bytes 393224 | tf_op jit(solution)/shard_map/ppermute | solution.py:344
  28.5 1.8 %collective-permute-start.7 = (bf16[512,128]{1,0:T(8,128)(2,1)S(1)}, bf16[512,128]{1,0:T(8,128)(2,1)S(1)}, u32[]{:S(2)}, u32[]{:S(2)}) collective-permute-start(bf16[512,128]{1,0:T(8,128)(2,1)S(1)} %get-tuple-element.17), channel_id=1, source_target_pairs={{1,9},{3,11},{9,17},{11,19},{17,25},{19,27},{25,29},{27,31},{29,21... | collective-permute-start | bytes 393224 | tf_op jit(solution)/shard_map/ppermute | solution.py:343
  30.4 0.7 %collective-permute-done.12.refs_2_ = bf16[512,128]{1,0:T(8,128)(2,1)S(1)} collective-permute-done((bf16[512,128]{1,0:T(8,128)(2,1)S(1)}, bf16[512,128]{1,0:T(8,128)(2,1)S(1)}, u32[]{:S(2)}, u32[]{:S(2)}) %collective-permute-start.12) | collective-permute-done | bytes 131104 | tf_op jit(solution)/shard_map/ppermute | solution.py:337
  31.1 0.0 collective-permute-start.16
  31.1 2.8 %collective-permute-done.13.refs_3_ = bf16[512,128]{1,0:T(8,128)(2,1)S(1)} collective-permute-done((bf16[512,128]{1,0:T(8,128)(2,1)S(1)}, bf16[512,128]{1,0:T(8,128)(2,1)S(1)}, u32[]{:S(2)}, u32[]{:S(2)}) %collective-permute-start.13) | collective-permute-done | bytes 131104 | tf_op jit(solution)/shard_map/ppermute | solution.py:337
  33.9 0.0 collective-permute-start.17
  33.9 0.0 collective-permute-done.6.refs_0_
  33.9 0.5 %collective-permute-start.14 = (bf16[512,128]{1,0:T(8,128)(2,1)S(1)}, bf16[512,128]{1,0:T(8,128)(2,1)S(1)}, u32[]{:S(2)}, u32[]{:S(2)}) collective-permute-start(bf16[512,128]{1,0:T(8,128)(2,1)S(1)} %collective-permute-done.6.refs_0_), channel_id=1, source_target_pairs={{0,1},{1,0},{2,3},{3,2},{4,5},{5,4},{6,7},{7,6},{8,9},{9,8},{10,11... | collective-permute-start | bytes 393224 | tf_op jit(solution)/shard_map/ppermute | solution.py:288
  34.4 0.0 collective-permute-done.7.refs_1_
  34.4 0.2 collective-permute-start.15
  34.6 0.0 collective-permute-done.19.refs_1_.refs_9_
  34.6 0.8 %early.1 = (f32[192,1024]{1,0:T(8,128)S(1)}, bf16[1024,384]{1,0:T(8,128)(2,1)S(1)}) custom-call(bf16[4992,128]{1,0:T(8,128)(2,1)S(1)} %get-tuple-element.21.refs_0_.refs_8_, bf16[4992,128]{1,0:T(8,128)(2,1)S(1)} %collective-permute-done.19.refs_1_.refs_9_), custom_call_target="tpu_custom_call" | custom-call | tf_op jit(solution)/shard_map/early/pallas_call | solution.py:271
  35.5 0.0 collective-permute-done.16.refs_6_
  35.5 0.0 collective-permute-done.17.refs_7_
  35.5 0.0 collective-permute-done.14.refs_4_
  35.5 0.2 collective-permute-done.15.refs_5_
  35.7 1.7 %product.1 = f32[192,384]{1,0:T(8,128)} custom-call(bf16[512,128]{1,0:T(8,128)(2,1)S(1)} %collective-permute-done.6.refs_0_, bf16[512,128]{1,0:T(8,128)(2,1)S(1)} %collective-permute-done.7.refs_1_, bf16[512,128]{1,0:T(8,128)(2,1)S(1)} %collective-permute-done.12.refs_2_, bf16[512,128]{1,0:T(8,128)(2,1)S(1)} %collective-permute-done.13.refs_3_, ...), custom_call_target="tpu_custom_call" | custom-call | tf_op jit(solution)/shard_map/product/pallas_call | solution.py:271
  (1 shorter events, 0.0 us)
Async XLA Ops:
  1.0 7.6 %collective-permute-start = (bf16[640,128]{1,0:T(8,128)(2,1)S(1)}, bf16[640,128]{1,0:T(8,128)(2,1)S(1)}, u32[]{:S(2)}, u32[]{:S(2)}) collective-permute-start(bf16[640,128]{1,0:T(8,128)(2,1)S(1)} %get-tuple-element.15.refs_0_), channel_id=1, source_target_pairs={{0,8},{1,9},{2,10},{3,11},{8,16},{9,17},{10,18},{11,19},{16,24},{1... | collective-permute-start | bytes 491528 | tf_op jit(solution)/shard_map/ppermute | solution.py:337
  4.1 7.1 %collective-permute-start.3 = (bf16[640,128]{1,0:T(8,128)(2,1)S(1)}, bf16[640,128]{1,0:T(8,128)(2,1)S(1)}, u32[]{:S(2)}, u32[]{:S(2)}) collective-permute-start(bf16[640,128]{1,0:T(8,128)(2,1)S(1)} %get-tuple-element.15.refs_0_), channel_id=1, source_target_pairs={{0,4},{1,5},{2,6},{3,7},{8,0},{9,1},{10,2},{11,3},{16,8},{17,9},{1... | collective-permute-start | bytes 491528 | tf_op jit(solution)/shard_map/ppermute | solution.py:337
  4.1 11.6 %collective-permute-start.10 = (bf16[640,128]{1,0:T(8,128)(2,1)S(1)}, bf16[640,128]{1,0:T(8,128)(2,1)S(1)}, u32[]{:S(2)}, u32[]{:S(2)}) collective-permute-start(bf16[640,128]{1,0:T(8,128)(2,1)S(1)} %get-tuple-element.15.refs_0_), channel_id=1, source_target_pairs={{0,6},{1,7},{2,4},{3,5},{8,2},{9,3},{10,0},{11,1},{16,10},{17,11},... | collective-permute-start | bytes 491528 | tf_op jit(solution)/shard_map/ppermute | solution.py:337
  7.0 9.5 %collective-permute-start.8 = (bf16[640,128]{1,0:T(8,128)(2,1)S(1)}, bf16[640,128]{1,0:T(8,128)(2,1)S(1)}, u32[]{:S(2)}, u32[]{:S(2)}) collective-permute-start(bf16[640,128]{1,0:T(8,128)(2,1)S(1)} %get-tuple-element.15.refs_0_), channel_id=1, source_target_pairs={{0,10},{1,11},{2,8},{3,9},{8,18},{9,19},{10,16},{11,17},{16,26},{1... | collective-permute-start | bytes 491528 | tf_op jit(solution)/shard_map/ppermute | solution.py:337
  8.6 9.1 %collective-permute-start.1 = (bf16[640,128]{1,0:T(8,128)(2,1)S(1)}, bf16[640,128]{1,0:T(8,128)(2,1)S(1)}, u32[]{:S(2)}, u32[]{:S(2)}) collective-permute-start(bf16[640,128]{1,0:T(8,128)(2,1)S(1)} %collective-permute-done.refs_1_), channel_id=1, source_target_pairs={{0,8},{1,9},{2,10},{3,11},{8,16},{9,17},{10,18},{11,19},{16,24},{1... | collective-permute-start | bytes 491528 | tf_op jit(solution)/shard_map/ppermute | solution.py:337
  11.2 8.3 %collective-permute-start.4 = (bf16[640,128]{1,0:T(8,128)(2,1)S(1)}, bf16[640,128]{1,0:T(8,128)(2,1)S(1)}, u32[]{:S(2)}, u32[]{:S(2)}) collective-permute-start(bf16[640,128]{1,0:T(8,128)(2,1)S(1)} %collective-permute-done.3.refs_2_), channel_id=1, source_target_pairs={{0,4},{1,5},{2,6},{3,7},{8,0},{9,1},{10,2},{11,3},{16,8},{17,9},{1... | collective-permute-start | bytes 491528 | tf_op jit(solution)/shard_map/ppermute | solution.py:337
  15.7 9.0 %collective-permute-start.11 = (bf16[640,128]{1,0:T(8,128)(2,1)S(1)}, bf16[640,128]{1,0:T(8,128)(2,1)S(1)}, u32[]{:S(2)}, u32[]{:S(2)}) collective-permute-start(bf16[640,128]{1,0:T(8,128)(2,1)S(1)} %collective-permute-done.10.refs_8_), channel_id=1, source_target_pairs={{0,4},{1,5},{2,6},{3,7},{8,0},{9,1},{10,2},{11,3},{16,8},{17,9},{1... | collective-permute-start | bytes 491528 | tf_op jit(solution)/shard_map/ppermute | solution.py:337
  16.5 8.2 %collective-permute-start.9 = (bf16[640,128]{1,0:T(8,128)(2,1)S(1)}, bf16[640,128]{1,0:T(8,128)(2,1)S(1)}, u32[]{:S(2)}, u32[]{:S(2)}) collective-permute-start(bf16[640,128]{1,0:T(8,128)(2,1)S(1)} %collective-permute-done.8.refs_7_), channel_id=1, source_target_pairs={{0,8},{1,9},{2,10},{3,11},{8,16},{9,17},{10,18},{11,19},{16,24},{1... | collective-permute-start | bytes 491528 | tf_op jit(solution)/shard_map/ppermute | solution.py:337
  17.7 7.0 %collective-permute-start.2 = (bf16[640,128]{1,0:T(8,128)(2,1)S(1)}, bf16[640,128]{1,0:T(8,128)(2,1)S(1)}, u32[]{:S(2)}, u32[]{:S(2)}) collective-permute-start(bf16[640,128]{1,0:T(8,128)(2,1)S(1)} %collective-permute-done.1.refs_3_), channel_id=1, source_target_pairs={{0,8},{1,9},{2,10},{3,11},{8,16},{9,17},{10,18},{11,19},{16,24},{1... | collective-permute-start | bytes 491528 | tf_op jit(solution)/shard_map/ppermute | solution.py:337
  19.5 5.3 %collective-permute-start.5 = (bf16[640,128]{1,0:T(8,128)(2,1)S(1)}, bf16[640,128]{1,0:T(8,128)(2,1)S(1)}, u32[]{:S(2)}, u32[]{:S(2)}) collective-permute-start(bf16[640,128]{1,0:T(8,128)(2,1)S(1)} %collective-permute-done.4.refs_4_), channel_id=1, source_target_pairs={{0,4},{1,5},{2,6},{3,7},{8,0},{9,1},{10,2},{11,3},{16,8},{17,9},{1... | collective-permute-start | bytes 491528 | tf_op jit(solution)/shard_map/ppermute | solution.py:337
  19.7 5.0 %collective-permute-start.18 = (bf16[512,128]{1,0:T(8,128)(2,1)S(1)}, bf16[512,128]{1,0:T(8,128)(2,1)S(1)}, u32[]{:S(2)}, u32[]{:S(2)}) collective-permute-start(bf16[512,128]{1,0:T(8,128)(2,1)S(1)} %get-tuple-element.20), channel_id=1, source_target_pairs={{0,2},{1,3},{2,0},{3,1},{4,6},{5,7},{6,4},{7,5},{8,10},{9,11},{10,... | collective-permute-start | bytes 393224 | tf_op jit(solution)/shard_map/ppermute | solution.py:288
  25.0 9.7 %collective-permute-start.19 = (bf16[4992,128]{1,0:T(8,128)(2,1)S(1)}, bf16[4992,128]{1,0:T(8,128)(2,1)S(1)}, u32[]{:S(2)}, u32[]{:S(2)}) collective-permute-start(bf16[4992,128]{1,0:T(8,128)(2,1)S(1)} %get-tuple-element.22), channel_id=1, source_target_pairs={{0,1},{1,0},{2,3},{3,2},{4,5},{5,4},{6,7},{7,6},{8,9},{9,8},{10,11... | collective-permute-start | bytes 3833864 | tf_op jit(solution)/shard_map/ppermute | solution.py:288
  25.1 5.9 %collective-permute-start.12 = (bf16[512,128]{1,0:T(8,128)(2,1)S(1)}, bf16[512,128]{1,0:T(8,128)(2,1)S(1)}, u32[]{:S(2)}, u32[]{:S(2)}) collective-permute-start(bf16[512,128]{1,0:T(8,128)(2,1)S(1)} %get-tuple-element.18), channel_id=1, source_target_pairs={{0,4},{1,5},{2,6},{3,7},{8,0},{9,1},{10,2},{11,3},{16,8},{17,9},{1... | collective-permute-start | bytes 393224 | tf_op jit(solution)/shard_map/ppermute | solution.py:337
  26.2 7.7 %collective-permute-start.13 = (bf16[512,128]{1,0:T(8,128)(2,1)S(1)}, bf16[512,128]{1,0:T(8,128)(2,1)S(1)}, u32[]{:S(2)}, u32[]{:S(2)}) collective-permute-start(bf16[512,128]{1,0:T(8,128)(2,1)S(1)} %get-tuple-element.19), channel_id=1, source_target_pairs={{0,8},{1,9},{2,10},{3,11},{8,16},{9,17},{10,18},{11,19},{16,24},{1... | collective-permute-start | bytes 393224 | tf_op jit(solution)/shard_map/ppermute | solution.py:337
  27.3 6.6 %collective-permute-start.6 = (bf16[512,128]{1,0:T(8,128)(2,1)S(1)}, bf16[512,128]{1,0:T(8,128)(2,1)S(1)}, u32[]{:S(2)}, u32[]{:S(2)}) collective-permute-start(bf16[512,128]{1,0:T(8,128)(2,1)S(1)} %get-tuple-element.16), channel_id=1, source_target_pairs={{1,11},{3,9},{9,19},{11,17},{17,27},{19,25},{25,31},{27,29},{29,23... | collective-permute-start | bytes 393224 | tf_op jit(solution)/shard_map/ppermute | solution.py:344
  28.5 5.9 %collective-permute-start.7 = (bf16[512,128]{1,0:T(8,128)(2,1)S(1)}, bf16[512,128]{1,0:T(8,128)(2,1)S(1)}, u32[]{:S(2)}, u32[]{:S(2)}) collective-permute-start(bf16[512,128]{1,0:T(8,128)(2,1)S(1)} %get-tuple-element.17), channel_id=1, source_target_pairs={{1,9},{3,11},{9,17},{11,19},{17,25},{19,27},{25,29},{27,31},{29,21... | collective-permute-start | bytes 393224 | tf_op jit(solution)/shard_map/ppermute | solution.py:343
  31.1 4.4 %collective-permute-start.16 = (bf16[512,128]{1,0:T(8,128)(2,1)S(1)}, bf16[512,128]{1,0:T(8,128)(2,1)S(1)}, u32[]{:S(2)}, u32[]{:S(2)}) collective-permute-start(bf16[512,128]{1,0:T(8,128)(2,1)S(1)} %collective-permute-done.12.refs_2_), channel_id=1, source_target_pairs={{0,1},{1,0},{2,3},{3,2},{4,5},{5,4},{6,7},{7,6},{8,9},{9,8},{10,11... | collective-permute-start | bytes 393224 | tf_op jit(solution)/shard_map/ppermute | solution.py:288
  33.9 1.6 %collective-permute-start.17 = (bf16[512,128]{1,0:T(8,128)(2,1)S(1)}, bf16[512,128]{1,0:T(8,128)(2,1)S(1)}, u32[]{:S(2)}, u32[]{:S(2)}) collective-permute-start(bf16[512,128]{1,0:T(8,128)(2,1)S(1)} %collective-permute-done.13.refs_3_), channel_id=1, source_target_pairs={{0,1},{1,0},{2,3},{3,2},{4,5},{5,4},{6,7},{7,6},{8,9},{9,8},{10,11... | collective-permute-start | bytes 393224 | tf_op jit(solution)/shard_map/ppermute | solution.py:288
  33.9 1.6 %collective-permute-start.14 = (bf16[512,128]{1,0:T(8,128)(2,1)S(1)}, bf16[512,128]{1,0:T(8,128)(2,1)S(1)}, u32[]{:S(2)}, u32[]{:S(2)}) collective-permute-start(bf16[512,128]{1,0:T(8,128)(2,1)S(1)} %collective-permute-done.6.refs_0_), channel_id=1, source_target_pairs={{0,1},{1,0},{2,3},{3,2},{4,5},{5,4},{6,7},{7,6},{8,9},{9,8},{10,11... | collective-permute-start | bytes 393224 | tf_op jit(solution)/shard_map/ppermute | solution.py:288
  34.4 1.3 %collective-permute-start.15 = (bf16[512,128]{1,0:T(8,128)(2,1)S(1)}, bf16[512,128]{1,0:T(8,128)(2,1)S(1)}, u32[]{:S(2)}, u32[]{:S(2)}) collective-permute-start(bf16[512,128]{1,0:T(8,128)(2,1)S(1)} %collective-permute-done.7.refs_1_), channel_id=1, source_target_pairs={{0,1},{1,0},{2,3},{3,2},{4,5},{5,4},{6,7},{7,6},{8,9},{9,8},{10,11... | collective-permute-start | bytes 393224 | tf_op jit(solution)/shard_map/ppermute | solution.py:288

commit v7 on v4

--- a/solution.py
+++ b/solution.py
@@ -332,8 +332,8 @@
     straight, diagonal = cut(
         [((1, 0), (-1, 1), 0), ((1, 0), (-1, 1), 1)], held[half - 1, 0][1], held[half + 1, 0][1]
     )
+    held[half, 2] = ("cross", lax.ppermute(diagonal, axes, [(i, j ^ 2) for i, j in split]), 0)
     held[half, 0] = ("cross", lax.ppermute(straight, axes, split), 0)
-    held[half, 2] = ("cross", lax.ppermute(diagonal, axes, [(i, j ^ 2) for i, j in split]), 0)
     early = {key: held[key] for key in held if min(key[0], count - key[0]) < half - key[1] // 2}
     early = dict(sorted(early.items()))
     got = exchange(early)

time: 37.7 us -> 38 us (level)
    ppermute x1, starting transfers between devices: 1.58 us -> 0.99 us  [gathering_body(): held[half, 0] = ('cross', lax.ppermute(straight, axes, split), 0)]
    ppermute x1, starting transfers between devices: 1.12 us -> 1.71 us  [gathering_body(): lax.ppermute(diagonal, axes, [(i, j ^ 2) for i, j in split])]
where the time goes in v7:
time: 38 us; the launch traced here: 37.5 us
  starting transfers between devices  19.3 us (51%)
  waiting for transfers between devices  14.3 us (38%)
  Pallas kernels  3.83 us (10%)
    ppermute x6, waiting for transfers between devices, gathering_body(): lax.ppermute(ahead, axes, ways[0])  8.61 us
    ppermute x6, starting transfers between devices, gathering_body(): lax.ppermute(ahead, axes, ways[0])  8.6 us
    ppermute x6, starting transfers between devices, gathering_body(): lax.ppermute(back, axes, ways[1])  6.61 us
    ppermute x6, waiting for transfers between devices, gathering_body(): lax.ppermute(back, axes, ways[1])  5.31 us
    pallas_call x6, Pallas kernels, call(): pl.pallas_call(functools.partial(kernel, *sizes, *given), out_shape=out,...  3.83 us
    ppermute x1, starting transfers between devices, gathering_body(): lax.ppermute(diagonal, axes, [(i, j ^ 2) for i, j in split])  1.71 us
    ppermute x6, starting transfers between devices, across(): return lax.ppermute(piece, axes, [(i, i ^ mask) for i in range(4 * count)])  1.34 us
    ppermute x1, starting transfers between devices, gathering_body(): held[half, 0] = ('cross', lax.ppermute(straight, axes, split), 0)  0.99 us
  transfers between devices with their start and end apart: 20, of which 12 were waited for; matrix products, arithmetic and copies ran while one was open for 0% of the time, Pallas kernels for 3%

profile of v7, /device:TPU:0, one launch (start us, length us, event | category | flops | bytes accessed | tf_op | source)
XLA Modules:
  0.0 37.5 jit_solution(11274038625633903997)
XLA Ops:
  0.0 1.0 %pack.1.refs_0_ = bf16[640,128]{1,0:T(8,128)(2,1)S(1)} custom-call(s32[8,8]{1,0:T(8,128)} %a_pattern.1, s32[8,12]{1,0:T(8,128)} %g_pattern.1, bf16[8,32,128]{2,1,0:T(8,128)(2,1)} %a_ref.1, bf16[32,1536]{1,0:T(8,128)(2,1)} %g_ref.1), custom_call_target="tpu_custom_call" | custom-call | tf_op jit(solution)/shard_map/pack/pallas_call | solution.py:262
  1.0 3.1 %collective-permute-start = (bf16[640,128]{1,0:T(8,128)(2,1)S(1)}, bf16[640,128]{1,0:T(8,128)(2,1)S(1)}, u32[]{:S(2)}, u32[]{:S(2)}) collective-permute-start(bf16[640,128]{1,0:T(8,128)(2,1)S(1)} %pack.1.refs_0_), channel_id=1, source_target_pairs={{0,8},{1,9},{2,10},{3,11},{8,16},{9,17},{10,18},{11,19},{16,24},{1... | collective-permute-start | bytes 491528 | tf_op jit(solution)/shard_map/ppermute | solution.py:328
  4.1 0.0 collective-permute-start.3
  4.1 2.9 %collective-permute-start.10 = (bf16[640,128]{1,0:T(8,128)(2,1)S(1)}, bf16[640,128]{1,0:T(8,128)(2,1)S(1)}, u32[]{:S(2)}, u32[]{:S(2)}) collective-permute-start(bf16[640,128]{1,0:T(8,128)(2,1)S(1)} %pack.1.refs_0_), channel_id=1, source_target_pairs={{0,6},{1,7},{2,4},{3,5},{8,2},{9,3},{10,0},{11,1},{16,10},{17,11},... | collective-permute-start | bytes 491528 | tf_op jit(solution)/shard_map/ppermute | solution.py:328
  7.0 0.1 collective-permute-start.8
  7.0 1.6 %collective-permute-done.refs_2_ = bf16[640,128]{1,0:T(8,128)(2,1)S(1)} collective-permute-done((bf16[640,128]{1,0:T(8,128)(2,1)S(1)}, bf16[640,128]{1,0:T(8,128)(2,1)S(1)}, u32[]{:S(2)}, u32[]{:S(2)}) %collective-permute-start) | collective-permute-done | bytes 163872 | tf_op jit(solution)/shard_map/ppermute | solution.py:328
  8.6 2.5 %collective-permute-start.1 = (bf16[640,128]{1,0:T(8,128)(2,1)S(1)}, bf16[640,128]{1,0:T(8,128)(2,1)S(1)}, u32[]{:S(2)}, u32[]{:S(2)}) collective-permute-start(bf16[640,128]{1,0:T(8,128)(2,1)S(1)} %collective-permute-done.refs_2_), channel_id=1, source_target_pairs={{0,8},{1,9},{2,10},{3,11},{8,16},{9,17},{10,18},{11,19},{16,24},{1... | collective-permute-start | bytes 491528 | tf_op jit(solution)/shard_map/ppermute | solution.py:328
  11.1 0.1 collective-permute-done.3.refs_10_
  11.2 2.5 %collective-permute-start.4 = (bf16[640,128]{1,0:T(8,128)(2,1)S(1)}, bf16[640,128]{1,0:T(8,128)(2,1)S(1)}, u32[]{:S(2)}, u32[]{:S(2)}) collective-permute-start(bf16[640,128]{1,0:T(8,128)(2,1)S(1)} %collective-permute-done.3.refs_10_), channel_id=1, source_target_pairs={{0,4},{1,5},{2,6},{3,7},{8,0},{9,1},{10,2},{11,3},{16,8},{17,9},{1... | collective-permute-start | bytes 491528 | tf_op jit(solution)/shard_map/ppermute | solution.py:328
  13.7 0.7 %collective-permute-start.18 = (bf16[640,128]{1,0:T(8,128)(2,1)S(1)}, bf16[640,128]{1,0:T(8,128)(2,1)S(1)}, u32[]{:S(2)}, u32[]{:S(2)}) collective-permute-start(bf16[640,128]{1,0:T(8,128)(2,1)S(1)} %pack.1.refs_0_), channel_id=1, source_target_pairs={{0,2},{1,3},{2,0},{3,1},{4,6},{5,7},{6,4},{7,5},{8,10},{9,11},{10,... | collective-permute-start | bytes 491528 | tf_op jit(solution)/shard_map/ppermute | solution.py:279
  14.4 1.2 %collective-permute-done.10.refs_11_ = bf16[640,128]{1,0:T(8,128)(2,1)S(1)} collective-permute-done((bf16[640,128]{1,0:T(8,128)(2,1)S(1)}, bf16[640,128]{1,0:T(8,128)(2,1)S(1)}, u32[]{:S(2)}, u32[]{:S(2)}) %collective-permute-start.10) | collective-permute-done | bytes 163872 | tf_op jit(solution)/shard_map/ppermute | solution.py:328
  15.6 0.0 collective-permute-start.11
  15.7 2.0 %collective-permute-done.8.refs_3_ = bf16[640,128]{1,0:T(8,128)(2,1)S(1)} collective-permute-done((bf16[640,128]{1,0:T(8,128)(2,1)S(1)}, bf16[640,128]{1,0:T(8,128)(2,1)S(1)}, u32[]{:S(2)}, u32[]{:S(2)}) %collective-permute-start.8) | collective-permute-done | bytes 163872 | tf_op jit(solution)/shard_map/ppermute | solution.py:328
  17.7 0.0 collective-permute-start.9
  17.7 0.0 collective-permute-done.1.refs_4_
  17.7 1.9 %collective-permute-start.2 = (bf16[640,128]{1,0:T(8,128)(2,1)S(1)}, bf16[640,128]{1,0:T(8,128)(2,1)S(1)}, u32[]{:S(2)}, u32[]{:S(2)}) collective-permute-start(bf16[640,128]{1,0:T(8,128)(2,1)S(1)} %collective-permute-done.1.refs_4_), channel_id=1, source_target_pairs={{0,8},{1,9},{2,10},{3,11},{8,16},{9,17},{10,18},{11,19},{16,24},{1... | collective-permute-start | bytes 491528 | tf_op jit(solution)/shard_map/ppermute | solution.py:328
  19.6 0.0 collective-permute-done.4.refs_8_
  19.6 0.2 collective-permute-start.5
  19.8 0.0 collective-permute-done.18.refs_1_
  19.8 2.7 %collective-permute-done.11.refs_1_.refs_9_ = bf16[640,128]{1,0:T(8,128)(2,1)S(1)} collective-permute-done((bf16[640,128]{1,0:T(8,128)(2,1)S(1)}, bf16[640,128]{1,0:T(8,128)(2,1)S(1)}, u32[]{:S(2)}, u32[]{:S(2)}) %collective-permute-start.11) | collective-permute-done | bytes 163872 | tf_op jit(solution)/shard_map/ppermute | solution.py:328
  22.5 0.5 %collective-permute-done.9.refs_0_.refs_5_ = bf16[640,128]{1,0:T(8,128)(2,1)S(1)} collective-permute-done((bf16[640,128]{1,0:T(8,128)(2,1)S(1)}, bf16[640,128]{1,0:T(8,128)(2,1)S(1)}, u32[]{:S(2)}, u32[]{:S(2)}) %collective-permute-start.9) | collective-permute-done | bytes 163872 | tf_op jit(solution)/shard_map/ppermute | solution.py:328
  23.0 1.8 %collective-permute-done.2.refs_0_.refs_6_ = bf16[640,128]{1,0:T(8,128)(2,1)S(1)} collective-permute-done((bf16[640,128]{1,0:T(8,128)(2,1)S(1)}, bf16[640,128]{1,0:T(8,128)(2,1)S(1)}, u32[]{:S(2)}, u32[]{:S(2)}) %collective-permute-start.2) | collective-permute-done | bytes 163872 | tf_op jit(solution)/shard_map/ppermute | solution.py:328
  24.7 0.2 collective-permute-done.5.refs_1_.refs_7_
  24.9 0.2 collect.1
  25.1 0.1 collective-permute-start.19
  25.2 1.0 %collective-permute-start.12 = (bf16[512,128]{1,0:T(8,128)(2,1)S(1)}, bf16[512,128]{1,0:T(8,128)(2,1)S(1)}, u32[]{:S(2)}, u32[]{:S(2)}) collective-permute-start(bf16[512,128]{1,0:T(8,128)(2,1)S(1)} %get-tuple-element.15), channel_id=1, source_target_pairs={{0,4},{1,5},{2,6},{3,7},{8,0},{9,1},{10,2},{11,3},{16,8},{17,9},{1... | collective-permute-start | bytes 393224 | tf_op jit(solution)/shard_map/ppermute | solution.py:328
  26.2 1.1 %collective-permute-start.13 = (bf16[512,128]{1,0:T(8,128)(2,1)S(1)}, bf16[512,128]{1,0:T(8,128)(2,1)S(1)}, u32[]{:S(2)}, u32[]{:S(2)}) collective-permute-start(bf16[512,128]{1,0:T(8,128)(2,1)S(1)} %get-tuple-element.16), channel_id=1, source_target_pairs={{0,8},{1,9},{2,10},{3,11},{8,16},{9,17},{10,18},{11,19},{16,24},{1... | collective-permute-start | bytes 393224 | tf_op jit(solution)/shard_map/ppermute | solution.py:328
  27.3 0.1 cut.2
  27.4 1.0 %collective-permute-start.6 = (bf16[512,128]{1,0:T(8,128)(2,1)S(1)}, bf16[512,128]{1,0:T(8,128)(2,1)S(1)}, u32[]{:S(2)}, u32[]{:S(2)}) collective-permute-start(bf16[512,128]{1,0:T(8,128)(2,1)S(1)} %get-tuple-element.13), channel_id=1, source_target_pairs={{1,9},{3,11},{9,17},{11,19},{17,25},{19,27},{25,29},{27,31},{29,21... | collective-permute-start | bytes 393224 | tf_op jit(solution)/shard_map/ppermute | solution.py:336
  28.3 1.7 %collective-permute-start.7 = (bf16[512,128]{1,0:T(8,128)(2,1)S(1)}, bf16[512,128]{1,0:T(8,128)(2,1)S(1)}, u32[]{:S(2)}, u32[]{:S(2)}) collective-permute-start(bf16[512,128]{1,0:T(8,128)(2,1)S(1)} %get-tuple-element.14), channel_id=1, source_target_pairs={{1,11},{3,9},{9,19},{11,17},{17,27},{19,25},{25,31},{27,29},{29,23... | collective-permute-start | bytes 393224 | tf_op jit(solution)/shard_map/ppermute | solution.py:335
  30.1 1.1 %collective-permute-done.12.refs_2_ = bf16[512,128]{1,0:T(8,128)(2,1)S(1)} collective-permute-done((bf16[512,128]{1,0:T(8,128)(2,1)S(1)}, bf16[512,128]{1,0:T(8,128)(2,1)S(1)}, u32[]{:S(2)}, u32[]{:S(2)}) %collective-permute-start.12) | collective-permute-done | bytes 131104 | tf_op jit(solution)/shard_map/ppermute | solution.py:328
  31.1 0.0 collective-permute-start.16
  31.1 2.8 %collective-permute-done.13.refs_3_ = bf16[512,128]{1,0:T(8,128)(2,1)S(1)} collective-permute-done((bf16[512,128]{1,0:T(8,128)(2,1)S(1)}, bf16[512,128]{1,0:T(8,128)(2,1)S(1)}, u32[]{:S(2)}, u32[]{:S(2)}) %collective-permute-start.13) | collective-permute-done | bytes 131104 | tf_op jit(solution)/shard_map/ppermute | solution.py:328
  33.9 0.0 collective-permute-start.17
  33.9 0.0 collective-permute-done.6.refs_0_
  33.9 0.5 %collective-permute-start.14 = (bf16[512,128]{1,0:T(8,128)(2,1)S(1)}, bf16[512,128]{1,0:T(8,128)(2,1)S(1)}, u32[]{:S(2)}, u32[]{:S(2)}) collective-permute-start(bf16[512,128]{1,0:T(8,128)(2,1)S(1)} %collective-permute-done.6.refs_0_), channel_id=1, source_target_pairs={{0,1},{1,0},{2,3},{3,2},{4,5},{5,4},{6,7},{7,6},{8,9},{9,8},{10,11... | collective-permute-start | bytes 393224 | tf_op jit(solution)/shard_map/ppermute | solution.py:279
  34.4 0.0 collective-permute-done.7.refs_1_
  34.4 0.1 collective-permute-start.15
  34.5 0.0 collective-permute-done.19.refs_1_.refs_9_
  34.5 0.8 %early.1 = (f32[192,1024]{1,0:T(8,128)S(1)}, bf16[1024,384]{1,0:T(8,128)(2,1)S(1)}) custom-call(bf16[4992,128]{1,0:T(8,128)(2,1)S(1)} %get-tuple-element.17.refs_0_.refs_8_, bf16[4992,128]{1,0:T(8,128)(2,1)S(1)} %collective-permute-done.19.refs_1_.refs_9_), custom_call_target="tpu_custom_call" | custom-call | tf_op jit(solution)/shard_map/early/pallas_call | solution.py:262
  35.4 0.0 collective-permute-done.16.refs_6_
  35.4 0.0 collective-permute-done.17.refs_7_
  35.4 0.1 collective-permute-done.14.refs_4_
  35.5 0.3 collective-permute-done.15.refs_5_
  35.8 1.7 %product.1 = f32[192,384]{1,0:T(8,128)} custom-call(bf16[512,128]{1,0:T(8,128)(2,1)S(1)} %collective-permute-done.6.refs_0_, bf16[512,128]{1,0:T(8,128)(2,1)S(1)} %collective-permute-done.7.refs_1_, bf16[512,128]{1,0:T(8,128)(2,1)S(1)} %collective-permute-done.12.refs_2_, bf16[512,128]{1,0:T(8,128)(2,1)S(1)} %collective-permute-done.13.refs_3_, ...), custom_call_target="tpu_custom_call" | custom-call | tf_op jit(solution)/shard_map/product/pallas_call | solution.py:262
  (1 shorter events, 0.0 us)
Async XLA Ops:
  1.0 7.6 %collective-permute-start = (bf16[640,128]{1,0:T(8,128)(2,1)S(1)}, bf16[640,128]{1,0:T(8,128)(2,1)S(1)}, u32[]{:S(2)}, u32[]{:S(2)}) collective-permute-start(bf16[640,128]{1,0:T(8,128)(2,1)S(1)} %pack.1.refs_0_), channel_id=1, source_target_pairs={{0,8},{1,9},{2,10},{3,11},{8,16},{9,17},{10,18},{11,19},{16,24},{1... | collective-permute-start | bytes 491528 | tf_op jit(solution)/shard_map/ppermute | solution.py:328
  4.1 7.1 %collective-permute-start.3 = (bf16[640,128]{1,0:T(8,128)(2,1)S(1)}, bf16[640,128]{1,0:T(8,128)(2,1)S(1)}, u32[]{:S(2)}, u32[]{:S(2)}) collective-permute-start(bf16[640,128]{1,0:T(8,128)(2,1)S(1)} %pack.1.refs_0_), channel_id=1, source_target_pairs={{0,4},{1,5},{2,6},{3,7},{8,0},{9,1},{10,2},{11,3},{16,8},{17,9},{1... | collective-permute-start | bytes 491528 | tf_op jit(solution)/shard_map/ppermute | solution.py:328
  4.1 11.6 %collective-permute-start.10 = (bf16[640,128]{1,0:T(8,128)(2,1)S(1)}, bf16[640,128]{1,0:T(8,128)(2,1)S(1)}, u32[]{:S(2)}, u32[]{:S(2)}) collective-permute-start(bf16[640,128]{1,0:T(8,128)(2,1)S(1)} %pack.1.refs_0_), channel_id=1, source_target_pairs={{0,6},{1,7},{2,4},{3,5},{8,2},{9,3},{10,0},{11,1},{16,10},{17,11},... | collective-permute-start | bytes 491528 | tf_op jit(solution)/shard_map/ppermute | solution.py:328
  7.0 10.7 %collective-permute-start.8 = (bf16[640,128]{1,0:T(8,128)(2,1)S(1)}, bf16[640,128]{1,0:T(8,128)(2,1)S(1)}, u32[]{:S(2)}, u32[]{:S(2)}) collective-permute-start(bf16[640,128]{1,0:T(8,128)(2,1)S(1)} %pack.1.refs_0_), channel_id=1, source_target_pairs={{0,10},{1,11},{2,8},{3,9},{8,18},{9,19},{10,16},{11,17},{16,26},{1... | collective-permute-start | bytes 491528 | tf_op jit(solution)/shard_map/ppermute | solution.py:328
  8.6 9.1 %collective-permute-start.1 = (bf16[640,128]{1,0:T(8,128)(2,1)S(1)}, bf16[640,128]{1,0:T(8,128)(2,1)S(1)}, u32[]{:S(2)}, u32[]{:S(2)}) collective-permute-start(bf16[640,128]{1,0:T(8,128)(2,1)S(1)} %collective-permute-done.refs_2_), channel_id=1, source_target_pairs={{0,8},{1,9},{2,10},{3,11},{8,16},{9,17},{10,18},{11,19},{16,24},{1... | collective-permute-start | bytes 491528 | tf_op jit(solution)/shard_map/ppermute | solution.py:328
  11.2 8.4 %collective-permute-start.4 = (bf16[640,128]{1,0:T(8,128)(2,1)S(1)}, bf16[640,128]{1,0:T(8,128)(2,1)S(1)}, u32[]{:S(2)}, u32[]{:S(2)}) collective-permute-start(bf16[640,128]{1,0:T(8,128)(2,1)S(1)} %collective-permute-done.3.refs_10_), channel_id=1, source_target_pairs={{0,4},{1,5},{2,6},{3,7},{8,0},{9,1},{10,2},{11,3},{16,8},{17,9},{1... | collective-permute-start | bytes 491528 | tf_op jit(solution)/shard_map/ppermute | solution.py:328
  13.7 6.0 %collective-permute-start.18 = (bf16[640,128]{1,0:T(8,128)(2,1)S(1)}, bf16[640,128]{1,0:T(8,128)(2,1)S(1)}, u32[]{:S(2)}, u32[]{:S(2)}) collective-permute-start(bf16[640,128]{1,0:T(8,128)(2,1)S(1)} %pack.1.refs_0_), channel_id=1, source_target_pairs={{0,2},{1,3},{2,0},{3,1},{4,6},{5,7},{6,4},{7,5},{8,10},{9,11},{10,... | collective-permute-start | bytes 491528 | tf_op jit(solution)/shard_map/ppermute | solution.py:279
  15.6 6.9 %collective-permute-start.11 = (bf16[640,128]{1,0:T(8,128)(2,1)S(1)}, bf16[640,128]{1,0:T(8,128)(2,1)S(1)}, u32[]{:S(2)}, u32[]{:S(2)}) collective-permute-start(bf16[640,128]{1,0:T(8,128)(2,1)S(1)} %collective-permute-done.10.refs_11_), channel_id=1, source_target_pairs={{0,4},{1,5},{2,6},{3,7},{8,0},{9,1},{10,2},{11,3},{16,8},{17,9},{1... | collective-permute-start | bytes 491528 | tf_op jit(solution)/shard_map/ppermute | solution.py:328
  17.7 5.3 %collective-permute-start.9 = (bf16[640,128]{1,0:T(8,128)(2,1)S(1)}, bf16[640,128]{1,0:T(8,128)(2,1)S(1)}, u32[]{:S(2)}, u32[]{:S(2)}) collective-permute-start(bf16[640,128]{1,0:T(8,128)(2,1)S(1)} %collective-permute-done.8.refs_3_), channel_id=1, source_target_pairs={{0,8},{1,9},{2,10},{3,11},{8,16},{9,17},{10,18},{11,19},{16,24},{1... | collective-permute-start | bytes 491528 | tf_op jit(solution)/shard_map/ppermute | solution.py:328
  17.7 7.1 %collective-permute-start.2 = (bf16[640,128]{1,0:T(8,128)(2,1)S(1)}, bf16[640,128]{1,0:T(8,128)(2,1)S(1)}, u32[]{:S(2)}, u32[]{:S(2)}) collective-permute-start(bf16[640,128]{1,0:T(8,128)(2,1)S(1)} %collective-permute-done.1.refs_4_), channel_id=1, source_target_pairs={{0,8},{1,9},{2,10},{3,11},{8,16},{9,17},{10,18},{11,19},{16,24},{1... | collective-permute-start | bytes 491528 | tf_op jit(solution)/shard_map/ppermute | solution.py:328
  19.6 5.3 %collective-permute-start.5 = (bf16[640,128]{1,0:T(8,128)(2,1)S(1)}, bf16[640,128]{1,0:T(8,128)(2,1)S(1)}, u32[]{:S(2)}, u32[]{:S(2)}) collective-permute-start(bf16[640,128]{1,0:T(8,128)(2,1)S(1)} %collective-permute-done.4.refs_8_), channel_id=1, source_target_pairs={{0,4},{1,5},{2,6},{3,7},{8,0},{9,1},{10,2},{11,3},{16,8},{17,9},{1... | collective-permute-start | bytes 491528 | tf_op jit(solution)/shard_map/ppermute | solution.py:328
  25.1 9.5 %collective-permute-start.19 = (bf16[4992,128]{1,0:T(8,128)(2,1)S(1)}, bf16[4992,128]{1,0:T(8,128)(2,1)S(1)}, u32[]{:S(2)}, u32[]{:S(2)}) collective-permute-start(bf16[4992,128]{1,0:T(8,128)(2,1)S(1)} %get-tuple-element.18), channel_id=1, source_target_pairs={{0,1},{1,0},{2,3},{3,2},{4,5},{5,4},{6,7},{7,6},{8,9},{9,8},{10,11... | collective-permute-start | bytes 3833864 | tf_op jit(solution)/shard_map/ppermute | solution.py:279
  25.2 5.9 %collective-permute-start.12 = (bf16[512,128]{1,0:T(8,128)(2,1)S(1)}, bf16[512,128]{1,0:T(8,128)(2,1)S(1)}, u32[]{:S(2)}, u32[]{:S(2)}) collective-permute-start(bf16[512,128]{1,0:T(8,128)(2,1)S(1)} %get-tuple-element.15), channel_id=1, source_target_pairs={{0,4},{1,5},{2,6},{3,7},{8,0},{9,1},{10,2},{11,3},{16,8},{17,9},{1... | collective-permute-start | bytes 393224 | tf_op jit(solution)/shard_map/ppermute | solution.py:328
  26.2 7.7 %collective-permute-start.13 = (bf16[512,128]{1,0:T(8,128)(2,1)S(1)}, bf16[512,128]{1,0:T(8,128)(2,1)S(1)}, u32[]{:S(2)}, u32[]{:S(2)}) collective-permute-start(bf16[512,128]{1,0:T(8,128)(2,1)S(1)} %get-tuple-element.16), channel_id=1, source_target_pairs={{0,8},{1,9},{2,10},{3,11},{8,16},{9,17},{10,18},{11,19},{16,24},{1... | collective-permute-start | bytes 393224 | tf_op jit(solution)/shard_map/ppermute | solution.py:328
  27.4 6.6 %collective-permute-start.6 = (bf16[512,128]{1,0:T(8,128)(2,1)S(1)}, bf16[512,128]{1,0:T(8,128)(2,1)S(1)}, u32[]{:S(2)}, u32[]{:S(2)}) collective-permute-start(bf16[512,128]{1,0:T(8,128)(2,1)S(1)} %get-tuple-element.13), channel_id=1, source_target_pairs={{1,9},{3,11},{9,17},{11,19},{17,25},{19,27},{25,29},{27,31},{29,21... | collective-permute-start | bytes 393224 | tf_op jit(solution)/shard_map/ppermute | solution.py:336
  28.3 6.1 %collective-permute-start.7 = (bf16[512,128]{1,0:T(8,128)(2,1)S(1)}, bf16[512,128]{1,0:T(8,128)(2,1)S(1)}, u32[]{:S(2)}, u32[]{:S(2)}) collective-permute-start(bf16[512,128]{1,0:T(8,128)(2,1)S(1)} %get-tuple-element.14), channel_id=1, source_target_pairs={{1,11},{3,9},{9,19},{11,17},{17,27},{19,25},{25,31},{27,29},{29,23... | collective-permute-start | bytes 393224 | tf_op jit(solution)/shard_map/ppermute | solution.py:335
  31.1 4.2 %collective-permute-start.16 = (bf16[512,128]{1,0:T(8,128)(2,1)S(1)}, bf16[512,128]{1,0:T(8,128)(2,1)S(1)}, u32[]{:S(2)}, u32[]{:S(2)}) collective-permute-start(bf16[512,128]{1,0:T(8,128)(2,1)S(1)} %collective-permute-done.12.refs_2_), channel_id=1, source_target_pairs={{0,1},{1,0},{2,3},{3,2},{4,5},{5,4},{6,7},{7,6},{8,9},{9,8},{10,11... | collective-permute-start | bytes 393224 | tf_op jit(solution)/shard_map/ppermute | solution.py:279
  33.9 1.4 %collective-permute-start.17 = (bf16[512,128]{1,0:T(8,128)(2,1)S(1)}, bf16[512,128]{1,0:T(8,128)(2,1)S(1)}, u32[]{:S(2)}, u32[]{:S(2)}) collective-permute-start(bf16[512,128]{1,0:T(8,128)(2,1)S(1)} %collective-permute-done.13.refs_3_), channel_id=1, source_target_pairs={{0,1},{1,0},{2,3},{3,2},{4,5},{5,4},{6,7},{7,6},{8,9},{9,8},{10,11... | collective-permute-start | bytes 393224 | tf_op jit(solution)/shard_map/ppermute | solution.py:279
  33.9 1.5 %collective-permute-start.14 = (bf16[512,128]{1,0:T(8,128)(2,1)S(1)}, bf16[512,128]{1,0:T(8,128)(2,1)S(1)}, u32[]{:S(2)}, u32[]{:S(2)}) collective-permute-start(bf16[512,128]{1,0:T(8,128)(2,1)S(1)} %collective-permute-done.6.refs_0_), channel_id=1, source_target_pairs={{0,1},{1,0},{2,3},{3,2},{4,5},{5,4},{6,7},{7,6},{8,9},{9,8},{10,11... | collective-permute-start | bytes 393224 | tf_op jit(solution)/shard_map/ppermute | solution.py:279
  34.4 1.3 %collective-permute-start.15 = (bf16[512,128]{1,0:T(8,128)(2,1)S(1)}, bf16[512,128]{1,0:T(8,128)(2,1)S(1)}, u32[]{:S(2)}, u32[]{:S(2)}) collective-permute-start(bf16[512,128]{1,0:T(8,128)(2,1)S(1)} %collective-permute-done.7.refs_1_), channel_id=1, source_target_pairs={{0,1},{1,0},{2,3},{3,2},{4,5},{5,4},{6,7},{7,6},{8,9},{9,8},{10,11... | collective-permute-start | bytes 393224 | tf_op jit(solution)/shard_map/ppermute | solution.py:279
